TPU v7x, 32 devices: a whole 2x2x4 slice. The times are simulated.
32 devices in a mesh: seq: 4 (over y, x), dp: 8 (over z, core).
Axes of the slice: x: 2, y: 2, z: 4, core: 2. Of those that a mesh axis runs over, the one named last changes fastest.
Arguments:
- inputs: bfloat16 [8, 1024, 1536], P('dp', 'seq'), may hold values from -6 to 6
- block_ids: int32 [8, 1024], P('dp', 'seq'), may hold values from 0 to 7, never falling along the last dimension, each value on 1 to 256 neighbouring positions
- cotangent: bfloat16 [8, 1024, 1536], P('dp', 'seq'), may hold values from -6 to 6
- first_gain: bfloat16 [1536], P(('seq', 'dp')), may hold values from 0.5 to 1.5
- query_weight: bfloat16 [1536, 1536], P(('seq', 'dp')), may hold values from -0.15625 to 0.15625
- query_bias: bfloat16 [1536], P(('seq', 'dp')), may hold values from -3 to 3
- key_weight: bfloat16 [1536, 256], P(('seq', 'dp')), may hold values from -0.15625 to 0.15625
- key_bias: bfloat16 [256], P(('seq', 'dp')), may hold values from -3 to 3
- value_weight: bfloat16 [1536, 256], P(('seq', 'dp')), may hold values from -0.15625 to 0.15625
- value_bias: bfloat16 [256], P(('seq', 'dp')), may hold values from -3 to 3
- output_weight: bfloat16 [1536, 1536], P(('seq', 'dp')), may hold values from -1.25 to 1.25
- second_gain: bfloat16 [1536], P(('seq', 'dp')), may hold values from 0.5 to 1.5
- gate_weight: bfloat16 [1536, 8960], P('dp', 'seq'), may hold values from -0.15625 to 0.15625
- up_weight: bfloat16 [1536, 8960], P('dp', 'seq'), may hold values from -0.15625 to 0.15625
- down_weight: bfloat16 [8960, 1536], P('seq', 'dp'), may hold values from -0.375 to 0.375
Outputs:
- layer_out: bfloat16 [8, 1024, 1536], P('dp', 'seq')
- input_grad: bfloat16 [8, 1024, 1536], P('dp', 'seq')
- first_gain_grad: float32 [1536], P(('seq', 'dp'))
- query_weight_grad: float32 [1536, 1536], P(('seq', 'dp'))
- query_bias_grad: float32 [1536], P(('seq', 'dp'))
- key_weight_grad: float32 [1536, 256], P(('seq', 'dp'))
- key_bias_grad: float32 [256], P(('seq', 'dp'))
- value_weight_grad: float32 [1536, 256], P(('seq', 'dp'))
- value_bias_grad: float32 [256], P(('seq', 'dp'))
- output_weight_grad: float32 [1536, 1536], P(('seq', 'dp'))
- second_gain_grad: float32 [1536], P(('seq', 'dp'))
- gate_weight_grad: float32 [1536, 8960], P('dp', 'seq')
- up_weight_grad: float32 [1536, 8960], P('dp', 'seq')
- down_weight_grad: float32 [8960, 1536], P('seq', 'dp')
Inputs may be any that keep to these rules, and one draw needn't show every extreme that they name: `block_ids`: along each sequence the block numbers start at 0, never fall and rise by one at a time; each block holds 1 to 256 tokens, one exactly 256.
All inputs are finite; a program needn't handle non-finite values.
Results may differ from a plain program's by a relative error of at most 0.028.
Values may be sent and summed in bfloat16 or wider, within the bound.
A program may use at most 256 MiB of HBM per device.

v0:
```python
import jax
import jax.numpy as jnp
from jax import lax
from jax.sharding import PartitionSpec as P

H = 12
KEY_VALUE_HEADS = 2
HEAD_SIZE = 128


EPS = 1e-06
THETA = 1000000.0


def rope_tables(positions):
    exponent = jnp.arange(0, HEAD_SIZE, 2).astype(jnp.float32) / HEAD_SIZE
    freqs = THETA ** (-exponent)
    angles = positions.astype(jnp.float32)[:, None] * freqs[None, :]
    angles = jnp.concatenate([angles, angles], axis=-1)
    return (jnp.cos(angles), jnp.sin(angles))


def rotate(field_in, cosine, sine):
    half_width = field_in.shape[-1] // 2
    turned = jnp.concatenate([-field_in[..., half_width:], field_in[..., :half_width]], axis=-1)
    return field_in * cosine[:, None, :] + turned * sine[:, None, :]


def rms_norm(vector, norm_gain):
    factor = lax.rsqrt(jnp.mean(vector * vector, axis=-1, keepdims=True) + EPS)
    return vector * factor * norm_gain


def swiglu(left_in, right_in):
    return jax.nn.silu(left_in) * right_in


def shards(
    inputs,
    block_ids,
    cotangent,
    first_gain,
    query_weight,
    query_bias,
    key_weight,
    key_bias,
    value_weight,
    value_bias,
    output_weight,
    second_gain,
    gate_weight,
    up_weight,
    down_weight,
):
    group_size = lax.axis_size("seq")
    seq_index = lax.axis_index("seq")
    heads_dev = H // group_size
    width_query = heads_dev * HEAD_SIZE
    kv_copies = group_size // KEY_VALUE_HEADS
    tokens = inputs[0].astype(jnp.float32)
    device_rows = tokens.shape[0]
    positions = seq_index * device_rows + jnp.arange(device_rows, dtype=jnp.int32)
    cosine, sine = rope_tables(positions)
    (
        gain_one,
        weight_query,
        bias_query,
        key_matrix,
        bias_key,
        weight_value,
        bias_value,
        weight_out,
        gain_two,
    ) = (
        lax.all_gather(first_gain, ("seq", "dp"), axis=0, tiled=True),
        lax.all_gather(query_weight, ("seq", "dp"), axis=0, tiled=True),
        lax.all_gather(query_bias, ("seq", "dp"), axis=0, tiled=True),
        lax.all_gather(key_weight, ("seq", "dp"), axis=0, tiled=True),
        lax.all_gather(key_bias, ("seq", "dp"), axis=0, tiled=True),
        lax.all_gather(value_weight, ("seq", "dp"), axis=0, tiled=True),
        lax.all_gather(value_bias, ("seq", "dp"), axis=0, tiled=True),
        lax.all_gather(output_weight, ("seq", "dp"), axis=0, tiled=True),
        lax.all_gather(second_gain, ("seq", "dp"), axis=0, tiled=True),
    )
    gain_first = gain_one.astype(jnp.float32)
    normalized_narrow = rms_norm(tokens, gain_first).astype(jnp.bfloat16)
    query_pre = (
        jnp.dot(normalized_narrow, weight_query, preferred_element_type=jnp.float32)
        + bias_query.astype(jnp.float32)
    ).reshape(device_rows, H, HEAD_SIZE)
    key_pre = (
        jnp.dot(normalized_narrow, key_matrix, preferred_element_type=jnp.float32)
        + bias_key.astype(jnp.float32)
    ).reshape(device_rows, KEY_VALUE_HEADS, HEAD_SIZE)
    value_pre = (
        jnp.dot(normalized_narrow, weight_value, preferred_element_type=jnp.float32)
        + bias_value.astype(jnp.float32)
    ).reshape(device_rows, KEY_VALUE_HEADS, HEAD_SIZE)
    query_rot = rotate(query_pre, cosine, sine).astype(jnp.bfloat16)
    key_rot = rotate(key_pre, cosine, sine).astype(jnp.bfloat16)
    packed = jnp.concatenate(
        [
            query_rot.reshape(device_rows, group_size, width_query),
            jnp.repeat(key_rot, kv_copies, axis=1),
            jnp.repeat(value_pre.astype(jnp.bfloat16), kv_copies, axis=1),
        ],
        axis=-1,
    )
    block_tiles = jnp.broadcast_to(block_ids[0][:, None, None], (device_rows, group_size, 1))
    gathered, tiles_back = (
        lax.all_to_all(packed, "seq", split_axis=1, concat_axis=0, tiled=True),
        lax.all_to_all(block_tiles, "seq", split_axis=1, concat_axis=0, tiled=True),
    )
    seq_length = gathered.shape[0]
    head_queries = gathered[:, 0, :width_query].reshape(seq_length, heads_dev, HEAD_SIZE)
    head_keys = gathered[:, 0, width_query : width_query + HEAD_SIZE]
    head_values = gathered[:, 0, width_query + HEAD_SIZE :]
    blocks = tiles_back[:, 0, 0]
    block_rows = min(512, seq_length)
    starts = jnp.arange(seq_length // block_rows, dtype=jnp.int32) * block_rows
    score_scale = HEAD_SIZE ** (-0.5)

    def scores_at(row_start):
        block_query = lax.dynamic_slice_in_dim(head_queries, row_start, block_rows, 0)
        block_ids_q = lax.dynamic_slice_in_dim(blocks, row_start, block_rows, 0)
        scores = (
            jnp.einsum("rhd,td->hrt", block_query, head_keys, preferred_element_type=jnp.float32)
            * score_scale
        )
        allowed = blocks[None, :] <= block_ids_q[:, None]
        return (jnp.where(allowed[None], scores, -1000000000.0), block_query)

    def attend_block(row_start):
        scores, block_query = scores_at(row_start)
        row_peak = jnp.max(scores, axis=-1, keepdims=True)
        row_exp = jnp.exp(scores - row_peak)
        row_total = jnp.sum(row_exp, axis=-1, keepdims=True)
        prob_low = (row_exp / row_total).astype(jnp.bfloat16)
        block_out = jnp.einsum(
            "hrt,td->rhd", prob_low, head_values, preferred_element_type=jnp.float32
        )
        return (block_out.astype(jnp.bfloat16), (row_peak + jnp.log(row_total))[..., 0])

    mixed_heads, logsums = lax.map(attend_block, starts)
    mixed_heads = mixed_heads.reshape(seq_length, 1, width_query)
    mixed = lax.all_to_all(mixed_heads, "seq", split_axis=0, concat_axis=1, tiled=True).reshape(
        device_rows, H * HEAD_SIZE
    )
    hidden = tokens + jnp.dot(mixed, weight_out, preferred_element_type=jnp.float32)
    weight_gate, weight_up, weight_down = (
        lax.all_gather(gate_weight, "dp", axis=0, tiled=True),
        lax.all_gather(up_weight, "dp", axis=0, tiled=True),
        lax.all_gather(down_weight, "dp", axis=1, tiled=True),
    )
    gain_second = gain_two.astype(jnp.float32)
    second = rms_norm(hidden, gain_second).astype(jnp.bfloat16)
    incoming = cotangent[0]
    second_rows, incoming_rows = (
        lax.all_gather(second, "seq", axis=0, tiled=True),
        lax.all_gather(incoming, "seq", axis=0, tiled=True),
    )
    gate_pre = jnp.dot(second_rows, weight_gate, preferred_element_type=jnp.float32)
    up_pre = jnp.dot(second_rows, weight_up, preferred_element_type=jnp.float32)
    active = swiglu(gate_pre, up_pre).astype(jnp.bfloat16)
    down_local = lax.psum_scatter(
        jnp.dot(active, weight_down, preferred_element_type=jnp.float32).astype(jnp.bfloat16),
        "seq",
        scatter_dimension=0,
        tiled=True,
    ).astype(jnp.float32)
    layer_out = hidden + down_local
    grad_down = jnp.einsum("tf,td->fd", active, incoming_rows, preferred_element_type=jnp.float32)
    grad_active = jnp.einsum(
        "td,fd->tf", incoming_rows, weight_down, preferred_element_type=jnp.float32
    )
    unused_out, pull_swiglu = jax.vjp(swiglu, gate_pre, up_pre)
    grad_gate_f, grad_up_f = pull_swiglu(grad_active)
    grad_gate_low = grad_gate_f.astype(jnp.bfloat16)
    grad_up_low = grad_up_f.astype(jnp.bfloat16)
    grad_wgate = jnp.einsum(
        "td,tf->df", second_rows, grad_gate_low, preferred_element_type=jnp.float32
    )
    grad_wup = jnp.einsum("td,tf->df", second_rows, grad_up_low, preferred_element_type=jnp.float32)
    grad_second = lax.psum_scatter(
        (
            jnp.einsum("tf,df->td", grad_gate_low, weight_gate, preferred_element_type=jnp.float32)
            + jnp.einsum("tf,df->td", grad_up_low, weight_up, preferred_element_type=jnp.float32)
        ).astype(jnp.bfloat16),
        "seq",
        scatter_dimension=0,
        tiled=True,
    ).astype(jnp.float32)
    unused_norm, pull_second = jax.vjp(rms_norm, hidden, gain_second)
    grad_hidden, grad_gain_two = pull_second(grad_second)
    grad_hidden = grad_hidden + incoming.astype(jnp.float32)
    out_gate, out_up, out_down = (
        lax.psum_scatter(
            grad_wgate.astype(jnp.bfloat16), "dp", scatter_dimension=0, tiled=True
        ).astype(jnp.float32),
        lax.psum_scatter(
            grad_wup.astype(jnp.bfloat16), "dp", scatter_dimension=0, tiled=True
        ).astype(jnp.float32),
        lax.psum_scatter(
            grad_down.astype(jnp.bfloat16), "dp", scatter_dimension=1, tiled=True
        ).astype(jnp.float32),
    )
    grad_branch = grad_hidden.astype(jnp.bfloat16)
    grad_wout = jnp.einsum("tq,td->qd", mixed, grad_branch, preferred_element_type=jnp.float32)
    grad_mixed = jnp.einsum(
        "td,qd->tq", grad_branch, weight_out, preferred_element_type=jnp.float32
    ).astype(jnp.bfloat16)
    grad_heads = lax.all_to_all(
        grad_mixed.reshape(device_rows, group_size, width_query),
        "seq",
        split_axis=1,
        concat_axis=0,
        tiled=True,
    )
    grad_heads = grad_heads.reshape(seq_length, heads_dev, HEAD_SIZE)

    def attend_back(sums_carry, scan_item):
        row_start, logsum = scan_item
        key_sum, value_sum = sums_carry
        scores, block_query = scores_at(row_start)
        block_grad = lax.dynamic_slice_in_dim(grad_heads, row_start, block_rows, 0)
        probs = jnp.exp(scores - logsum[:, :, None])
        grad_probs = jnp.einsum(
            "rhd,td->hrt", block_grad, head_values, preferred_element_type=jnp.float32
        )
        row_delta = jnp.sum(probs * grad_probs, axis=-1, keepdims=True)
        grad_scores = (probs * (grad_probs - row_delta)).astype(jnp.bfloat16)
        grad_query = (
            jnp.einsum("hrt,td->rhd", grad_scores, head_keys, preferred_element_type=jnp.float32)
            * score_scale
        )
        key_sum = (
            key_sum
            + jnp.einsum(
                "hrt,rhd->td", grad_scores, block_query, preferred_element_type=jnp.float32
            )
            * score_scale
        )
        value_sum = value_sum + jnp.einsum(
            "hrt,rhd->td",
            probs.astype(jnp.bfloat16),
            block_grad,
            preferred_element_type=jnp.float32,
        )
        return ((key_sum, value_sum), grad_query)

    empty_sum = jnp.zeros((seq_length, HEAD_SIZE), jnp.float32)
    (grad_keys, grad_values), grad_queries = lax.scan(
        attend_back, (empty_sum, empty_sum), (starts, logsums)
    )
    returned = jnp.concatenate(
        [grad_queries.reshape(seq_length, width_query), grad_keys, grad_values], axis=-1
    )
    returned_tokens = lax.all_to_all(
        returned.reshape(seq_length, 1, width_query + 2 * HEAD_SIZE).astype(jnp.bfloat16),
        "seq",
        split_axis=0,
        concat_axis=1,
        tiled=True,
    ).astype(jnp.float32)
    grad_qrot = returned_tokens[:, :, :width_query].reshape(device_rows, H, HEAD_SIZE)
    key_rotated_gradient = (
        returned_tokens[:, :, width_query : width_query + HEAD_SIZE]
        .reshape(device_rows, KEY_VALUE_HEADS, kv_copies, HEAD_SIZE)
        .sum(axis=2)
    )
    grad_vpre = (
        returned_tokens[:, :, width_query + HEAD_SIZE :]
        .reshape(device_rows, KEY_VALUE_HEADS, kv_copies, HEAD_SIZE)
        .sum(axis=2)
    )

    def rotate_here(field_in):
        return rotate(field_in, cosine, sine)

    unused_query, pull_query = jax.vjp(rotate_here, query_pre)
    unused_key, fetch_key_rows = jax.vjp(rotate_here, key_pre)
    grad_qlow = pull_query(grad_qrot)[0].reshape(device_rows, H * HEAD_SIZE).astype(jnp.bfloat16)
    key_narrow_gradient = (
        fetch_key_rows(key_rotated_gradient)[0]
        .reshape(device_rows, KEY_VALUE_HEADS * HEAD_SIZE)
        .astype(jnp.bfloat16)
    )
    grad_vlow = grad_vpre.reshape(device_rows, KEY_VALUE_HEADS * HEAD_SIZE).astype(jnp.bfloat16)
    grad_wquery = jnp.einsum(
        "gl,gn->ln", normalized_narrow, grad_qlow, preferred_element_type=jnp.float32
    )
    key_weight_gradient = jnp.einsum(
        "gl,gn->ln", normalized_narrow, key_narrow_gradient, preferred_element_type=jnp.float32
    )
    grad_wvalue = jnp.einsum(
        "gl,gn->ln", normalized_narrow, grad_vlow, preferred_element_type=jnp.float32
    )
    grad_bquery = jnp.sum(grad_qlow.astype(jnp.float32), axis=0)
    key_bias_gradient = jnp.sum(key_narrow_gradient.astype(jnp.float32), axis=0)
    grad_bvalue = jnp.sum(grad_vlow.astype(jnp.float32), axis=0)
    grad_normed = (
        jnp.einsum("hi,ri->hr", grad_qlow, weight_query, preferred_element_type=jnp.float32)
        + jnp.einsum(
            "hi,ri->hr", key_narrow_gradient, key_matrix, preferred_element_type=jnp.float32
        )
        + jnp.einsum("hi,ri->hr", grad_vlow, weight_value, preferred_element_type=jnp.float32)
    )
    unused_first, pull_first = jax.vjp(rms_norm, tokens, gain_first)
    grad_tokens, grad_gain_one = pull_first(grad_normed)
    input_grad = (grad_hidden + grad_tokens).astype(jnp.bfloat16)[None]
    part_one, part_wq, part_bq, part_wk, part_bk, part_wv, part_bv, part_wo, part_two = (
        lax.psum_scatter(
            grad_gain_one.astype(jnp.bfloat16), "seq", scatter_dimension=0, tiled=True
        ).astype(jnp.float32),
        lax.psum_scatter(
            grad_wquery.astype(jnp.bfloat16), "seq", scatter_dimension=0, tiled=True
        ).astype(jnp.float32),
        lax.psum_scatter(
            grad_bquery.astype(jnp.bfloat16), "seq", scatter_dimension=0, tiled=True
        ).astype(jnp.float32),
        lax.psum_scatter(
            key_weight_gradient.astype(jnp.bfloat16), "seq", scatter_dimension=0, tiled=True
        ).astype(jnp.float32),
        lax.psum_scatter(
            key_bias_gradient.astype(jnp.bfloat16), "seq", scatter_dimension=0, tiled=True
        ).astype(jnp.float32),
        lax.psum_scatter(
            grad_wvalue.astype(jnp.bfloat16), "seq", scatter_dimension=0, tiled=True
        ).astype(jnp.float32),
        lax.psum_scatter(
            grad_bvalue.astype(jnp.bfloat16), "seq", scatter_dimension=0, tiled=True
        ).astype(jnp.float32),
        lax.psum_scatter(
            grad_wout.astype(jnp.bfloat16), "seq", scatter_dimension=0, tiled=True
        ).astype(jnp.float32),
        lax.psum_scatter(
            grad_gain_two.astype(jnp.bfloat16), "seq", scatter_dimension=0, tiled=True
        ).astype(jnp.float32),
    )
    out_one, out_wq, out_bq, out_wk, out_bk, out_wv, out_bv, out_wo, out_gain_two = (
        lax.psum_scatter(
            part_one.astype(jnp.bfloat16), "dp", scatter_dimension=0, tiled=True
        ).astype(jnp.float32),
        lax.psum_scatter(
            part_wq.astype(jnp.bfloat16), "dp", scatter_dimension=0, tiled=True
        ).astype(jnp.float32),
        lax.psum_scatter(
            part_bq.astype(jnp.bfloat16), "dp", scatter_dimension=0, tiled=True
        ).astype(jnp.float32),
        lax.psum_scatter(
            part_wk.astype(jnp.bfloat16), "dp", scatter_dimension=0, tiled=True
        ).astype(jnp.float32),
        lax.psum_scatter(
            part_bk.astype(jnp.bfloat16), "dp", scatter_dimension=0, tiled=True
        ).astype(jnp.float32),
        lax.psum_scatter(
            part_wv.astype(jnp.bfloat16), "dp", scatter_dimension=0, tiled=True
        ).astype(jnp.float32),
        lax.psum_scatter(
            part_bv.astype(jnp.bfloat16), "dp", scatter_dimension=0, tiled=True
        ).astype(jnp.float32),
        lax.psum_scatter(
            part_wo.astype(jnp.bfloat16), "dp", scatter_dimension=0, tiled=True
        ).astype(jnp.float32),
        lax.psum_scatter(
            part_two.astype(jnp.bfloat16), "dp", scatter_dimension=0, tiled=True
        ).astype(jnp.float32),
    )
    return (
        layer_out.astype(jnp.bfloat16)[None],
        input_grad,
        out_one,
        out_wq,
        out_bq,
        out_wk,
        out_bk,
        out_wv,
        out_bv,
        out_wo,
        out_gain_two,
        out_gate,
        out_up,
        out_down,
    )


def solution(mesh):
    in_specs = (
        P("dp", "seq", None),
        P("dp", "seq"),
        P("dp", "seq", None),
        P(("seq", "dp")),
        P(("seq", "dp"), None),
        P(("seq", "dp")),
        P(("seq", "dp"), None),
        P(("seq", "dp")),
        P(("seq", "dp"), None),
        P(("seq", "dp")),
        P(("seq", "dp"), None),
        P(("seq", "dp")),
        P("dp", "seq"),
        P("dp", "seq"),
        P("seq", "dp"),
    )
    out_specs = (
        P("dp", "seq", None),
        P("dp", "seq", None),
        P(("seq", "dp")),
        P(("seq", "dp"), None),
        P(("seq", "dp")),
        P(("seq", "dp"), None),
        P(("seq", "dp")),
        P(("seq", "dp"), None),
        P(("seq", "dp")),
        P(("seq", "dp"), None),
        P(("seq", "dp")),
        P("dp", "seq"),
        P("dp", "seq"),
        P("seq", "dp"),
    )
    return jax.shard_map(shards, mesh=mesh, in_specs=in_specs, out_specs=out_specs, check_vma=False)
```

profile of v0, /device:TPU:0, one launch (start us, length us, event | category | flops | bytes accessed | tf_op | source)
XLA Modules:
  0.0 1255.8 jit_solution(2797844206683081290)
XLA Ops:
  13.7 42.3 %all-reduce.19 = (bf16[256]{0:T(256)(128)(2,1)S(1)}, bf16[1536]{0:T(1024)(128)(2,1)S(1)}, bf16[256]{0:T(256)(128)(2,1)S(1)}, bf16[1536]{0:T(1024)(128)(2,1)S(1)}, bf16[1536]{0:T(1024)(128)(2,1)S(1)}) all-reduce(bf16[256]{0:T(256)(128)(2,1)S(1)} %dynamic-update-slice.3, ...), channel_id=1, replica_groups=mesh['seq'=4,'dp'=8] {'seq','dp'}, use_global_device_ids=true, to_apply=%add.7 | all-reduce | flops 5120 | bytes 20480
  58.6 45.0 %all_gather.45 = bf16[1536,256]{1,0:T(8,128)(2,1)S(1)} all-gather(bf16[48,256]{1,0:T(8,128)(2,1)S(1)} %copy-done.44), channel_id=1, replica_groups=mesh['seq'=4,'dp'=8] {'seq','dp'}, dimensions={0}, use_global_device_ids=true | all-gather | bytes 811008 | tf_op jit(solution)/shard_map/all_gather | solution.py:78
  105.1 44.4 %all_gather.47 = bf16[1536,256]{1,0:T(8,128)(2,1)S(1)} all-gather(bf16[48,256]{1,0:T(8,128)(2,1)S(1)} %copy-done.45), channel_id=1, replica_groups=mesh['seq'=4,'dp'=8] {'seq','dp'}, dimensions={0}, use_global_device_ids=true | all-gather | bytes 811008 | tf_op jit(solution)/shard_map/all_gather | solution.py:80
  163.6 17.2 %all-to-all-done.1 = bf16[256,4,640]{0,2,1:T(8,128)(2,1)S(1)} async-done(((bf16[256,4,640]{0,2,1:T(8,128)(2,1)}), bf16[256,4,640]{0,2,1:T(8,128)(2,1)S(1)}, u32[]{:S(2)}, u32[]{:S(2)}) %all-to-all-start.1) | async-done | bytes 1310752 | tf_op jit(solution)/shard_map/all_to_all | solution.py:111
  189.7 19.3 %while.27 = (s32[]{:T(128)}, bf16[2,512,3,128]{3,1,2,0:T(8,128)(2,1)}, f32[2,3,512]{2,1,0:T(4,128)S(1)}, s32[1024,1,1]{0,2,1:T(1,128)S(1)}, s32[2]{0:T(128)S(1)}...) while((s32[]{:T(128)}, ...), condition=%wide.region_4.5_spmd, body=%wide.region_1.4_spmd.sunk | while | flops 824900096 | bytes 28643564 | solution.py:144
  250.0 39.4 %all-gather.13.cloned.1.call-done = bf16[1024,1536]{1,0:T(8,128)(2,1)} async-done(((bf16[256,1536]{1,0:T(8,128)(2,1)}), bf16[1024,1536]{1,0:T(8,128)(2,1)}) %all-gather.13.cloned.1.call-update) | async-done | bytes 3145744 | tf_op jit(solution)/shard_map/all_gather | solution.py:159
  289.4 13.3 %fusion.95 = f32[1024,2240]{0,1:T(8,128)} fusion(bf16[1024,1536]{1,0:T(8,128)(2,1)} %all-gather.13.cloned.1.call-done, bf16[1536,2240]{1,0:T(8,128)(2,1)} %all-gather.15.cloned.1.call-done), kind=kOutput, calls=%fused_computation.161 | convolution fusion | flops 7046430720 | bytes 19202048 | tf_op jit(solution)/shard_map/dot_general | solution.py:162
  302.7 59.5 %all-gather.17.cloned.1.call-done = bf16[1536,2240]{1,0:T(8,128)(2,1)} async-done(((bf16[192,2240]{1,0:T(8,128)(2,1)}), bf16[1536,2240]{1,0:T(8,128)(2,1)}) %all-gather.17.cloned.1.call-update) | async-done | bytes 6881296 | tf_op jit(solution)/shard_map/all_gather | solution.py:152
  362.1 13.2 %fusion.96 = f32[1024,2240]{0,1:T(8,128)} fusion(bf16[1024,1536]{1,0:T(8,128)(2,1)} %all-gather.13.cloned.1.call-done, bf16[1536,2240]{1,0:T(8,128)(2,1)} %all-gather.17.cloned.1.call-done), kind=kOutput, calls=%fused_computation.162 | convolution fusion | flops 7046430720 | bytes 19202048 | tf_op jit(solution)/shard_map/dot_general | solution.py:163
  375.3 31.1 %all-gather.21.cloned.1.call-done = bf16[1,1024,1536]{2,1,0:T(8,128)(2,1)} async-done(((bf16[1,256,1536]{2,1,0:T(8,128)(2,1)}), bf16[1,1024,1536]{2,1,0:T(8,128)(2,1)}) %all-gather.21.cloned.1.call-update) | async-done | bytes 3145744 | tf_op jit(solution)/shard_map/all_gather | solution.py:160
  406.4 72.9 %all-gather.19.cloned.1.call-done = bf16[2240,1536]{0,1:T(8,128)(2,1)} async-done(((bf16[2240,192]{0,1:T(8,128)(2,1)}), bf16[2240,1536]{0,1:T(8,128)(2,1)}) %all-gather.19.cloned.1.call-update) | async-done | bytes 6881296 | tf_op jit(solution)/shard_map/all_gather | solution.py:153
  479.4 20.5 %multiply_convert_fusion = (bf16[1024,2240]{0,1:T(8,128)(2,1)}, bf16[1024,2240]{0,1:T(8,128)(2,1)}, bf16[1024,2240]{0,1:T(8,128)(2,1)}) fusion(f32[1024,2240]{0,1:T(8,128)} %fusion.95, f32[1024,2240]{0,1:T(8,128)} %fusion.96, bf16[2240,1536]{0,1:T(8,128)(2,1)} %all-gather.19.cloned.1.call-done, bf16[1,1024,1536]{2,1,0:T(8,128)(2,1)} %all-gather.21.cloned.1.call-done), kind=kOutput, calls=%fused_computation.61 | convolution fusion | flops 7083130880 | bytes 42139648 | tf_op jit(solution)/shard_map/td,fd->tf/dot_general | solution.py:173
  499.9 11.4 fusion.97
  521.0 12.4 convolution_convert_fusion.5
  533.4 30.2 %reduce-scatter.16.cloned.1.call-done = bf16[256,1536]{1,0:T(8,128)(2,1)} async-done(((bf16[1024,1536]{1,0:T(8,128)(2,1)}), bf16[256,1536]{1,0:T(8,128)(2,1)}) %reduce-scatter.16.cloned.1.call-update) | async-done | bytes 786448 | tf_op jit(solution)/shard_map/reduce_scatter | solution.py:184
  565.8 44.8 %reduce-scatter.14.cloned.1.call-done = bf16[256,1536]{1,0:T(8,128)(2,1)} async-done(((bf16[1024,1536]{1,0:T(8,128)(2,1)}), bf16[256,1536]{1,0:T(8,128)(2,1)}) %reduce-scatter.14.cloned.1.call-update) | async-done | bytes 786448 | tf_op jit(solution)/shard_map/reduce_scatter | solution.py:165
  635.2 39.8 %while.28 = (s32[]{:T(128)}, f32[1024,128]{1,0:T(8,128)}, f32[1024,128]{1,0:T(8,128)}, bf16[2,512,3,128]{3,1,2,0:T(8,128)(2,1)}, s32[1024,1,1]{0,2,1:T(1,128)S(1...) while((s32[]{:T(128)}, f32[1024,128]{1,0:T(8,128)}, ...), condition=%wide.region_11.12_spmd.clone, body=%wide.region_9.11_spmd.clone.sunk | while | flops 2038233600 | bytes 97573840 | solution.py:252
  682.3 19.8 %all_to_all.75 = bf16[4,2,81920]{2,1,0:T(2,128)(2,1)} all-to-all(bf16[4,2,81920]{2,1,0:T(2,128)(2,1)S(1)} %reshape.427), channel_id=1, replica_groups=mesh['seq'=4,'dp'=8] {'seq'}, dimensions={0} | all-to-all | bytes 2621440 | tf_op jit(solution)/shard_map/all_to_all | solution.py:258
  734.5 29.5 %reduce-scatter.26.cloned.1.call-done = bf16[384,256]{1,0:T(8,128)(2,1)} async-done(((bf16[1536,256]{1,0:T(8,128)(2,1)}), bf16[384,256]{1,0:T(8,128)(2,1)}) %reduce-scatter.26.cloned.1.call-update) | async-done | bytes 196624 | tf_op jit(solution)/shard_map/reduce_scatter | solution.py:327
  764.1 12.3 convolution_convert_fusion.2
  776.5 12.7 %convolution_convert_fusion.1 = bf16[1536,2240]{1,0:T(8,128)(2,1)} fusion(bf16[1024,1536]{1,0:T(8,128)(2,1)} %all-gather.13.cloned.1.call-done, bf16[1024,2240]{0,1:T(8,128)(2,1)} %get-tuple-element.325), kind=kOutput, calls=%fused_computation.56 | convolution fusion | flops 7049871360 | bytes 14614528 | tf_op jit(solution)/shard_map/td,tf->df/dot_general | solution.py:183
  789.2 12.6 %convolution_convert_fusion = bf16[2240,1536]{0,1:T(8,128)(2,1)} fusion(bf16[1024,2240]{0,1:T(8,128)(2,1)} %get-tuple-element.327, bf16[1,1024,1536]{2,1,0:T(8,128)(2,1)} %all-gather.21.cloned.1.call-done), kind=kOutput, calls=%fused_computation.55 | convolution fusion | flops 7049871360 | bytes 14614528 | tf_op jit(solution)/shard_map/tf,td->fd/dot_general | solution.py:172
  801.9 22.1 %reduce-scatter.30.cloned.1.call-done = bf16[384,1536]{1,0:T(8,128)(2,1)} async-done(((bf16[1536,1536]{1,0:T(8,128)(2,1)}), bf16[384,1536]{1,0:T(8,128)(2,1)}) %reduce-scatter.30.cloned.1.call-update) | async-done | bytes 1179664 | tf_op jit(solution)/shard_map/reduce_scatter | solution.py:333
  824.0 60.1 %reduce-scatter.18.cloned.1.call-done = bf16[384,1536]{1,0:T(8,128)(2,1)} async-done(((bf16[1536,1536]{1,0:T(8,128)(2,1)}), bf16[384,1536]{1,0:T(8,128)(2,1)}) %reduce-scatter.18.cloned.1.call-update) | async-done | bytes 1179664 | tf_op jit(solution)/shard_map/reduce_scatter | solution.py:315
  894.9 15.0 %all-reduce.21 = (bf16[1536]{0:T(1024)(128)(2,1)S(1)}, bf16[1536]{0:T(1024)(128)(2,1)S(1)}, bf16[256]{0:T(256)(128)(2,1)S(1)}, bf16[256]{0:T(256)(128)(2,1)S(1)}, bf16[1536]{0:T(1024)(128)(2,1)S(1)}) all-reduce(bf16[1536]{0:T(1024)(128)(2,1)S(1)} %get-tuple-element.258, ...), channel_id=5, replica_groups=mesh['seq'=4,'dp'=8] {'seq'}, use_global_device_ids=true, to_apply=%region_16.17.clone | all-reduce | flops 5120 | bytes 20480
  910.3 13.6 %all-reduce.20 = (bf16[384]{0:T(512)(128)(2,1)S(1)}, bf16[384]{0:T(512)(128)(2,1)S(1)}, bf16[64]{0:T(256)(128)(2,1)S(1)}, bf16[64]{0:T(256)(128)(2,1)S(1)}, bf16[384]{0:T(512)(128)(2,1)S(1)}) all-reduce(bf16[384]{0:T(512)(128)(2,1)S(1)} %dynamic-slice.1, ...), channel_id=6, replica_groups=mesh['seq'=4,'dp'=8] {'dp'}, use_global_device_ids=true, to_apply=%region_17.18.clone | all-reduce | flops 1280 | bytes 5120
  929.8 17.5 %reduce-scatter.28.cloned.1.call-done = bf16[48,256]{1,0:T(8,128)(2,1)} async-done(((bf16[384,256]{1,0:T(8,128)(2,1)}), bf16[48,256]{1,0:T(8,128)(2,1)}) %reduce-scatter.28.cloned.1.call-update) | async-done | bytes 24592 | tf_op jit(solution)/shard_map/reduce_scatter | solution.py:356
  948.6 76.2 %reduce-scatter.34.cloned.1.call-done = bf16[192,2240]{1,0:T(8,128)(2,1)} async-done(((bf16[1536,2240]{1,0:T(8,128)(2,1)}), bf16[192,2240]{1,0:T(8,128)(2,1)}) %reduce-scatter.34.cloned.1.call-update) | async-done | bytes 860176 | tf_op jit(solution)/shard_map/reduce_scatter | solution.py:197
  1027.3 75.3 %reduce-scatter.36.cloned.1.call-done = bf16[192,2240]{1,0:T(8,128)(2,1)} async-done(((bf16[1536,2240]{1,0:T(8,128)(2,1)}), bf16[192,2240]{1,0:T(8,128)(2,1)}) %reduce-scatter.36.cloned.1.call-update) | async-done | bytes 860176 | tf_op jit(solution)/shard_map/reduce_scatter | solution.py:200
  1105.2 75.3 %reduce-scatter.38.cloned.1.call-done = bf16[2240,192]{0,1:T(8,128)(2,1)} async-done(((bf16[2240,1536]{0,1:T(8,128)(2,1)}), bf16[2240,192]{0,1:T(8,128)(2,1)}) %reduce-scatter.38.cloned.1.call-update) | async-done | bytes 860176 | tf_op jit(solution)/shard_map/reduce_scatter | solution.py:203
  1182.9 31.0 %reduce-scatter.32.cloned.1.call-done = bf16[48,1536]{1,0:T(8,128)(2,1)} async-done(((bf16[384,1536]{1,0:T(8,128)(2,1)}), bf16[48,1536]{1,0:T(8,128)(2,1)}) %reduce-scatter.32.cloned.1.call-update) | async-done | bytes 147472 | tf_op jit(solution)/shard_map/reduce_scatter | solution.py:362
  1215.6 31.3 %reduce-scatter.20.cloned.1.call-done = bf16[48,1536]{1,0:T(8,128)(2,1)} async-done(((bf16[384,1536]{1,0:T(8,128)(2,1)}), bf16[48,1536]{1,0:T(8,128)(2,1)}) %reduce-scatter.20.cloned.1.call-update) | async-done | bytes 147472 | tf_op jit(solution)/shard_map/reduce_scatter | solution.py:344
  (332 shorter events, 227.4 us)
Async XLA Ops:
  7.2 96.4 %copy-start.5 = (bf16[1,256,1536]{2,1,0:T(8,128)(2,1)S(1)}, bf16[1,256,1536]{2,1,0:T(8,128)(2,1)}, u32[]{:S(2)}) copy-start(bf16[1,256,1536]{2,1,0:T(8,128)(2,1)} %param.19) | copy-start | bytes 2359300
  7.2 143.7 %all-gather.9.cloned.1.call-start = ((), (), s32[]{:S(2)}) async-start(), calls=%async_computation.18 | async-start | bytes 4866048 | tf_op jit(solution)/shard_map/all_gather | solution.py:76
  7.9 234.9 %all-gather.11.cloned.1.call-start = ((), (), s32[]{:S(2)}) async-start(), calls=%async_computation.19 | async-start | bytes 4866048 | tf_op jit(solution)/shard_map/all_gather | solution.py:82
  8.7 241.3 %all-gather.15.cloned.1.call-start = ((), (), s32[]{:S(2)}) async-start(), calls=%async_computation.21 | async-start | bytes 7962624 | tf_op jit(solution)/shard_map/all_gather | solution.py:151
  56.0 94.9 %copy-start.40 = (f32[1536]{0:T(1024)}, f32[1536]{0:T(1024)S(1)}, u32[]{:S(2)}) copy-start(f32[1536]{0:T(1024)S(1)} %convert_element_type.257) | copy-start | bytes 18436
  56.8 101.2 %copy-start.28 = (f32[256,128]{0,1:T(8,128)}, f32[256,128]{0,1:T(8,128)S(1)}, u32[]{:S(2)}) copy-start(f32[256,128]{0,1:T(8,128)S(1)} %copy.107) | copy-start | bytes 393220
  56.9 101.2 %copy-start.30 = (f32[256,128]{0,1:T(8,128)}, f32[256,128]{0,1:T(8,128)S(1)}, u32[]{:S(2)}) copy-start(f32[256,128]{0,1:T(8,128)S(1)} %copy.104) | copy-start | bytes 393220
  58.6 92.3 %copy-start.42 = (f32[256]{0:T(256)}, f32[256]{0:T(256)S(1)}, u32[]{:S(2)}) copy-start(f32[256]{0:T(256)S(1)} %fusion.83) | copy-start | bytes 3076
  160.0 20.8 %all-to-all-start.1 = ((bf16[256,4,640]{0,2,1:T(8,128)(2,1)}), bf16[256,4,640]{0,2,1:T(8,128)(2,1)S(1)}, u32[]{:S(2)}, u32[]{:S(2)}) async-start(bf16[256,4,640]{0,2,1:T(8,128)(2,1)} %pad_maximum_fusion), calls=%async_computation.1 | async-start | bytes 2621440 | tf_op jit(solution)/shard_map/all_to_all | solution.py:111
  181.4 8.3 all-to-all-start
  222.1 15.0 %all-to-all-start.2 = ((bf16[4,2,49152]{2,1,0:T(2,128)(2,1)}), bf16[4,2,49152]{2,1,0:T(2,128)(2,1)}, u32[]{:S(2)}, u32[]{:S(2)}) async-start(bf16[4,2,49152]{2,1,0:T(2,128)(2,1)} %reshape.425), calls=%async_computation.2 | async-start | bytes 1572864 | tf_op jit(solution)/shard_map/all_to_all | solution.py:146
  226.3 63.1 %all-gather.13.cloned.1.call-start = ((), (), s32[]{:S(2)}) async-start(), calls=%async_computation.20 | async-start | bytes 3932160 | tf_op jit(solution)/shard_map/all_gather | solution.py:159
  248.0 114.2 %all-gather.17.cloned.1.call-start = ((), (), s32[]{:S(2)}) async-start(), calls=%async_computation.22 | async-start | bytes 7962624 | tf_op jit(solution)/shard_map/all_gather | solution.py:152
  248.6 157.9 %all-gather.21.cloned.1.call-start = ((), (), s32[]{:S(2)}) async-start(), calls=%async_computation.37 | async-start | bytes 3932160 | tf_op jit(solution)/shard_map/all_gather | solution.py:160
  249.1 230.2 %all-gather.19.cloned.1.call-start = ((), (), s32[]{:S(2)}) async-start(), calls=%async_computation.23 | async-start | bytes 7962624 | tf_op jit(solution)/shard_map/all_gather | solution.py:153
  249.9 313.7 %reduce-scatter.16.cloned.1.call-start = ((), (), s32[]{:S(2)}) async-start(), calls=%async_computation.25 | async-start | bytes 3932160 | tf_op jit(solution)/shard_map/reduce_scatter | solution.py:184
  520.9 89.7 %reduce-scatter.14.cloned.1.call-start = ((), (), s32[]{:S(2)}) async-start(), calls=%async_computation.24 | async-start | bytes 3932160 | tf_op jit(solution)/shard_map/reduce_scatter | solution.py:165
  619.4 14.6 %all-to-all-start.3 = ((bf16[256,4,384]{0,2,1:T(8,128)(2,1)}), bf16[256,4,384]{0,2,1:T(8,128)(2,1)S(1)}, u32[]{:S(2)}, u32[]{:S(2)}) async-start(bf16[256,4,384]{0,2,1:T(8,128)(2,1)} %bitcast.36), calls=%async_computation.5 | async-start | bytes 1572864 | tf_op jit(solution)/shard_map/all_to_all | solution.py:212
  622.9 111.5 %reduce-scatter.22.cloned.1.call-start = ((), (), s32[]{:S(2)}) async-start(), calls=%async_computation.28 | async-start | bytes 983040 | tf_op jit(solution)/shard_map/reduce_scatter | solution.py:321
  708.7 55.3 %reduce-scatter.26.cloned.1.call-start = ((), (), s32[]{:S(2)}) async-start(), calls=%async_computation.30 | async-start | bytes 983040 | tf_op jit(solution)/shard_map/reduce_scatter | solution.py:327
  710.3 113.7 %reduce-scatter.30.cloned.1.call-start = ((), (), s32[]{:S(2)}) async-start(), calls=%async_computation.32 | async-start | bytes 5898240 | tf_op jit(solution)/shard_map/reduce_scatter | solution.py:333
  714.0 170.1 %reduce-scatter.18.cloned.1.call-start = ((), (), s32[]{:S(2)}) async-start(), calls=%async_computation.26 | async-start | bytes 5898240 | tf_op jit(solution)/shard_map/reduce_scatter | solution.py:315
  724.1 204.3 %reduce-scatter.24.cloned.1.call-start = ((), (), s32[]{:S(2)}) async-start(), calls=%async_computation.29 | async-start | bytes 221184 | tf_op jit(solution)/shard_map/reduce_scatter | solution.py:350
  734.4 212.9 %reduce-scatter.28.cloned.1.call-start = ((), (), s32[]{:S(2)}) async-start(), calls=%async_computation.31 | async-start | bytes 221184 | tf_op jit(solution)/shard_map/reduce_scatter | solution.py:356
  764.0 260.8 %reduce-scatter.34.cloned.1.call-start = ((), (), s32[]{:S(2)}) async-start(), calls=%async_computation.34 | async-start | bytes 7962624 | tf_op jit(solution)/shard_map/reduce_scatter | solution.py:197
  776.4 326.2 %reduce-scatter.36.cloned.1.call-start = ((), (), s32[]{:S(2)}) async-start(), calls=%async_computation.35 | async-start | bytes 7962624 | tf_op jit(solution)/shard_map/reduce_scatter | solution.py:200
  789.2 391.3 %reduce-scatter.38.cloned.1.call-start = ((), (), s32[]{:S(2)}) async-start(), calls=%async_computation.36 | async-start | bytes 7962624 | tf_op jit(solution)/shard_map/reduce_scatter | solution.py:203
  801.8 82.3 %copy-start.52 = (u32[32]{0:T(128)S(1)}, u32[32]{0:T(128)}, u32[]{:S(2)}) copy-start(u32[32]{0:T(128)} %constant.125) | copy-start | bytes 388
  801.8 84.2 %copy-start.51 = (u32[32]{0:T(128)S(1)}, u32[32]{0:T(128)}, u32[]{:S(2)}) copy-start(u32[32]{0:T(128)} %constant.129) | copy-start | bytes 388
  801.8 86.1 %copy-start.33 = (bf16[256,2,128]{2,0,1:T(8,128)(2,1)S(1)}, bf16[256,2,128]{2,0,1:T(8,128)(2,1)}, u32[]{:S(2)}) copy-start(bf16[256,2,128]{2,0,1:T(8,128)(2,1)} %copy-done.32) | copy-start | bytes 393220
  801.9 412.1 %reduce-scatter.32.cloned.1.call-start = ((), (), s32[]{:S(2)}) async-start(), calls=%async_computation.33 | async-start | bytes 1327104 | tf_op jit(solution)/shard_map/reduce_scatter | solution.py:362
  824.0 422.9 %reduce-scatter.20.cloned.1.call-start = ((), (), s32[]{:S(2)}) async-start(), calls=%async_computation.27 | async-start | bytes 1327104 | tf_op jit(solution)/shard_map/reduce_scatter | solution.py:344
  (56 other events, 589.1 us)
Sparse Core Ops, SparseCore 0:
  11.1 67.5 all-gather.8
  81.7 64.7 all-gather.10
  148.1 70.9 all-gather.14
  248.1 41.2 all-gather.12
  290.8 71.2 all-gather.16
  363.8 42.5 all-gather.20
  408.1 71.2 all-gather.18
  521.0 42.5 reduce-scatter.15
  566.6 43.9 reduce-scatter.13
  708.8 25.5 reduce-scatter.21
  737.9 26.0 reduce-scatter.25
  766.8 57.0 reduce-scatter.29
  827.0 57.0 reduce-scatter.17
  886.2 30.3 reduce-scatter.23
  918.7 28.4 reduce-scatter.27
  949.5 75.3 reduce-scatter.33
  1027.0 75.6 reduce-scatter.35
  1104.8 75.5 reduce-scatter.37
  1182.7 31.1 reduce-scatter.31
  1216.1 30.7 reduce-scatter.19
where the time goes:
time: 1260 us
  waiting for transfers between devices  750 us (60%)
  matrix products  185 us (15%)
  blocking collectives  180 us (14%)
  local copies, waits for them, and re-layouts  51.5 us (4%)
  other arithmetic  46.9 us (4%)
  between operations  18.4 us (1%)
  starting transfers between devices  15.9 us (1%)
    reduce_scatter x1, waiting for transfers between devices, shards(): lax.psum_scatter(grad_wgate.astype(jnp.bfloat16), 'dp', scatter_dimension...  76.2 us
    reduce_scatter x1, waiting for transfers between devices, shards(): lax.psum_scatter(grad_wup.astype(jnp.bfloat16), 'dp', scatter_dimension=0...  75.3 us
    reduce_scatter x1, waiting for transfers between devices, shards(): lax.psum_scatter(grad_down.astype(jnp.bfloat16), 'dp', scatter_dimension=...  75.3 us
    all_gather x1, waiting for transfers between devices, shards(): lax.all_gather(down_weight, 'dp', axis=1, tiled=True)  72.9 us
    unnamed x3, blocking collectives  70.9 us
    reduce_scatter x1, waiting for transfers between devices, shards(): lax.psum_scatter(grad_wquery.astype(jnp.bfloat16), 'seq', scatter_dimensi...  60.1 us
    all_gather x1, waiting for transfers between devices, shards(): lax.all_gather(up_weight, 'dp', axis=0, tiled=True)  59.5 us
    all_gather x1, blocking collectives, shards(): lax.all_gather(key_weight, ('seq', 'dp'), axis=0, tiled=True)  45 us
  transfers between devices with their start and end apart: 24, of which 20 were waited for; matrix products, arithmetic and copies ran while one was open for 14% of the time, Pallas kernels for 0%

commit v1 on v0

v1 whole, which is shorter than its diff:
```python
import jax
import jax.numpy as jnp
from jax import lax
from jax.sharding import PartitionSpec as P

H = 12
KEY_VALUE_HEADS = 2
HEAD_SIZE = 128
EPS = 1e-06
THETA = 1000000.0
SCALE = HEAD_SIZE ** (-0.5)
BF = jnp.bfloat16
F32 = jnp.float32


def dot(a, b, dims, out=F32):
    return lax.dot_general(a, b, (dims, ((), ())), preferred_element_type=F32).astype(out)


def nn(a, b, out=F32):
    return dot(a, b, ((1,), (0,)), out)


def nt(a, b, out=F32):
    return dot(a, b, ((1,), (1,)), out)


def tn(a, b, out=F32):
    return dot(a, b, ((0,), (0,)), out)


def rope_tables(positions):
    exponent = jnp.arange(0, HEAD_SIZE, 2).astype(F32) / HEAD_SIZE
    freqs = THETA ** (-exponent)
    angles = positions.astype(F32)[:, None] * freqs[None, :]
    angles = jnp.concatenate([angles, angles], axis=-1)
    return jnp.cos(angles), jnp.sin(angles)


def turn(u):
    half = u.shape[-1] // 2
    return jnp.concatenate([-u[..., half:], u[..., :half]], axis=-1)


def turn_back(w):
    half = w.shape[-1] // 2
    return jnp.concatenate([w[..., half:], -w[..., :half]], axis=-1)


def swap_seq(value, k):
    size = lax.axis_size("seq")
    return lax.ppermute(value, "seq", [(i, i ^ k) for i in range(size)])


def gather_seq(value):
    half = value.shape[0] // 2
    one = swap_seq(value, 1)
    two = swap_seq(value, 2)
    far = jnp.concatenate([swap_seq(two[:half], 1), swap_seq(one[half:], 2)], axis=0)
    return [value, one, two, far]


def scatter_seq(parts):
    low = [part.astype(BF) for part in parts[1:]]
    half = low[0].shape[0] // 2
    from_one = swap_seq(low[2][:half], 1)
    from_two = swap_seq(low[2][half:], 2)
    wide = [part.astype(F32) for part in parts]
    to_one = jnp.concatenate([wide[1][:half], wide[1][half:] + from_two.astype(F32)], axis=0).astype(BF)
    to_two = jnp.concatenate([wide[2][:half] + from_one.astype(F32), wide[2][half:]], axis=0).astype(BF)
    return wide[0] + swap_seq(to_one, 1).astype(F32) + swap_seq(to_two, 2).astype(F32)


def by_index(slots, index):
    stacked = jnp.stack(slots)
    return [
        lax.dynamic_index_in_dim(stacked, index ^ i, 0, keepdims=False) for i in range(len(slots))
    ]


def swap_core(value):
    size = lax.axis_size("dp")
    return lax.ppermute(value, "dp", [(i, i ^ 1) for i in range(size)])


def ring_gather(value):
    size = lax.axis_size("dp")
    chips = size // 2
    index = lax.axis_index("dp")
    chip, core = index // 2, index % 2
    blocks = [value]
    for _ in range(chips - 1):
        blocks.append(
            lax.ppermute(blocks[-1], "dp", [(i, (i - 2) % size) for i in range(size)])
        )
    own = jnp.stack(blocks)
    other = swap_core(own)
    both = jnp.where(core == 0, jnp.stack([own, other], 1), jnp.stack([other, own], 1))
    return lax.dynamic_slice_in_dim(jnp.concatenate([both, both], 0), chips - chip, chips, 0)


def ring_scatter(terms):
    size = lax.axis_size("dp")
    chips = size // 2
    index = lax.axis_index("dp")
    chip, core = index // 2, index % 2
    give = lax.dynamic_index_in_dim(terms, 1 - core, 1, keepdims=False)
    keep = lax.dynamic_index_in_dim(terms, core, 1, keepdims=False)
    got = swap_core(give)

    def term(which):
        pick = lambda field: lax.dynamic_index_in_dim(field, which, 0, keepdims=False).astype(F32)
        return pick(keep) + pick(got)

    came = None
    for step in range(chips - 1):
        send = term((chip + chips - 1 - step) % chips)
        if came is not None:
            send = send + came.astype(F32)
        came = lax.ppermute(send.astype(BF), "dp", [(i, (i + 2) % size) for i in range(size)])
    total = term(chip)
    return total if came is None else total + came.astype(F32)


def shards(
    inputs,
    block_ids,
    cotangent,
    first_gain,
    query_weight,
    query_bias,
    key_weight,
    key_bias,
    value_weight,
    value_bias,
    output_weight,
    second_gain,
    gate_weight,
    up_weight,
    down_weight,
):
    seqs = lax.axis_size("seq")
    seq = lax.axis_index("seq")
    dps = lax.axis_size("dp")
    dpi = lax.axis_index("dp")
    chips, chip, core = dps // 2, dpi // 2, dpi % 2
    heads = H // seqs
    copies = seqs // KEY_VALUE_HEADS
    wq = heads * HEAD_SIZE
    wide = wq + 2 * HEAD_SIZE
    tokens_here, model = inputs.shape[1:]
    share = first_gain.shape[0]
    kv_share = key_bias.shape[0]
    hidden_units = gate_weight.shape[1]

    small = jnp.concatenate([first_gain, second_gain, query_bias, key_bias, value_bias])
    small = jnp.concatenate(by_index([v[0] for v in gather_seq_small(small[None])], seq))
    packed = jnp.concatenate(
        [
            query_weight.reshape(share, seqs, wq),
            jnp.repeat(key_weight.reshape(share, KEY_VALUE_HEADS, HEAD_SIZE), copies, axis=1),
            jnp.repeat(value_weight.reshape(share, KEY_VALUE_HEADS, HEAD_SIZE), copies, axis=1),
        ],
        axis=-1,
    )
    rows = [
        lax.dynamic_index_in_dim(packed, seq ^ k, 1, keepdims=False) for k in range(seqs)
    ]
    rows = by_index([rows[0]] + [swap_seq(rows[k], k) for k in range(1, seqs)], seq)
    small_row = jnp.zeros((1, -(-small.shape[0] // wide) * wide), BF).at[0, : small.shape[0]].set(small)
    small_rows = small_row.reshape(-1, wide)
    extra = jnp.zeros((16, wide), BF).at[: small_rows.shape[0]].set(small_rows)
    qkv_pack = ring_gather(jnp.concatenate(rows + [extra], axis=0))
    out_head = ring_gather(output_weight).reshape(dps * share, model)
    weight_qkv = (
        qkv_pack[:, :, : seqs * share]
        .reshape(chips, 2, seqs, share, wide)
        .transpose(2, 0, 1, 3, 4)
        .reshape(model, wide)
    )
    smalls = qkv_pack[:, :, seqs * share : seqs * share + small_rows.shape[0]]
    smalls = smalls.reshape(dps, -1)[:, : small.shape[0]].reshape(dps, seqs, -1)
    smalls = smalls.transpose(1, 0, 2).astype(F32)
    gain_first = smalls[:, :, :share].reshape(model)
    gain_second = smalls[:, :, share : 2 * share].reshape(model)
    bias_q = lax.dynamic_index_in_dim(smalls, seq, 0, keepdims=False)[:, 2 * share : 3 * share].reshape(wq)
    group = seq // copies
    bias_k = smalls[:, :, 3 * share : 3 * share + kv_share].reshape(KEY_VALUE_HEADS, HEAD_SIZE)
    bias_v = smalls[:, :, 3 * share + kv_share :].reshape(KEY_VALUE_HEADS, HEAD_SIZE)
    bias = jnp.concatenate(
        [
            bias_q,
            lax.dynamic_index_in_dim(bias_k, group, 0, keepdims=False),
            lax.dynamic_index_in_dim(bias_v, group, 0, keepdims=False),
        ]
    )

    tokens = jnp.concatenate(gather_seq(inputs[0]), axis=0).astype(F32)
    blocks = jnp.concatenate(
        [block_ids[0]] + [swap_seq(block_ids[0], k) for k in range(1, seqs)], axis=0
    )
    positions = jnp.concatenate(
        [(seq ^ k) * tokens_here + jnp.arange(tokens_here, dtype=jnp.int32) for k in range(seqs)]
    )
    length = tokens.shape[0]
    cosine, sine = rope_tables(positions)

    half_rows = out_head.shape[0] // 2
    mine = jnp.stack(gather_seq(lax.dynamic_slice_in_dim(out_head, core * half_rows, half_rows, 0)))
    theirs = swap_core(mine)
    weight_out = jnp.where(
        core == 0, jnp.stack([mine, theirs], 1), jnp.stack([theirs, mine], 1)
    ).reshape(model, model)

    down_turned = down_weight.T
    whole_gate, whole_up, whole_down = (
        lax.all_gather(field, "dp", axis=0, tiled=True)
        for field in (gate_weight, up_weight, down_turned)
    )

    first_factor = lax.rsqrt(jnp.mean(tokens * tokens, axis=-1, keepdims=True) + EPS)
    normed = (tokens * first_factor * gain_first).astype(BF)
    pre = nn(normed, weight_qkv) + bias
    rotating = pre[:, : wq + HEAD_SIZE].reshape(length, heads + 1, HEAD_SIZE)
    rotated = (rotating * cosine[:, None] + turn(rotating) * sine[:, None]).astype(BF)
    queries, keys = rotated[:, :heads], rotated[:, heads]
    values = pre[:, wq + HEAD_SIZE :].astype(BF)
    allowed = blocks[None, :] <= blocks[:, None]

    scores = jnp.einsum("rhd,td->hrt", queries, keys, preferred_element_type=F32) * SCALE
    scores = jnp.where(allowed[None], scores, -1000000000.0)
    peak = jnp.max(scores, axis=-1, keepdims=True)
    raised = jnp.exp(scores - peak)
    total = jnp.sum(raised, axis=-1, keepdims=True)
    probs_low = (raised / total).astype(BF)
    logsum = peak + jnp.log(total)
    mixed = jnp.einsum("hrt,td->rhd", probs_low, values, preferred_element_type=F32).astype(BF)
    mixed = mixed.reshape(length, wq)
    all_mixed = []
    for k, field in enumerate(gather_seq(mixed)):
        split = field.reshape(seqs, tokens_here, wq)
        all_mixed.append(jnp.stack([split[i ^ k] for i in range(seqs)]).reshape(length, wq))
    hidden = tokens + nn(jnp.concatenate(all_mixed, axis=1), weight_out)

    incoming = jnp.concatenate(gather_seq(cotangent[0]), axis=0)
    second_factor = lax.rsqrt(jnp.mean(hidden * hidden, axis=-1, keepdims=True) + EPS)
    second = (hidden * second_factor * gain_second).astype(BF)
    gate = nn(second, whole_gate)
    up = nn(second, whole_up)
    back = nn(incoming, whole_down)
    sigma = jax.nn.sigmoid(gate)
    silu = gate * sigma
    active = (silu * up).astype(BF)
    grad_gate = (back * up * sigma * (1.0 + gate * (1.0 - sigma))).astype(BF)
    grad_up = (back * silu).astype(BF)
    second_sum = nt(grad_gate, whole_gate) + nt(grad_up, whole_up)
    out_sum = nt(active, whole_down)
    down_grad, gate_grad, up_grad = (
        lax.psum_scatter(tn(left, right, BF), "dp", scatter_dimension=0, tiled=True).astype(F32)
        for left, right in ((incoming, active), (second, grad_gate), (second, grad_up))
    )
    split = lambda field: [field[k * tokens_here : (k + 1) * tokens_here] for k in range(seqs)]
    grad_second = scatter_seq(split(second_sum))
    layer_out = (hidden[:tokens_here] + scatter_seq(split(out_sum))).astype(BF)

    gain_two_grad = jnp.sum(second_sum * (hidden * second_factor), axis=0)
    unit = hidden[:tokens_here] * second_factor[:tokens_here]
    scaled = grad_second * gain_second
    grad_hidden = cotangent[0].astype(F32) + second_factor[:tokens_here] * (
        scaled - unit * jnp.mean(scaled * unit, axis=-1, keepdims=True)
    )
    branch = jnp.concatenate(gather_seq(grad_hidden.astype(BF)), axis=0)
    out_weight_grad = tn(mixed, branch, BF)
    grad_mixed = nt(branch, out_head, BF).reshape(length, heads, HEAD_SIZE)

    probs = jnp.exp(scores - logsum)
    grad_probs = jnp.einsum("rhd,td->hrt", grad_mixed, values, preferred_element_type=F32)
    delta = jnp.sum(probs * grad_probs, axis=-1, keepdims=True)
    grad_scores = (probs * (grad_probs - delta)).astype(BF)
    grad_queries = jnp.einsum("hrt,td->rhd", grad_scores, keys, preferred_element_type=F32) * SCALE
    grad_keys = jnp.einsum("hrt,rhd->td", grad_scores, queries, preferred_element_type=F32) * SCALE
    grad_values = jnp.einsum(
        "hrt,rhd->td", probs.astype(BF), grad_mixed, preferred_element_type=F32
    )
    grad_rotated = jnp.concatenate([grad_queries, grad_keys[:, None]], axis=1)
    grad_rotating = grad_rotated * cosine[:, None] + turn_back(grad_rotated * sine[:, None])
    grad_pre = jnp.concatenate(
        [grad_rotating.reshape(length, wq + HEAD_SIZE), grad_values], axis=1
    ).astype(BF)
    grad_normed = nt(grad_pre, weight_qkv)
    unit = tokens * first_factor
    gain_one_grad = jnp.sum(grad_normed * unit, axis=0)
    grad_normed = scatter_seq(split(grad_normed))
    unit = unit[:tokens_here]
    scaled = grad_normed * gain_first
    input_grad = grad_hidden + first_factor[:tokens_here] * (
        scaled - unit * jnp.mean(scaled * unit, axis=-1, keepdims=True)
    )
    input_grad = input_grad.astype(BF)

    bias_grad = jnp.sum(grad_pre.astype(F32), axis=0)
    place = lambda field, count, at: jnp.where(
        (jnp.arange(count) == at)[:, None], field[None], 0.0
    ).reshape(seqs, dps, -1)
    small_grad = jnp.concatenate(
        [
            gain_one_grad.reshape(seqs, dps, share),
            gain_two_grad.reshape(seqs, dps, share),
            place(bias_grad[:wq], seqs, seq),
            place(bias_grad[wq : wq + HEAD_SIZE], KEY_VALUE_HEADS, group),
            place(bias_grad[wq + HEAD_SIZE :], KEY_VALUE_HEADS, group),
        ],
        axis=-1,
    )
    one = small_grad.shape[-1]
    small_grad = small_grad.transpose(1, 0, 2).reshape(dps, seqs * one).astype(BF)
    small_grad = jnp.pad(small_grad, ((0, 0), (0, small_rows.size - seqs * one)))
    small_grad = jnp.pad(
        small_grad.reshape(dps, -1, wide), ((0, 0), (0, 16 - small_rows.shape[0]), (0, 0))
    )
    qkv_grad = tn(normed, grad_pre, BF).reshape(seqs, dps, share, wide)
    qkv_grad = qkv_grad.transpose(1, 0, 2, 3).reshape(dps, seqs * share, wide)
    qkv_grad = ring_scatter(
        jnp.concatenate([qkv_grad, small_grad], axis=1).reshape(chips, 2, -1, wide)
    ).astype(BF)
    out_weight_grad = ring_scatter(out_weight_grad.reshape(chips, 2, share, model))
    smalls = qkv_grad[seqs * share : seqs * share + small_rows.shape[0]]
    smalls = smalls.reshape(-1)[: seqs * one].reshape(seqs, 1, one)
    smalls = jnp.pad(smalls, ((0, 0), (0, 15), (0, wide - one)))
    qkv_grad = qkv_grad[: seqs * share].reshape(seqs, share, wide)
    qkv_grad = jnp.concatenate([qkv_grad, smalls], axis=1)
    parts = [lax.dynamic_index_in_dim(qkv_grad, seq ^ k, 0, keepdims=False) for k in range(seqs)]
    parts = by_index([parts[0]] + [swap_seq(parts[k], k) for k in range(1, seqs)], seq)
    query_weight_grad = jnp.concatenate([part[:share, :wq] for part in parts], axis=1).astype(F32)
    pairs = [
        sum(part[:share, wq:].astype(F32) for part in parts[g * copies : (g + 1) * copies])
        for g in range(KEY_VALUE_HEADS)
    ]
    key_weight_grad = jnp.concatenate([pair[:, :HEAD_SIZE] for pair in pairs], axis=1)
    value_weight_grad = jnp.concatenate([pair[:, HEAD_SIZE:] for pair in pairs], axis=1)
    small_sum = sum(part[share, :one].astype(F32) for part in parts)
    gain_one_grad, gain_two_grad, query_bias_grad, key_bias_grad, value_bias_grad = jnp.split(
        small_sum, [share, 2 * share, 3 * share, 3 * share + kv_share]
    )

    return (
        layer_out[None],
        input_grad[None],
        gain_one_grad,
        query_weight_grad,
        query_bias_grad,
        key_weight_grad,
        key_bias_grad,
        value_weight_grad,
        value_bias_grad,
        out_weight_grad,
        gain_two_grad,
        gate_grad,
        up_grad,
        down_grad.T,
    )


def gather_seq_small(value):
    size = lax.axis_size("seq")
    return [value] + [swap_seq(value, k) for k in range(1, size)]


def solution(mesh):
    tokens = P("dp", "seq", None)
    whole = P(("seq", "dp"))
    matrix = P(("seq", "dp"), None)
    feed = P("dp", "seq")
    in_specs = (
        tokens,
        P("dp", "seq"),
        tokens,
        whole,
        matrix,
        whole,
        matrix,
        whole,
        matrix,
        whole,
        matrix,
        whole,
        feed,
        feed,
        P("seq", "dp"),
    )
    out_specs = (
        tokens,
        tokens,
        whole,
        matrix,
        whole,
        matrix,
        whole,
        matrix,
        whole,
        matrix,
        whole,
        feed,
        feed,
        P("seq", "dp"),
    )
    return jax.shard_map(shards, mesh=mesh, in_specs=in_specs, out_specs=out_specs, check_vma=False)
```

time: 1260 us -> 601 us (0.48)
  waiting for transfers between devices: 750 us -> 187 us
  blocking collectives: 180 us -> 0 us
  starting transfers between devices: 15.9 us -> 66.8 us
  other arithmetic: 46.9 us -> 73.9 us
  local copies, waits for them, and re-layouts: 51.5 us -> 77.6 us
  matrix products: 185 us -> 171 us
    reduce_scatter x13 -> x3, waiting for transfers between devices: 504 us -> 0.01 us  [shards(): lax.psum_scatter(tn(left, right, BF), 'dp', scatter_dimension=0, tiled=True)]
    all_gather x7 -> x3, waiting for transfers between devices: 203 us -> 0.02 us  [shards(): lax.all_gather(field, 'dp', axis=0, tiled=True)]
    ppermute x0 -> x61, waiting for transfers between devices: none -> 186 us  [the longest x44 110 us: swap_seq(): return lax.ppermute(value, 'seq', [(i, i ^ k) for i in range(size)])]
    all_gather x2 -> x0, blocking collectives: 89.3 us -> none  [the longest x1 45 us: shards(): lax.all_gather(key_weight, ('seq', 'dp'), axis=0, tiled=True)]
    unnamed x3 -> x0, blocking collectives: 70.9 us -> none
    ppermute x0 -> x61, starting transfers between devices: none -> 66.6 us  [the longest x44 53.8 us: swap_seq(): return lax.ppermute(value, 'seq', [(i, i ^ k) for i in range(size)])]
    all_to_all x4 -> x0, waiting for transfers between devices: 39 us -> none  [the longest x1 17.2 us: shards(): lax.all_to_all(packed, 'seq', split_axis=1, concat_axis=0, tiled=True)]
    all_to_all x1 -> x0, blocking collectives: 19.8 us -> none  [shards(): lax.all_to_all(returned.reshape(seq_length, 1, width_query + 2 * HEAD_SIZ...]
  transfers between devices with their start and end apart: 24 -> 67, of which waited for: 20 -> 29; matrix products, arithmetic and copies ran while one was open for 14% -> 46% of each run, Pallas kernels for 0% -> 0%
where the time goes in v1:
time: 601 us; the launch traced here: 593 us
  waiting for transfers between devices  187 us (31%)
  matrix products  171 us (28%)
  local copies, waits for them, and re-layouts  77.6 us (13%)
  other arithmetic  73.9 us (12%)
  starting transfers between devices  66.8 us (11%)
  between operations  15.8 us (3%)
    dot_general x15, matrix products, dot(): lax.dot_general(a, b, (dims, ((), ())), preferred_element_type=F32)  144 us
    ppermute x44, waiting for transfers between devices, swap_seq(): return lax.ppermute(value, 'seq', [(i, i ^ k) for i in range(size)])  110 us
    ppermute x44, starting transfers between devices, swap_seq(): return lax.ppermute(value, 'seq', [(i, i ^ k) for i in range(size)])  53.8 us
    ppermute x6, waiting for transfers between devices, ring_scatter(): lax.ppermute(send.astype(BF), 'dp', [(i, (i + 2) % size) for i in range(s...  41.3 us
    ppermute x6, waiting for transfers between devices, ring_gather(): lax.ppermute(blocks[-1], 'dp', [(i, (i - 2) % size) for i in range(size)])  34.3 us
    unnamed x118, local copies, waits for them, and re-layouts  23 us
  transfers between devices with their start and end apart: 67, of which 29 were waited for; matrix products, arithmetic and copies ran while one was open for 46% of the time, Pallas kernels for 0%

profile of v1, /device:TPU:0, one launch (start us, length us, event | category | flops | bytes accessed | tf_op | source)
XLA Modules:
  0.0 592.6 jit_solution(17398654796853441824)
XLA Ops:
  38.3 12.9 %collective-permute-done.4 = bf16[48,640]{1,0:T(8,128)(2,1)S(1)} collective-permute-done((bf16[48,640]{1,0:T(8,128)(2,1)S(1)}, bf16[48,640]{1,0:T(8,128)(2,1)S(1)}, u32[]{:S(2)}, u32[]{:S(2)}) %collective-permute-start.4) | collective-permute-done | bytes 61472 | tf_op jit(solution)/shard_map/ppermute | solution.py:52
  57.6 7.0 %collective-permute-done.21 = bf16[48,1536]{1,0:T(8,128)(2,1)S(1)} collective-permute-done((bf16[48,1536]{1,0:T(8,128)(2,1)S(1)}, bf16[48,1536]{1,0:T(8,128)(2,1)S(1)}, u32[]{:S(2)}, u32[]{:S(2)}) %collective-permute-start.21) | collective-permute-done | bytes 147488 | tf_op jit(solution)/shard_map/ppermute | solution.py:94
  68.7 22.1 %collective-permute-done.22 = bf16[48,1536]{1,0:T(8,128)(2,1)S(1)} collective-permute-done((bf16[48,1536]{1,0:T(8,128)(2,1)S(1)}, bf16[48,1536]{1,0:T(8,128)(2,1)S(1)}, u32[]{:S(2)}, u32[]{:S(2)}) %collective-permute-start.22) | collective-permute-done | bytes 147488 | tf_op jit(solution)/shard_map/ppermute | solution.py:94
  107.9 10.2 %collective-permute-done.35 = bf16[256,1536]{1,0:T(8,128)(2,1)S(1)} collective-permute-done((bf16[256,1536]{1,0:T(8,128)(2,1)S(1)}, bf16[256,1536]{1,0:T(8,128)(2,1)S(1)}, u32[]{:S(2)}, u32[]{:S(2)}) %collective-permute-start.35) | collective-permute-done | bytes 786464 | tf_op jit(solution)/shard_map/ppermute | solution.py:52
  126.6 6.6 %collective-permute-done.25 = bf16[192,1536]{1,0:T(8,128)(2,1)S(1)} collective-permute-done((bf16[192,1536]{1,0:T(8,128)(2,1)S(1)}, bf16[192,1536]{1,0:T(8,128)(2,1)S(1)}, u32[]{:S(2)}, u32[]{:S(2)}) %collective-permute-start.25) | collective-permute-done | bytes 589856 | tf_op jit(solution)/shard_map/ppermute | solution.py:52
  133.5 12.3 %collective-permute-done.26 = bf16[192,1536]{1,0:T(8,128)(2,1)S(1)} collective-permute-done((bf16[192,1536]{1,0:T(8,128)(2,1)S(1)}, bf16[192,1536]{1,0:T(8,128)(2,1)S(1)}, u32[]{:S(2)}, u32[]{:S(2)}) %collective-permute-start.26) | collective-permute-done | bytes 589856 | tf_op jit(solution)/shard_map/ppermute | solution.py:52
  210.7 12.7 %collective-permute-done.18 = bf16[1024,384]{1,0:T(8,128)(2,1)S(1)} collective-permute-done((bf16[1024,384]{1,0:T(8,128)(2,1)}, bf16[1024,384]{1,0:T(8,128)(2,1)S(1)}, u32[]{:S(2)}, u32[]{:S(2)}) %collective-permute-start.18) | collective-permute-done | bytes 786464 | tf_op jit(solution)/shard_map/ppermute | solution.py:52
  227.0 7.4 %collective-permute-done.20 = bf16[512,384]{1,0:T(8,128)(2,1)S(1)} collective-permute-done((bf16[512,384]{1,0:T(8,128)(2,1)S(1)}, bf16[512,384]{1,0:T(8,128)(2,1)S(1)}, u32[]{:S(2)}, u32[]{:S(2)}) %collective-permute-start.20) | collective-permute-done | bytes 393248 | tf_op jit(solution)/shard_map/ppermute | solution.py:52
  241.2 5.2 multiply_reduce_fusion.2
  249.7 13.0 %fusion.108 = f32[1024,2240]{0,1:T(8,128)} fusion(bf16[1024,1536]{1,0:T(8,128)(2,1)S(1)} %multiply_convert_fusion.3, bf16[1536,2240]{1,0:T(8,128)(2,1)} %all-gather.6.cloned.1.call-done), kind=kOutput, calls=%fused_computation.293 | convolution fusion | flops 7046430720 | bytes 19202048 | tf_op jit(solution)/shard_map/dot_general | solution.py:17
  262.6 11.9 %fusion.107 = f32[1024,2240]{0,1:T(8,128)} fusion(bf16[1024,1536]{1,0:T(8,128)(2,1)S(1)} %multiply_convert_fusion.3, bf16[1536,2240]{1,0:T(8,128)(2,1)} %all-gather.4.cloned.1.call-done), kind=kOutput, calls=%fused_computation.292 | convolution fusion | flops 7046430720 | bytes 19202048 | tf_op jit(solution)/shard_map/dot_general | solution.py:17
  274.5 20.4 %multiply_convert_fusion = (bf16[1024,2240]{0,1:T(8,128)(2,1)}, bf16[1024,2240]{0,1:T(8,128)(2,1)}, bf16[1024,2240]{0,1:T(8,128)(2,1)}) fusion(f32[1024,2240]{0,1:T(8,128)} %fusion.107, f32[1024,2240]{0,1:T(8,128)} %fusion.108, bf16[1024,1536]{1,0:T(8,128)(2,1)} %constant_dynamic-update-slice_fusion.6, bf16[1536,2240]{1,0:T(8,128)(2,1)} %all-gather.8.cloned.1.call-done), kind=kOutput, calls=%fused_computation.17 | convolution fusion | flops 7080837120 | bytes 42139648 | tf_op jit(solution)/shard_map/dot_general | solution.py:17
  294.9 11.7 %convolution_convert_fusion.1 = bf16[1536,2240]{1,0:T(8,128)(2,1)} fusion(bf16[1024,1536]{1,0:T(8,128)(2,1)S(1)} %multiply_convert_fusion.3, bf16[1024,2240]{0,1:T(8,128)(2,1)} %get-tuple-element.45), kind=kOutput, calls=%fused_computation.10 | convolution fusion | flops 7049871360 | bytes 14614528 | tf_op jit(solution)/shard_map/dot_general | solution.py:17
  308.6 11.7 %convolution_convert_fusion = bf16[1536,2240]{1,0:T(8,128)(2,1)} fusion(bf16[1024,1536]{1,0:T(8,128)(2,1)S(1)} %copy-done.32, bf16[1024,2240]{0,1:T(8,128)(2,1)} %get-tuple-element.47), kind=kOutput, calls=%fused_computation.9 | convolution fusion | flops 7049871360 | bytes 14614528 | tf_op jit(solution)/shard_map/dot_general | solution.py:17
  320.3 13.4 %fusion.109 = f32[1024,1536]{1,0:T(8,128)} fusion(bf16[1024,2240]{0,1:T(8,128)(2,1)} %get-tuple-element.46, bf16[1536,2240]{1,0:T(8,128)(2,1)} %all-gather.4.cloned.1.call-done), kind=kOutput, calls=%fused_computation.294 | convolution fusion | flops 7046430720 | bytes 17760256 | tf_op jit(solution)/shard_map/dot_general | solution.py:17
  333.7 14.1 %multiply_reduce_fusion = (bf16[1536]{0:T(1024)(128)(2,1)S(1)}, bf16[1024,1536]{1,0:T(8,128)(2,1)}, f32[1024,1536]{1,0:T(8,128)S(1)}) fusion(f32[1024,1536]{1,0:T(8,128)S(1)} %bitcast.289, f32[1024]{0:T(1024)S(1)} %add_rsqrt_fusion, f32[1024,1536]{1,0:T(8,128)} %fusion.109, bf16[1024,2240]{0,1:T(8,128)(2,1)} %get-tuple-element.45, ...), kind=kOutput, calls=%fused_computation.24 | convolution fusion | flops 7054293504 | bytes 33496064 | tf_op jit(solution)/shard_map/dot_general | solution.py:17
  352.7 11.6 %fusion.106 = (bf16[1024,1536]{1,0:T(8,128)(2,1)S(1)}, f32[1024,1536]{1,0:T(8,128)S(1)}) fusion(bf16[1024,2240]{0,1:T(8,128)(2,1)} %get-tuple-element.47, bf16[1536,2240]{1,0:T(8,128)(2,1)} %all-gather.8.cloned.1.call-done), kind=kOutput, calls=%fused_computation.291 | convolution fusion | flops 7048003584 | bytes 20905984 | tf_op jit(solution)/shard_map/dot_general | solution.py:17
  368.9 7.6 %collective-permute-done.32 = bf16[128,1536]{1,0:T(8,128)(2,1)S(1)} collective-permute-done((bf16[128,1536]{1,0:T(8,128)(2,1)S(1)}, bf16[128,1536]{1,0:T(8,128)(2,1)S(1)}, u32[]{:S(2)}, u32[]{:S(2)}) %collective-permute-start.32) | collective-permute-done | bytes 393248 | tf_op jit(solution)/shard_map/ppermute | solution.py:52
  382.7 12.1 %collective-permute-done.41 = bf16[256,1536]{1,0:T(8,128)(2,1)S(1)} collective-permute-done((bf16[256,1536]{1,0:T(8,128)(2,1)S(1)}, bf16[256,1536]{1,0:T(8,128)(2,1)S(1)}, u32[]{:S(2)}, u32[]{:S(2)}) %collective-permute-start.41) | collective-permute-done | bytes 786464 | tf_op jit(solution)/shard_map/ppermute | solution.py:52
  394.8 13.8 %collective-permute-done.33 = bf16[256,1536]{1,0:T(8,128)(2,1)} collective-permute-done((bf16[256,1536]{1,0:T(8,128)(2,1)}, bf16[256,1536]{1,0:T(8,128)(2,1)}, u32[]{:S(2)}, u32[]{:S(2)}) %collective-permute-start.33) | collective-permute-done | bytes 786464 | tf_op jit(solution)/shard_map/ppermute | solution.py:52
  408.6 4.5 multiply_reduce_fusion.4
  418.5 11.8 %convolution_convert_fusion.2 = bf16[1536,2240]{1,0:T(8,128)(2,1)} fusion(bf16[1024,1536]{1,0:T(8,128)(2,1)S(1)} %copy-done.16, bf16[1024,2240]{0,1:T(8,128)(2,1)} %get-tuple-element.46), kind=kOutput, calls=%fused_computation.11 | convolution fusion | flops 7049871360 | bytes 14614528 | tf_op jit(solution)/shard_map/dot_general | solution.py:17
  447.8 6.3 %fusion = (f32[3,1024]{1,0:T(4,128)S(1)}, f32[1024,1024,3]{1,0,2:T(8,128)S(1)}) fusion(f32[3,1024,1024]{1,2,0:T(8,128)} %copy-done, f32[3,1024]{1,0:T(4,128)S(1)} %log_add_fusion, bf16[1024,3,128]{0,2,1:T(8,128)(2,1)S(1)} %bitcast.306, f32[1024,640]{0,1:T(8,128)} %copy-done.23), kind=kOutput, calls=%fused_computation.2 | convolution fusion | flops 814740480 | bytes 26238976 | tf_op jit(solution)/shard_map/rhd,td->hrt/dot_general | solution.py:277
  456.4 5.6 fusion.2
  462.1 5.6 multiply_bitcast_fusion
  473.9 7.1 %fusion.36 = bf16[1024,128]{0,1:T(8,128)(2,1)S(1)} fusion(bf16[1024,3,128]{0,2,1:T(8,128)(2,1)S(1)} %bitcast.307, f32[3,1024,1024]{1,2,0:T(8,128)} %copy-done, f32[3,1024]{1,0:T(4,128)S(1)} %log_add_fusion), kind=kOutput, calls=%fused_computation.95 | convolution fusion | flops 811728896 | bytes 13643776 | tf_op jit(solution)/shard_map/hrt,rhd->td/dot_general | solution.py:282
  481.0 6.3 %multiply_reduce_fusion.1 = (bf16[1536]{0:T(1024)(128)(2,1)S(1)}, bf16[1024,1536]{1,0:T(8,128)(2,1)S(1)}, f32[1024,1536]{1,0:T(8,128)}, f32[1024,1536]{1,0:T(8,128)}) fusion(f32[1024]{0:T(1024)S(1)} %copy-done.42, bf16[1024,1536]{1,0:T(8,128)(2,1)S(1)} %copy-done.4, bf16[1536,640]{1,0:T(8,128)(2,1)S(1)} %bitcast.295, bf16[1024,128]{0,1:T(8,128)(2,1)S(1)} %fusion.36, ...), kind=kOutput, calls=%fused_computation.25 | convolution fusion | flops 2023750144 | bytes 22158336 | tf_op jit(solution)/shard_map/dot_general | solution.py:17
  493.5 4.5 convolution_convert_fusion.3
  516.1 9.2 %collective-permute-done.58 = bf16[48,1536]{1,0:T(8,128)(2,1)S(1)} collective-permute-done((bf16[48,1536]{1,0:T(8,128)(2,1)S(1)}, bf16[48,1536]{1,0:T(8,128)(2,1)S(1)}, u32[]{:S(2)}, u32[]{:S(2)}) %collective-permute-start.58) | collective-permute-done | bytes 147488 | tf_op jit(solution)/shard_map/ppermute | solution.py:120
  528.4 9.8 %collective-permute-done.59 = bf16[48,1536]{1,0:T(8,128)(2,1)S(1)} collective-permute-done((bf16[48,1536]{1,0:T(8,128)(2,1)S(1)}, bf16[48,1536]{1,0:T(8,128)(2,1)S(1)}, u32[]{:S(2)}, u32[]{:S(2)}) %collective-permute-start.59) | collective-permute-done | bytes 147488 | tf_op jit(solution)/shard_map/ppermute | solution.py:120
  539.3 10.3 %collective-permute-done.51 = bf16[208,640]{1,0:T(8,128)(2,1)S(1)} collective-permute-done((bf16[208,640]{1,0:T(8,128)(2,1)S(1)}, bf16[208,640]{1,0:T(8,128)(2,1)S(1)}, u32[]{:S(2)}, u32[]{:S(2)}) %collective-permute-start.51) | collective-permute-done | bytes 266272 | tf_op jit(solution)/shard_map/ppermute | solution.py:120
  561.4 5.2 collective-permute-done.53
  (424 shorter events, 253.0 us)
Async XLA Ops:
  7.2 242.5 %all-gather.6.cloned.1.call-start = ((), (), s32[]{:S(2)}) async-start(), calls=%async_computation.4 | async-start | bytes 7962624 | tf_op jit(solution)/shard_map/all_gather | solution.py:217
  7.9 254.7 %all-gather.4.cloned.1.call-start = ((), (), s32[]{:S(2)}) async-start(), calls=%async_computation.3 | async-start | bytes 7962624 | tf_op jit(solution)/shard_map/all_gather | solution.py:217
  8.7 265.8 %all-gather.8.cloned.1.call-start = ((), (), s32[]{:S(2)}) async-start(), calls=%async_computation.5 | async-start | bytes 7962624 | tf_op jit(solution)/shard_map/all_gather | solution.py:217
  20.6 557.4 %reduce-scatter.6.cloned.1.call-start = ((), (), s32[]{:S(2)}) async-start(), calls=%async_computation.7 | async-start | bytes 7962624 | tf_op jit(solution)/shard_map/reduce_scatter | solution.py:259
  29.7 71.3 %collective-permute-start.1 = (bf16[256,1536]{1,0:T(8,128)(2,1)}, bf16[256,1536]{1,0:T(8,128)(2,1)S(1)}, u32[]{:S(2)}, u32[]{:S(2)}) collective-permute-start(bf16[256,1536]{1,0:T(8,128)(2,1)} %bitcast.328), channel_id=1, source_target_pairs={{0,16},{8,24},{16,0},{24,8},{1,17},{9,25},{17,1},{25,9},{2,18},{10... | collective-permute-start | bytes 2359304 | tf_op jit(solution)/shard_map/ppermute | solution.py:52
  31.7 71.7 %collective-permute-start = (bf16[256,1536]{1,0:T(8,128)(2,1)}, bf16[256,1536]{1,0:T(8,128)(2,1)S(1)}, u32[]{:S(2)}, u32[]{:S(2)}) collective-permute-start(bf16[256,1536]{1,0:T(8,128)(2,1)} %bitcast.329), channel_id=1, source_target_pairs={{0,8},{8,0},{16,24},{24,16},{1,9},{9,1},{17,25},{25,17},{2,10},{10... | collective-permute-start | bytes 2359304 | tf_op jit(solution)/shard_map/ppermute | solution.py:52
  34.7 20.7 %collective-permute-start.5 = (bf16[48,640]{1,0:T(8,128)(2,1)S(1)}, bf16[48,640]{1,0:T(8,128)(2,1)S(1)}, u32[]{:S(2)}, u32[]{:S(2)}) collective-permute-start(bf16[48,640]{1,0:T(8,128)(2,1)S(1)} %bitcast.353), channel_id=1, source_target_pairs={{0,16},{8,24},{16,0},{24,8},{1,17},{9,25},{17,1},{25,9},{2,18},{10... | collective-permute-start | bytes 184328 | tf_op jit(solution)/shard_map/ppermute | solution.py:52
  34.7 22.1 %collective-permute-start.6 = (bf16[48,640]{1,0:T(8,128)(2,1)S(1)}, bf16[48,640]{1,0:T(8,128)(2,1)S(1)}, u32[]{:S(2)}, u32[]{:S(2)}) collective-permute-start(bf16[48,640]{1,0:T(8,128)(2,1)S(1)} %bitcast.352), channel_id=1, source_target_pairs={{0,24},{8,16},{16,8},{24,0},{1,25},{9,17},{17,9},{25,1},{2,26},{10... | collective-permute-start | bytes 184328 | tf_op jit(solution)/shard_map/ppermute | solution.py:52
  55.4 50.0 %collective-permute-start.34 = (bf16[256,1536]{1,0:T(8,128)(2,1)}, bf16[256,1536]{1,0:T(8,128)(2,1)S(1)}, u32[]{:S(2)}, u32[]{:S(2)}) collective-permute-start(bf16[256,1536]{1,0:T(8,128)(2,1)} %bitcast.311), channel_id=1, source_target_pairs={{0,8},{8,0},{16,24},{24,16},{1,9},{9,1},{17,25},{25,17},{2,10},{10... | collective-permute-start | bytes 2359304 | tf_op jit(solution)/shard_map/ppermute | solution.py:52
  57.0 34.6 %collective-permute-start.10 = (bf16[208,640]{1,0:T(8,128)(2,1)S(1)}, bf16[208,640]{1,0:T(8,128)(2,1)S(1)}, u32[]{:S(2)}, u32[]{:S(2)}) collective-permute-start(bf16[208,640]{1,0:T(8,128)(2,1)S(1)} %constant_dynamic-update-slice_fusion.5), channel_id=1, source_target_pairs={{0,6},{1,7},{2,0},{3,1},{4,2},{5,3},{6,4},{7,5},{8,14},{9,15},{10,... | collective-permute-start | bytes 798728 | tf_op jit(solution)/shard_map/ppermute | solution.py:94
  64.6 26.2 %collective-permute-start.22 = (bf16[48,1536]{1,0:T(8,128)(2,1)S(1)}, bf16[48,1536]{1,0:T(8,128)(2,1)S(1)}, u32[]{:S(2)}, u32[]{:S(2)}) collective-permute-start(bf16[48,1536]{1,0:T(8,128)(2,1)S(1)} %collective-permute-done.21), channel_id=1, source_target_pairs={{0,6},{1,7},{2,0},{3,1},{4,2},{5,3},{6,4},{7,5},{8,14},{9,15},{10,... | collective-permute-start | bytes 442376 | tf_op jit(solution)/shard_map/ppermute | solution.py:94
  97.6 20.5 %collective-permute-start.35 = (bf16[256,1536]{1,0:T(8,128)(2,1)S(1)}, bf16[256,1536]{1,0:T(8,128)(2,1)S(1)}, u32[]{:S(2)}, u32[]{:S(2)}) collective-permute-start(bf16[256,1536]{1,0:T(8,128)(2,1)S(1)} %bitcast.312), channel_id=1, source_target_pairs={{0,16},{8,24},{16,0},{24,8},{1,17},{9,25},{17,1},{25,9},{2,18},{10... | collective-permute-start | bytes 2359304 | tf_op jit(solution)/shard_map/ppermute | solution.py:52
  103.5 21.2 %collective-permute-start.2 = (bf16[128,1536]{1,0:T(8,128)(2,1)S(1)}, bf16[128,1536]{1,0:T(8,128)(2,1)S(1)}, u32[]{:S(2)}, u32[]{:S(2)}) collective-permute-start(bf16[128,1536]{1,0:T(8,128)(2,1)S(1)} %slice.504), channel_id=1, source_target_pairs={{0,8},{8,0},{16,24},{24,16},{1,9},{9,1},{17,25},{25,17},{2,10},{10... | collective-permute-start | bytes 1179656 | tf_op jit(solution)/shard_map/ppermute | solution.py:52
  105.4 21.1 %collective-permute-start.3 = (bf16[128,1536]{1,0:T(8,128)(2,1)S(1)}, bf16[128,1536]{1,0:T(8,128)(2,1)S(1)}, u32[]{:S(2)}, u32[]{:S(2)}) collective-permute-start(bf16[128,1536]{1,0:T(8,128)(2,1)S(1)} %slice.505), channel_id=1, source_target_pairs={{0,16},{8,24},{16,0},{24,8},{1,17},{9,25},{17,1},{25,9},{2,18},{10... | collective-permute-start | bytes 1179656 | tf_op jit(solution)/shard_map/ppermute | solution.py:52
  118.1 89.8 %collective-permute-start.37 = (bf16[128,1536]{1,0:T(8,128)(2,1)S(1)}, bf16[128,1536]{1,0:T(8,128)(2,1)}, u32[]{:S(2)}, u32[]{:S(2)}) collective-permute-start(bf16[128,1536]{1,0:T(8,128)(2,1)S(1)} %slice.548), channel_id=1, source_target_pairs={{0,16},{8,24},{16,0},{24,8},{1,17},{9,25},{17,1},{25,9},{2,18},{10... | collective-permute-start | bytes 1179656 | tf_op jit(solution)/shard_map/ppermute | solution.py:52
  123.2 22.6 %collective-permute-start.26 = (bf16[192,1536]{1,0:T(8,128)(2,1)S(1)}, bf16[192,1536]{1,0:T(8,128)(2,1)S(1)}, u32[]{:S(2)}, u32[]{:S(2)}) collective-permute-start(bf16[192,1536]{1,0:T(8,128)(2,1)S(1)} %constant_dynamic-slice_fusion.1), channel_id=1, source_target_pairs={{0,16},{8,24},{16,0},{24,8},{1,17},{9,25},{17,1},{25,9},{2,18},{10... | collective-permute-start | bytes 1769480 | tf_op jit(solution)/shard_map/ppermute | solution.py:52
  124.7 81.5 %collective-permute-start.36 = (bf16[128,1536]{1,0:T(8,128)(2,1)}, bf16[128,1536]{1,0:T(8,128)(2,1)}, u32[]{:S(2)}, u32[]{:S(2)}) collective-permute-start(bf16[128,1536]{1,0:T(8,128)(2,1)} %slice.547), channel_id=1, source_target_pairs={{0,8},{8,0},{16,24},{24,16},{1,9},{9,1},{17,25},{25,17},{2,10},{10... | collective-permute-start | bytes 1179656 | tf_op jit(solution)/shard_map/ppermute | solution.py:52
  126.5 29.0 %collective-permute-start.13 = (bf16[4,208,640]{2,1,0:T(8,128)(2,1)S(1)}, bf16[4,208,640]{2,1,0:T(8,128)(2,1)S(1)}, u32[]{:S(2)}, u32[]{:S(2)}) collective-permute-start(bf16[4,208,640]{2,1,0:T(8,128)(2,1)S(1)} %get-tuple-element.80), channel_id=1, source_target_pairs={{0,1},{1,0},{2,3},{3,2},{4,5},{5,4},{6,7},{7,6},{8,9},{9,8},{10,11... | collective-permute-start | bytes 3194888 | tf_op jit(solution)/shard_map/ppermute | solution.py:83
  155.5 80.3 %collective-permute-start.29 = (bf16[4,192,1536]{2,1,0:T(8,128)(2,1)}, bf16[4,192,1536]{2,1,0:T(8,128)(2,1)}, u32[]{:S(2)}, u32[]{:S(2)}) collective-permute-start(bf16[4,192,1536]{2,1,0:T(8,128)(2,1)} %get-tuple-element.74), channel_id=1, source_target_pairs={{0,1},{1,0},{2,3},{3,2},{4,5},{5,4},{6,7},{7,6},{8,9},{9,8},{10,11... | collective-permute-start | bytes 7077896 | tf_op jit(solution)/shard_map/ppermute | solution.py:83
  203.1 20.2 %collective-permute-start.18 = (bf16[1024,384]{1,0:T(8,128)(2,1)}, bf16[1024,384]{1,0:T(8,128)(2,1)S(1)}, u32[]{:S(2)}, u32[]{:S(2)}) collective-permute-start(bf16[1024,384]{1,0:T(8,128)(2,1)} %copy.124), channel_id=1, source_target_pairs={{0,16},{8,24},{16,0},{24,8},{1,17},{9,25},{17,1},{25,9},{2,18},{10... | collective-permute-start | bytes 2359304 | tf_op jit(solution)/shard_map/ppermute | solution.py:52
  204.8 20.2 %collective-permute-start.17 = (bf16[1024,384]{1,0:T(8,128)(2,1)}, bf16[1024,384]{1,0:T(8,128)(2,1)S(1)}, u32[]{:S(2)}, u32[]{:S(2)}) collective-permute-start(bf16[1024,384]{1,0:T(8,128)(2,1)} %copy.124), channel_id=1, source_target_pairs={{0,8},{8,0},{16,24},{24,16},{1,9},{9,1},{17,25},{25,17},{2,10},{10... | collective-permute-start | bytes 2359304 | tf_op jit(solution)/shard_map/ppermute | solution.py:52
  306.7 273.9 %reduce-scatter.8.cloned.1.call-start = ((), (), s32[]{:S(2)}) async-start(), calls=%async_computation.8 | async-start | bytes 7962624 | tf_op jit(solution)/shard_map/reduce_scatter | solution.py:259
  320.3 262.8 %reduce-scatter.4.cloned.1.call-start = ((), (), s32[]{:S(2)}) async-start(), calls=%async_computation.6 | async-start | bytes 7962624 | tf_op jit(solution)/shard_map/reduce_scatter | solution.py:259
  366.6 28.1 %collective-permute-start.41 = (bf16[256,1536]{1,0:T(8,128)(2,1)S(1)}, bf16[256,1536]{1,0:T(8,128)(2,1)S(1)}, u32[]{:S(2)}, u32[]{:S(2)}) collective-permute-start(bf16[256,1536]{1,0:T(8,128)(2,1)S(1)} %pad_maximum_fusion.11), channel_id=1, source_target_pairs={{0,16},{8,24},{16,0},{24,8},{1,17},{9,25},{17,1},{25,9},{2,18},{10... | collective-permute-start | bytes 2359304 | tf_op jit(solution)/shard_map/ppermute | solution.py:52
  368.3 26.5 %collective-permute-start.39 = (bf16[256,1536]{1,0:T(8,128)(2,1)S(1)}, bf16[256,1536]{1,0:T(8,128)(2,1)S(1)}, u32[]{:S(2)}, u32[]{:S(2)}) collective-permute-start(bf16[256,1536]{1,0:T(8,128)(2,1)S(1)} %pad_maximum_fusion.10), channel_id=1, source_target_pairs={{0,8},{8,0},{16,24},{24,16},{1,9},{9,1},{17,25},{25,17},{2,10},{10... | collective-permute-start | bytes 2359304 | tf_op jit(solution)/shard_map/ppermute | solution.py:52
  379.0 29.6 %collective-permute-start.33 = (bf16[256,1536]{1,0:T(8,128)(2,1)}, bf16[256,1536]{1,0:T(8,128)(2,1)}, u32[]{:S(2)}, u32[]{:S(2)}) collective-permute-start(bf16[256,1536]{1,0:T(8,128)(2,1)} %pad_maximum_fusion.9), channel_id=1, source_target_pairs={{0,16},{8,24},{16,0},{24,8},{1,17},{9,25},{17,1},{25,9},{2,18},{10... | collective-permute-start | bytes 2359304 | tf_op jit(solution)/shard_map/ppermute | solution.py:52
  380.5 28.1 %collective-permute-start.31 = (bf16[256,1536]{1,0:T(8,128)(2,1)}, bf16[256,1536]{1,0:T(8,128)(2,1)}, u32[]{:S(2)}, u32[]{:S(2)}) collective-permute-start(bf16[256,1536]{1,0:T(8,128)(2,1)} %pad_maximum_fusion.8), channel_id=1, source_target_pairs={{0,8},{8,0},{16,24},{24,16},{1,9},{9,1},{17,25},{25,17},{2,10},{10... | collective-permute-start | bytes 2359304 | tf_op jit(solution)/shard_map/ppermute | solution.py:52
  488.5 22.5 %collective-permute-start.48 = (bf16[128,1536]{1,0:T(8,128)(2,1)}, bf16[128,1536]{1,0:T(8,128)(2,1)}, u32[]{:S(2)}, u32[]{:S(2)}) collective-permute-start(bf16[128,1536]{1,0:T(8,128)(2,1)} %get-tuple-element.63), channel_id=1, source_target_pairs={{0,8},{8,0},{16,24},{24,16},{1,9},{9,1},{17,25},{25,17},{2,10},{10... | collective-permute-start | bytes 1179656 | tf_op jit(solution)/shard_map/ppermute | solution.py:52
  489.1 21.9 %collective-permute-start.46 = (bf16[128,1536]{1,0:T(8,128)(2,1)}, bf16[128,1536]{1,0:T(8,128)(2,1)}, u32[]{:S(2)}, u32[]{:S(2)}) collective-permute-start(bf16[128,1536]{1,0:T(8,128)(2,1)} %get-tuple-element.64), channel_id=1, source_target_pairs={{0,16},{8,24},{16,0},{24,8},{1,17},{9,25},{17,1},{25,9},{2,18},{10... | collective-permute-start | bytes 1179656 | tf_op jit(solution)/shard_map/ppermute | solution.py:52
  515.5 42.9 %collective-permute-start.49 = (bf16[256,1536]{1,0:T(8,128)(2,1)S(1)}, bf16[256,1536]{1,0:T(8,128)(2,1)S(1)}, u32[]{:S(2)}, u32[]{:S(2)}) collective-permute-start(bf16[256,1536]{1,0:T(8,128)(2,1)S(1)} %pad_maximum_fusion.13), channel_id=1, source_target_pairs={{0,16},{8,24},{16,0},{24,8},{1,17},{9,25},{17,1},{25,9},{2,18},{10... | collective-permute-start | bytes 2359304 | tf_op jit(solution)/shard_map/ppermute | solution.py:52
  526.4 32.0 %collective-permute-start.47 = (bf16[256,1536]{1,0:T(8,128)(2,1)S(1)}, bf16[256,1536]{1,0:T(8,128)(2,1)S(1)}, u32[]{:S(2)}, u32[]{:S(2)}) collective-permute-start(bf16[256,1536]{1,0:T(8,128)(2,1)S(1)} %pad_maximum_fusion.12), channel_id=1, source_target_pairs={{0,8},{8,0},{16,24},{24,16},{1,9},{9,1},{17,25},{25,17},{2,10},{10... | collective-permute-start | bytes 2359304 | tf_op jit(solution)/shard_map/ppermute | solution.py:52
  528.3 21.2 %collective-permute-start.51 = (bf16[208,640]{1,0:T(8,128)(2,1)S(1)}, bf16[208,640]{1,0:T(8,128)(2,1)S(1)}, u32[]{:S(2)}, u32[]{:S(2)}) collective-permute-start(bf16[208,640]{1,0:T(8,128)(2,1)S(1)} %fusion.53), channel_id=1, source_target_pairs={{0,2},{1,3},{2,4},{3,5},{4,6},{5,7},{6,0},{7,1},{8,10},{9,11},{10,... | collective-permute-start | bytes 798728 | tf_op jit(solution)/shard_map/ppermute | solution.py:120
  (85 other events, 944.2 us)
Sparse Core Ops, SparseCore 0:
  9.7 86.4 all-gather.5
  97.8 78.3 all-gather.3
  177.8 69.8 all-gather.7
  306.8 75.7 reduce-scatter.5
  384.8 75.5 reduce-scatter.7
  462.6 87.8 reduce-scatter.3

commit v2 on v1

--- a/solution.py
+++ b/solution.py
@@ -1,6 +1,8 @@
 import jax
 import jax.numpy as jnp
 from jax import lax
+from jax.experimental import pallas as pl
+from jax.experimental.pallas import tpu as pltpu
 from jax.sharding import PartitionSpec as P
 
 H = 12
@@ -83,20 +85,135 @@
     return lax.ppermute(value, "dp", [(i, i ^ 1) for i in range(size)])
 
 
-def ring_gather(value):
-    size = lax.axis_size("dp")
-    chips = size // 2
-    index = lax.axis_index("dp")
-    chip, core = index // 2, index % 2
-    blocks = [value]
-    for _ in range(chips - 1):
-        blocks.append(
-            lax.ppermute(blocks[-1], "dp", [(i, (i - 2) % size) for i in range(size)])
+def start_kernel(
+    x_in, ids_in, small_in, pack_in, out_in,
+    x_out, ids_out, small_out, pack_out, out_out,
+    local_sem, seq_send, seq_recv, far_send, far_recv, ring_send, ring_recv, core_send, core_recv,
+):
+    seqs, dps = lax.axis_size("seq"), lax.axis_size("dp")
+    chips = dps // 2
+    seq, dpi = lax.axis_index("seq"), lax.axis_index("dp")
+    chip, core = dpi // 2, dpi % 2
+    ahead = ((chip + chips - 1) % chips) * 2 + core
+    behind = ((chip + 1) % chips) * 2 + core
+    sibling = chip * 2 + 1 - core
+
+    barrier = pltpu.get_barrier_semaphore()
+    for k in range(1, seqs):
+        pl.semaphore_signal(barrier, inc=1, device_id=(seq ^ k, dpi), device_id_type=pl.DeviceIdType.MESH)
+    for other in (ahead, behind, sibling):
+        pl.semaphore_signal(barrier, inc=1, device_id=(seq, other), device_id_type=pl.DeviceIdType.MESH)
+    pl.semaphore_wait(barrier, seqs + 2)
+
+    rows = x_in.shape[0]
+    half = rows // 2
+
+    def remote(src, dst, send, recv, where):
+        return pltpu.make_async_remote_copy(
+            src_ref=src, dst_ref=dst, send_sem=send, recv_sem=recv,
+            device_id=where, device_id_type=pl.DeviceIdType.MESH,
         )
-    own = jnp.stack(blocks)
-    other = swap_core(own)
-    both = jnp.where(core == 0, jnp.stack([own, other], 1), jnp.stack([other, own], 1))
-    return lax.dynamic_slice_in_dim(jnp.concatenate([both, both], 0), chips - chip, chips, 0)
+
+    small_sends = [
+        remote(small_in, small_out.at[dpi, seq], seq_send.at[0, k], seq_recv.at[0, k], (seq ^ k, dpi))
+        for k in range(1, seqs)
+    ]
+    pack_sends = [
+        remote(
+            pack_in.at[seq ^ k], pack_out.at[seq, dpi], seq_send.at[1, k], seq_recv.at[1, k], (seq ^ k, dpi)
+        )
+        for k in range(1, seqs)
+    ]
+    id_sends = [
+        remote(ids_in, ids_out.at[k], seq_send.at[2, k], seq_recv.at[2, k], (seq ^ k, dpi))
+        for k in range(1, seqs)
+    ]
+    x_sends = [
+        remote(x_in, x_out.at[pl.ds(k * rows, rows)], seq_send.at[3, k], seq_recv.at[3, k], (seq ^ k, dpi))
+        for k in (1, 2)
+    ]
+    locals_ = [
+        pltpu.make_async_copy(small_in, small_out.at[dpi, seq], local_sem.at[0]),
+        pltpu.make_async_copy(pack_in.at[seq], pack_out.at[seq, dpi], local_sem.at[1]),
+        pltpu.make_async_copy(out_in, out_out.at[dpi], local_sem.at[2]),
+        pltpu.make_async_copy(ids_in, ids_out.at[0], local_sem.at[3]),
+        pltpu.make_async_copy(x_in, x_out.at[pl.ds(0, rows)], local_sem.at[4]),
+    ]
+    for copy in small_sends + pack_sends + locals_[:3] + id_sends + x_sends + locals_[3:]:
+        copy.start()
+    for copy in locals_[:3] + small_sends + pack_sends:
+        copy.wait()
+
+    far_sends = [
+        remote(
+            x_out.at[pl.ds(2 * rows, half)], x_out.at[pl.ds(3 * rows, half)],
+            far_send.at[0], far_recv.at[0], (seq ^ 1, dpi),
+        ),
+        remote(
+            x_out.at[pl.ds(rows + half, half)], x_out.at[pl.ds(3 * rows + half, half)],
+            far_send.at[1], far_recv.at[1], (seq ^ 2, dpi),
+        ),
+    ]
+
+    def hop_sends(hop, to_core):
+        block = ((chip + hop) % chips) * 2 + core
+        send, recv = (core_send, core_recv) if to_core else (ring_send, ring_recv)
+        where = (seq, sibling) if to_core else (seq, ahead)
+        return [
+            remote(field, field, send.at[i, hop], recv.at[i, hop], where)
+            for i, field in enumerate((small_out.at[block], pack_out.at[:, block], out_out.at[block]))
+        ]
+
+    flying = []
+    for hop in range(chips):
+        if hop > 0:
+            for copy in rings:
+                copy.wait_recv()
+            flying += rings
+        rings = hop_sends(hop, False) if hop < chips - 1 else []
+        cores = hop_sends(hop, True)
+        for copy in rings + cores:
+            copy.start()
+        flying += cores
+        if hop == 0:
+            for copy in x_sends:
+                copy.wait()
+            for copy in far_sends:
+                copy.start()
+    for copy in flying:
+        copy.wait_send()
+    for hop in range(chips):
+        for copy in hop_sends(hop, True):
+            copy.wait_recv()
+    for copy in far_sends + id_sends + locals_[3:]:
+        copy.wait()
+
+
+def start_call(x, ids, small, pack, out):
+    seqs, dps = lax.axis_size("seq"), lax.axis_size("dp")
+    chips = dps // 2
+    share, wide = pack.shape[1:]
+    any_space = pl.BlockSpec(memory_space=pl.ANY)
+    shapes = (
+        jax.ShapeDtypeStruct((seqs * x.shape[0], x.shape[1]), x.dtype),
+        jax.ShapeDtypeStruct((seqs,) + ids.shape, ids.dtype),
+        jax.ShapeDtypeStruct((dps, seqs) + small.shape, small.dtype),
+        jax.ShapeDtypeStruct((seqs, dps, share, wide), pack.dtype),
+        jax.ShapeDtypeStruct((dps,) + out.shape, out.dtype),
+    )
+    dma = pltpu.SemaphoreType.DMA
+    return pl.pallas_call(
+        start_kernel,
+        out_shape=shapes,
+        in_specs=[any_space] * 5,
+        out_specs=(any_space,) * 5,
+        scratch_shapes=[
+            dma((5,)), dma((4, seqs)), dma((4, seqs)), dma((2,)), dma((2,)),
+            dma((3, chips)), dma((3, chips)), dma((3, chips)), dma((3, chips)),
+        ],
+        compiler_params=pltpu.CompilerParams(collective_id=0, has_side_effects=True),
+        name="start_gather",
+    )(x, ids, small, pack, out)
 
 
 def ring_scatter(terms):
@@ -154,7 +271,6 @@
     hidden_units = gate_weight.shape[1]
 
     small = jnp.concatenate([first_gain, second_gain, query_bias, key_bias, value_bias])
-    small = jnp.concatenate(by_index([v[0] for v in gather_seq_small(small[None])], seq))
     packed = jnp.concatenate(
         [
             query_weight.reshape(share, seqs, wq),
@@ -162,25 +278,17 @@
             jnp.repeat(value_weight.reshape(share, KEY_VALUE_HEADS, HEAD_SIZE), copies, axis=1),
         ],
         axis=-1,
-    )
-    rows = [
-        lax.dynamic_index_in_dim(packed, seq ^ k, 1, keepdims=False) for k in range(seqs)
-    ]
-    rows = by_index([rows[0]] + [swap_seq(rows[k], k) for k in range(1, seqs)], seq)
-    small_row = jnp.zeros((1, -(-small.shape[0] // wide) * wide), BF).at[0, : small.shape[0]].set(small)
-    small_rows = small_row.reshape(-1, wide)
-    extra = jnp.zeros((16, wide), BF).at[: small_rows.shape[0]].set(small_rows)
-    qkv_pack = ring_gather(jnp.concatenate(rows + [extra], axis=0))
-    out_head = ring_gather(output_weight).reshape(dps * share, model)
-    weight_qkv = (
-        qkv_pack[:, :, : seqs * share]
-        .reshape(chips, 2, seqs, share, wide)
-        .transpose(2, 0, 1, 3, 4)
-        .reshape(model, wide)
-    )
-    smalls = qkv_pack[:, :, seqs * share : seqs * share + small_rows.shape[0]]
-    smalls = smalls.reshape(dps, -1)[:, : small.shape[0]].reshape(dps, seqs, -1)
-    smalls = smalls.transpose(1, 0, 2).astype(F32)
+    ).transpose(1, 0, 2)
+    one = small.shape[0]
+    small = jnp.pad(small[None], ((0, 15), (0, -one % 128)))
+    tokens, blocks, smalls, weight_qkv, out_head = start_call(
+        inputs[0], block_ids.reshape(-1, 128), small, packed, output_weight
+    )
+    tokens = tokens.astype(F32)
+    blocks = blocks.reshape(-1)
+    weight_qkv = weight_qkv.reshape(model, wide)
+    out_head = out_head.reshape(dps * share, model)
+    smalls = smalls[:, :, 0, :one].transpose(1, 0, 2).astype(F32)
     gain_first = smalls[:, :, :share].reshape(model)
     gain_second = smalls[:, :, share : 2 * share].reshape(model)
     bias_q = lax.dynamic_index_in_dim(smalls, seq, 0, keepdims=False)[:, 2 * share : 3 * share].reshape(wq)
@@ -193,11 +301,6 @@
             lax.dynamic_index_in_dim(bias_k, group, 0, keepdims=False),
             lax.dynamic_index_in_dim(bias_v, group, 0, keepdims=False),
         ]
-    )
-
-    tokens = jnp.concatenate(gather_seq(inputs[0]), axis=0).astype(F32)
-    blocks = jnp.concatenate(
-        [block_ids[0]] + [swap_seq(block_ids[0], k) for k in range(1, seqs)], axis=0
     )
     positions = jnp.concatenate(
         [(seq ^ k) * tokens_here + jnp.arange(tokens_here, dtype=jnp.int32) for k in range(seqs)]
@@ -242,23 +345,23 @@
         all_mixed.append(jnp.stack([split[i ^ k] for i in range(seqs)]).reshape(length, wq))
     hidden = tokens + nn(jnp.concatenate(all_mixed, axis=1), weight_out)
 
-    incoming = jnp.concatenate(gather_seq(cotangent[0]), axis=0)
+    incoming = jnp.concatenate(gather_seq(lax.optimization_barrier((cotangent, tokens))[0][0]), axis=0)
     second_factor = lax.rsqrt(jnp.mean(hidden * hidden, axis=-1, keepdims=True) + EPS)
     second = (hidden * second_factor * gain_second).astype(BF)
     gate = nn(second, whole_gate)
     up = nn(second, whole_up)
-    back = nn(incoming, whole_down)
     sigma = jax.nn.sigmoid(gate)
     silu = gate * sigma
     active = (silu * up).astype(BF)
+    scatter = lambda field: lax.psum_scatter(field, "dp", scatter_dimension=0, tiled=True)
+    down_grad = scatter(tn(incoming, active, BF)).astype(F32)
+    back = nn(incoming, whole_down)
     grad_gate = (back * up * sigma * (1.0 + gate * (1.0 - sigma))).astype(BF)
     grad_up = (back * silu).astype(BF)
     second_sum = nt(grad_gate, whole_gate) + nt(grad_up, whole_up)
     out_sum = nt(active, whole_down)
-    down_grad, gate_grad, up_grad = (
-        lax.psum_scatter(tn(left, right, BF), "dp", scatter_dimension=0, tiled=True).astype(F32)
-        for left, right in ((incoming, active), (second, grad_gate), (second, grad_up))
-    )
+    gate_grad = scatter(tn(second, grad_gate, BF)).astype(F32)
+    up_grad = scatter(tn(second, grad_up, BF)).astype(F32)
     split = lambda field: [field[k * tokens_here : (k + 1) * tokens_here] for k in range(seqs)]
     grad_second = scatter_seq(split(second_sum))
     layer_out = (hidden[:tokens_here] + scatter_seq(split(out_sum))).astype(BF)
@@ -312,19 +415,17 @@
         ],
         axis=-1,
     )
-    one = small_grad.shape[-1]
+    small_rows = -(-seqs * one // wide)
     small_grad = small_grad.transpose(1, 0, 2).reshape(dps, seqs * one).astype(BF)
-    small_grad = jnp.pad(small_grad, ((0, 0), (0, small_rows.size - seqs * one)))
-    small_grad = jnp.pad(
-        small_grad.reshape(dps, -1, wide), ((0, 0), (0, 16 - small_rows.shape[0]), (0, 0))
-    )
+    small_grad = jnp.pad(small_grad, ((0, 0), (0, small_rows * wide - seqs * one)))
+    small_grad = jnp.pad(small_grad.reshape(dps, -1, wide), ((0, 0), (0, 16 - small_rows), (0, 0)))
     qkv_grad = tn(normed, grad_pre, BF).reshape(seqs, dps, share, wide)
     qkv_grad = qkv_grad.transpose(1, 0, 2, 3).reshape(dps, seqs * share, wide)
     qkv_grad = ring_scatter(
         jnp.concatenate([qkv_grad, small_grad], axis=1).reshape(chips, 2, -1, wide)
     ).astype(BF)
     out_weight_grad = ring_scatter(out_weight_grad.reshape(chips, 2, share, model))
-    smalls = qkv_grad[seqs * share : seqs * share + small_rows.shape[0]]
+    smalls = qkv_grad[seqs * share : seqs * share + small_rows]
     smalls = smalls.reshape(-1)[: seqs * one].reshape(seqs, 1, one)
     smalls = jnp.pad(smalls, ((0, 0), (0, 15), (0, wide - one)))
     qkv_grad = qkv_grad[: seqs * share].reshape(seqs, share, wide)
@@ -361,11 +462,6 @@
     )
 
 
-def gather_seq_small(value):
-    size = lax.axis_size("seq")
-    return [value] + [swap_seq(value, k) for k in range(1, size)]
-
-
 def solution(mesh):
     tokens = P("dp", "seq", None)
     whole = P(("seq", "dp"))

time: 601 us -> 586 us (0.975)
  Pallas kernels: 0 us -> 90.4 us
  waiting for transfers between devices: 187 us -> 130 us
  starting transfers between devices: 66.8 us -> 35.8 us
  local copies, waits for them, and re-layouts: 77.6 us -> 58.3 us
  other arithmetic: 73.9 us -> 61.6 us
  matrix products: 171 us -> 183 us
    pallas_call x0 -> x1, Pallas kernels: none -> 90.4 us  [start_call(): pl.pallas_call(start_kernel, out_shape=shapes, in_specs=[any_space] * 5,...]
    ppermute x44 -> x31, waiting for transfers between devices: 110 us -> 75.1 us  [swap_seq(): return lax.ppermute(value, 'seq', [(i, i ^ k) for i in range(size)])]
    ppermute x6 -> x0, waiting for transfers between devices: 34.3 us -> none  [ring_gather(): lax.ppermute(blocks[-1], 'dp', [(i, (i - 2) % size) for i in range(size)])]
    ppermute x44 -> x31, starting transfers between devices: 53.8 us -> 34.3 us  [swap_seq(): return lax.ppermute(value, 'seq', [(i, i ^ k) for i in range(size)])]
    ppermute x6, waiting for transfers between devices: 41.3 us -> 53.5 us  [ring_scatter(): lax.ppermute(send.astype(BF), 'dp', [(i, (i + 2) % size) for i in range(s...]
    dot_general x15, matrix products: 144 us -> 155 us  [dot(): lax.dot_general(a, b, (dims, ((), ())), preferred_element_type=F32)]
    ppermute x6 -> x0, starting transfers between devices: 10.2 us -> none  [ring_gather(): lax.ppermute(blocks[-1], 'dp', [(i, (i - 2) % size) for i in range(size)])]
    unnamed x118 -> x109, local copies, waits for them, and re-layouts: 23 us -> 20.9 us
  transfers between devices with their start and end apart: 67 -> 46, of which waited for: 29 -> 16; matrix products, arithmetic and copies ran while one was open for 46% -> 45% of each run, Pallas kernels for 0% -> 16%
where the time goes in v2:
time: 586 us; the launch traced here: 575 us
  matrix products  183 us (31%)
  waiting for transfers between devices  130 us (22%)
  Pallas kernels  90.4 us (15%)
  other arithmetic  61.6 us (11%)
  local copies, waits for them, and re-layouts  58.3 us (10%)
  starting transfers between devices  35.8 us (6%)
  between operations  15.8 us (3%)
    dot_general x15, matrix products, dot(): lax.dot_general(a, b, (dims, ((), ())), preferred_element_type=F32)  155 us
    pallas_call x1, Pallas kernels, start_call(): pl.pallas_call(start_kernel, out_shape=shapes, in_specs=[any_space] * 5,...  90.4 us
    ppermute x31, waiting for transfers between devices, swap_seq(): return lax.ppermute(value, 'seq', [(i, i ^ k) for i in range(size)])  75.1 us
    ppermute x6, waiting for transfers between devices, ring_scatter(): lax.ppermute(send.astype(BF), 'dp', [(i, (i + 2) % size) for i in range(s...  53.5 us
    ppermute x31, starting transfers between devices, swap_seq(): return lax.ppermute(value, 'seq', [(i, i ^ k) for i in range(size)])  34.3 us
    unnamed x109, local copies, waits for them, and re-layouts  20.9 us
  transfers between devices with their start and end apart: 46, of which 16 were waited for; matrix products, arithmetic and copies ran while one was open for 45% of the time, Pallas kernels for 16%

profile of v2, /device:TPU:0, one launch (start us, length us, event | category | flops | bytes accessed | tf_op | source)
XLA Modules:
  0.0 575.1 jit_solution(11439988049746555003)
XLA Ops:
  19.8 90.4 %start_gather.1 = (bf16[1024,1536]{1,0:T(8,128)(2,1)}, s32[4,2,128]{2,1,0:T(2,128)}, bf16[8,4,16,256]{3,2,1,0:T(8,128)(2,1)}, bf16[4,8,48,640]{3,2,1,0:T(8,128)(2,1)}, bf16[8,48,1536]{2,1,0:T(8,128)(2,1)}) custom-call(bf16[256,1536]{1,0:T(8,128)(2,1)} %bitcast.308, s32[2,128]{1,0:T(2,128)} %bitcast.321, bf16[16,256]{1,0:T(8,128)(2,1)} %pad.12.small_in, ...), custom_call_target="tpu_custom_call" | custom-call | tf_op jit(solution)/shard_map/start_gather/pallas_call | solution.py:205
  153.2 18.7 %collective-permute-done.7 = bf16[96,1536]{1,0:T(8,128)(2,1)S(1)} collective-permute-done((bf16[96,1536]{1,0:T(8,128)(2,1)S(1)}, bf16[96,1536]{1,0:T(8,128)(2,1)S(1)}, u32[]{:S(2)}, u32[]{:S(2)}) %collective-permute-start.7) | collective-permute-done | bytes 294944 | tf_op jit(solution)/shard_map/ppermute | solution.py:54
  186.7 6.0 %collective-permute-done = bf16[1024,384]{1,0:T(8,128)(2,1)} collective-permute-done((bf16[1024,384]{1,0:T(8,128)(2,1)}, bf16[1024,384]{1,0:T(8,128)(2,1)}, u32[]{:S(2)}, u32[]{:S(2)}) %collective-permute-start) | collective-permute-done | bytes 786464 | tf_op jit(solution)/shard_map/ppermute | solution.py:54
  201.5 5.9 %collective-permute-done.3 = bf16[512,384]{1,0:T(8,128)(2,1)S(1)} collective-permute-done((bf16[512,384]{1,0:T(8,128)(2,1)S(1)}, bf16[512,384]{1,0:T(8,128)(2,1)S(1)}, u32[]{:S(2)}, u32[]{:S(2)}) %collective-permute-start.3) | collective-permute-done | bytes 393248 | tf_op jit(solution)/shard_map/ppermute | solution.py:54
  212.7 5.2 multiply_reduce_fusion.2
  221.2 13.1 %fusion.99 = f32[1024,2240]{0,1:T(8,128)} fusion(bf16[1024,1536]{1,0:T(8,128)(2,1)S(1)} %multiply_convert_fusion.3, bf16[1536,2240]{1,0:T(8,128)(2,1)} %all-gather.6.cloned.1.call-done), kind=kOutput, calls=%fused_computation.254 | convolution fusion | flops 7046430720 | bytes 19202048 | tf_op jit(solution)/shard_map/dot_general | solution.py:19
  234.3 22.5 %fusion.98 = f32[1024,2240]{0,1:T(8,128)} fusion(bf16[1024,1536]{1,0:T(8,128)(2,1)S(1)} %multiply_convert_fusion.3, bf16[1536,2240]{1,0:T(8,128)(2,1)} %all-gather.4.cloned.1.call-done), kind=kOutput, calls=%fused_computation.253 | convolution fusion | flops 7046430720 | bytes 19202048 | tf_op jit(solution)/shard_map/dot_general | solution.py:19
  256.8 20.0 %multiply_convert_fusion = (bf16[1024,2240]{0,1:T(8,128)(2,1)}, bf16[1024,2240]{0,1:T(8,128)(2,1)}, bf16[1024,2240]{0,1:T(8,128)(2,1)}) fusion(f32[1024,2240]{0,1:T(8,128)} %fusion.98, f32[1024,2240]{0,1:T(8,128)} %fusion.99, bf16[1024,1536]{1,0:T(8,128)(2,1)} %constant_dynamic-update-slice_fusion, bf16[1536,2240]{1,0:T(8,128)(2,1)} %all-gather.8.cloned.1.call-done), kind=kOutput, calls=%fused_computation.14 | convolution fusion | flops 7080837120 | bytes 42139648 | tf_op jit(solution)/shard_map/dot_general | solution.py:19
  276.8 11.7 %convolution_convert_fusion.1 = bf16[1536,2240]{1,0:T(8,128)(2,1)} fusion(bf16[1024,1536]{1,0:T(8,128)(2,1)S(1)} %multiply_convert_fusion.3, bf16[1024,2240]{0,1:T(8,128)(2,1)} %get-tuple-element.29), kind=kOutput, calls=%fused_computation.10 | convolution fusion | flops 7049871360 | bytes 14614528 | tf_op jit(solution)/shard_map/dot_general | solution.py:19
  290.4 11.7 %convolution_convert_fusion = bf16[1536,2240]{1,0:T(8,128)(2,1)} fusion(bf16[1024,1536]{1,0:T(8,128)(2,1)S(1)} %copy-done.34, bf16[1024,2240]{0,1:T(8,128)(2,1)} %get-tuple-element.31), kind=kOutput, calls=%fused_computation.9 | convolution fusion | flops 7049871360 | bytes 14614528 | tf_op jit(solution)/shard_map/dot_general | solution.py:19
  302.2 13.8 %fusion.100 = f32[1024,1536]{1,0:T(8,128)} fusion(bf16[1024,2240]{0,1:T(8,128)(2,1)} %get-tuple-element.30, bf16[1536,2240]{1,0:T(8,128)(2,1)} %all-gather.4.cloned.1.call-done), kind=kOutput, calls=%fused_computation.255 | convolution fusion | flops 7046430720 | bytes 17760256 | tf_op jit(solution)/shard_map/dot_general | solution.py:19
  316.0 14.1 %multiply_reduce_fusion = (bf16[1536]{0:T(1024)(128)(2,1)S(1)}, bf16[1024,1536]{1,0:T(8,128)(2,1)}, f32[1024,1536]{1,0:T(8,128)S(1)}) fusion(f32[1024,1536]{1,0:T(8,128)S(1)} %bitcast.269, f32[1024]{0:T(1024)S(1)} %add_rsqrt_fusion, f32[1024,1536]{1,0:T(8,128)} %fusion.100, bf16[1024,2240]{0,1:T(8,128)(2,1)} %get-tuple-element.29, ...), kind=kOutput, calls=%fused_computation.20 | convolution fusion | flops 7054293504 | bytes 33496064 | tf_op jit(solution)/shard_map/dot_general | solution.py:19
  335.4 11.5 %fusion.97 = (bf16[1024,1536]{1,0:T(8,128)(2,1)S(1)}, f32[1024,1536]{1,0:T(8,128)S(1)}) fusion(bf16[1024,2240]{0,1:T(8,128)(2,1)} %get-tuple-element.31, bf16[1536,2240]{1,0:T(8,128)(2,1)} %all-gather.8.cloned.1.call-done), kind=kOutput, calls=%fused_computation.252 | convolution fusion | flops 7048003584 | bytes 20905984 | tf_op jit(solution)/shard_map/dot_general | solution.py:19
  351.6 7.5 %collective-permute-done.11 = bf16[128,1536]{1,0:T(8,128)(2,1)S(1)} collective-permute-done((bf16[128,1536]{1,0:T(8,128)(2,1)S(1)}, bf16[128,1536]{1,0:T(8,128)(2,1)S(1)}, u32[]{:S(2)}, u32[]{:S(2)}) %collective-permute-start.11) | collective-permute-done | bytes 393248 | tf_op jit(solution)/shard_map/ppermute | solution.py:54
  364.0 12.5 %collective-permute-done.20 = bf16[256,1536]{1,0:T(8,128)(2,1)S(1)} collective-permute-done((bf16[256,1536]{1,0:T(8,128)(2,1)S(1)}, bf16[256,1536]{1,0:T(8,128)(2,1)S(1)}, u32[]{:S(2)}, u32[]{:S(2)}) %collective-permute-start.20) | collective-permute-done | bytes 786464 | tf_op jit(solution)/shard_map/ppermute | solution.py:54
  376.6 15.2 %collective-permute-done.12 = bf16[256,1536]{1,0:T(8,128)(2,1)} collective-permute-done((bf16[256,1536]{1,0:T(8,128)(2,1)}, bf16[256,1536]{1,0:T(8,128)(2,1)}, u32[]{:S(2)}, u32[]{:S(2)}) %collective-permute-start.12) | collective-permute-done | bytes 786464 | tf_op jit(solution)/shard_map/ppermute | solution.py:54
  391.8 4.5 multiply_reduce_fusion.5
  396.4 4.2 constant_dynamic-update-slice_fusion.9
  402.6 11.8 %convolution_convert_fusion.2 = bf16[1536,2240]{1,0:T(8,128)(2,1)} fusion(bf16[1024,1536]{1,0:T(8,128)(2,1)S(1)} %copy-done.14, bf16[1024,2240]{0,1:T(8,128)(2,1)} %get-tuple-element.30), kind=kOutput, calls=%fused_computation.11 | convolution fusion | flops 7049871360 | bytes 14614528 | tf_op jit(solution)/shard_map/dot_general | solution.py:19
  423.1 4.1 collective-permute-done.23
  432.7 6.3 %fusion = (f32[3,1024]{1,0:T(4,128)S(1)}, f32[1024,1024,3]{1,0,2:T(8,128)S(1)}) fusion(f32[3,1024,1024]{1,2,0:T(8,128)} %copy-done.2, f32[3,1024]{1,0:T(4,128)S(1)} %log_add_fusion, bf16[1024,3,128]{0,2,1:T(8,128)(2,1)S(1)} %bitcast.280, f32[1024,640]{0,1:T(8,128)} %copy-done.20), kind=kOutput, calls=%fused_computation.2 | convolution fusion | flops 814740480 | bytes 26238976 | tf_op jit(solution)/shard_map/rhd,td->hrt/dot_general | solution.py:380
  441.3 5.4 fusion.2
  446.8 6.2 %multiply_bitcast_fusion = f32[1024,3,128]{2,0,1:T(8,128)S(1)} fusion(bf16[3,1024,1024]{1,2,0:T(8,128)(2,1)} %fusion.2, bf16[1024,4,128]{2,0,1:T(8,128)(2,1)S(1)} %copy-done.23), kind=kOutput, calls=%fused_computation.73 | convolution fusion | flops 805699584 | bytes 8126464 | tf_op jit(solution)/shard_map/hrt,td->rhd/dot_general | solution.py:383
  457.3 7.2 %fusion.34 = bf16[1024,128]{0,1:T(8,128)(2,1)S(1)} fusion(bf16[1024,3,128]{0,2,1:T(8,128)(2,1)S(1)} %bitcast.281, f32[3,1024,1024]{1,2,0:T(8,128)} %copy-done.2, f32[3,1024]{1,0:T(4,128)S(1)} %log_add_fusion), kind=kOutput, calls=%fused_computation.88 | convolution fusion | flops 811728896 | bytes 13643776 | tf_op jit(solution)/shard_map/hrt,rhd->td/dot_general | solution.py:385
  464.5 6.3 %multiply_reduce_fusion.1 = (bf16[1536]{0:T(1024)(128)(2,1)S(1)}, bf16[1024,1536]{1,0:T(8,128)(2,1)S(1)}, f32[1024,1536]{1,0:T(8,128)}, f32[1024,1536]{1,0:T(8,128)}) fusion(f32[1024]{0:T(1024)S(1)} %copy-done.43, bf16[1024,1536]{1,0:T(8,128)(2,1)S(1)} %copy-done.7, bf16[1536,640]{1,0:T(8,128)(2,1)S(1)} %bitcast.288, bf16[1024,128]{0,1:T(8,128)(2,1)S(1)} %fusion.34, ...), kind=kOutput, calls=%fused_computation.21 | convolution fusion | flops 2023750144 | bytes 22158336 | tf_op jit(solution)/shard_map/dot_general | solution.py:19
  475.9 4.7 convolution_convert_fusion.3
  487.4 10.8 %collective-permute-done.37 = bf16[48,1536]{1,0:T(8,128)(2,1)S(1)} collective-permute-done((bf16[48,1536]{1,0:T(8,128)(2,1)S(1)}, bf16[48,1536]{1,0:T(8,128)(2,1)S(1)}, u32[]{:S(2)}, u32[]{:S(2)}) %collective-permute-start.37) | collective-permute-done | bytes 147488 | tf_op jit(solution)/shard_map/ppermute | solution.py:237
  500.3 10.8 %collective-permute-done.38 = bf16[48,1536]{1,0:T(8,128)(2,1)S(1)} collective-permute-done((bf16[48,1536]{1,0:T(8,128)(2,1)S(1)}, bf16[48,1536]{1,0:T(8,128)(2,1)S(1)}, u32[]{:S(2)}, u32[]{:S(2)}) %collective-permute-start.38) | collective-permute-done | bytes 147488 | tf_op jit(solution)/shard_map/ppermute | solution.py:237
  512.2 10.4 %collective-permute-done.30 = bf16[208,640]{1,0:T(8,128)(2,1)S(1)} collective-permute-done((bf16[208,640]{1,0:T(8,128)(2,1)S(1)}, bf16[208,640]{1,0:T(8,128)(2,1)S(1)}, u32[]{:S(2)}, u32[]{:S(2)}) %collective-permute-start.30) | collective-permute-done | bytes 266272 | tf_op jit(solution)/shard_map/ppermute | solution.py:237
  522.8 6.1 %collective-permute-done.39 = bf16[48,1536]{1,0:T(8,128)(2,1)S(1)} collective-permute-done((bf16[48,1536]{1,0:T(8,128)(2,1)S(1)}, bf16[48,1536]{1,0:T(8,128)(2,1)S(1)}, u32[]{:S(2)}, u32[]{:S(2)}) %collective-permute-start.39) | collective-permute-done | bytes 147488 | tf_op jit(solution)/shard_map/ppermute | solution.py:237
  530.5 9.2 %collective-permute-done.31 = bf16[208,640]{1,0:T(8,128)(2,1)S(1)} collective-permute-done((bf16[208,640]{1,0:T(8,128)(2,1)S(1)}, bf16[208,640]{1,0:T(8,128)(2,1)S(1)}, u32[]{:S(2)}, u32[]{:S(2)}) %collective-permute-start.31) | collective-permute-done | bytes 266272 | tf_op jit(solution)/shard_map/ppermute | solution.py:237
  542.7 6.1 %collective-permute-done.32 = bf16[208,640]{1,0:T(8,128)(2,1)S(1)} collective-permute-done((bf16[208,640]{1,0:T(8,128)(2,1)S(1)}, bf16[208,640]{1,0:T(8,128)(2,1)S(1)}, u32[]{:S(2)}, u32[]{:S(2)}) %collective-permute-start.32) | collective-permute-done | bytes 266272 | tf_op jit(solution)/shard_map/ppermute | solution.py:237
  (349 shorter events, 165.3 us)
Async XLA Ops:
  7.2 214.0 %all-gather.6.cloned.1.call-start = ((), (), s32[]{:S(2)}) async-start(), calls=%async_computation.4 | async-start | bytes 7962624 | tf_op jit(solution)/shard_map/all_gather | solution.py:320
  7.9 226.4 %all-gather.4.cloned.1.call-start = ((), (), s32[]{:S(2)}) async-start(), calls=%async_computation.3 | async-start | bytes 7962624 | tf_op jit(solution)/shard_map/all_gather | solution.py:320
  8.7 248.1 %all-gather.8.cloned.1.call-start = ((), (), s32[]{:S(2)}) async-start(), calls=%async_computation.5 | async-start | bytes 7962624 | tf_op jit(solution)/shard_map/all_gather | solution.py:320
  8.7 171.8 %collective-permute-start.14 = (bf16[256,1536]{1,0:T(8,128)(2,1)}, bf16[256,1536]{1,0:T(8,128)(2,1)}, u32[]{:S(2)}, u32[]{:S(2)}) collective-permute-start(bf16[256,1536]{1,0:T(8,128)(2,1)} %bitcast.285), channel_id=1, source_target_pairs={{0,16},{8,24},{16,0},{24,8},{1,17},{9,25},{17,1},{25,9},{2,18},{10... | collective-permute-start | bytes 2359304 | tf_op jit(solution)/shard_map/ppermute | solution.py:54
  11.8 171.2 %collective-permute-start.13 = (bf16[256,1536]{1,0:T(8,128)(2,1)}, bf16[256,1536]{1,0:T(8,128)(2,1)}, u32[]{:S(2)}, u32[]{:S(2)}) collective-permute-start(bf16[256,1536]{1,0:T(8,128)(2,1)} %bitcast.286), channel_id=1, source_target_pairs={{0,8},{8,0},{16,24},{24,16},{1,9},{9,1},{17,25},{25,17},{2,10},{10... | collective-permute-start | bytes 2359304 | tf_op jit(solution)/shard_map/ppermute | solution.py:54
  112.3 34.4 %collective-permute-start.4 = (bf16[192,1536]{1,0:T(8,128)(2,1)}, bf16[192,1536]{1,0:T(8,128)(2,1)}, u32[]{:S(2)}, u32[]{:S(2)}) collective-permute-start(bf16[192,1536]{1,0:T(8,128)(2,1)} %constant_dynamic-slice_fusion.1), channel_id=1, source_target_pairs={{0,8},{8,0},{16,24},{24,16},{1,9},{9,1},{17,25},{25,17},{2,10},{10... | collective-permute-start | bytes 1769480 | tf_op jit(solution)/shard_map/ppermute | solution.py:54
  113.7 36.4 %collective-permute-start.5 = (bf16[192,1536]{1,0:T(8,128)(2,1)}, bf16[192,1536]{1,0:T(8,128)(2,1)}, u32[]{:S(2)}, u32[]{:S(2)}) collective-permute-start(bf16[192,1536]{1,0:T(8,128)(2,1)} %constant_dynamic-slice_fusion.1), channel_id=1, source_target_pairs={{0,16},{8,24},{16,0},{24,8},{1,17},{9,25},{17,1},{25,9},{2,18},{10... | collective-permute-start | bytes 1769480 | tf_op jit(solution)/shard_map/ppermute | solution.py:54
  115.2 445.1 %reduce-scatter.6.cloned.1.call-start = ((), (), s32[]{:S(2)}) async-start(), calls=%async_computation.7 | async-start | bytes 7962624 | tf_op jit(solution)/shard_map/reduce_scatter | solution.py:356
  146.1 38.6 %collective-permute-start.1 = (bf16[1024,384]{1,0:T(8,128)(2,1)}, bf16[1024,384]{1,0:T(8,128)(2,1)}, u32[]{:S(2)}, u32[]{:S(2)}) collective-permute-start(bf16[1024,384]{1,0:T(8,128)(2,1)} %copy.61), channel_id=1, source_target_pairs={{0,16},{8,24},{16,0},{24,8},{1,17},{9,25},{17,1},{25,9},{2,18},{10... | collective-permute-start | bytes 2359304 | tf_op jit(solution)/shard_map/ppermute | solution.py:54
  147.6 24.2 %collective-permute-start.7 = (bf16[96,1536]{1,0:T(8,128)(2,1)S(1)}, bf16[96,1536]{1,0:T(8,128)(2,1)S(1)}, u32[]{:S(2)}, u32[]{:S(2)}) collective-permute-start(bf16[96,1536]{1,0:T(8,128)(2,1)S(1)} %slice.491), channel_id=1, source_target_pairs={{0,16},{8,24},{16,0},{24,8},{1,17},{9,25},{17,1},{25,9},{2,18},{10... | collective-permute-start | bytes 884744 | tf_op jit(solution)/shard_map/ppermute | solution.py:54
  151.8 23.6 %collective-permute-start.6 = (bf16[96,1536]{1,0:T(8,128)(2,1)}, bf16[96,1536]{1,0:T(8,128)(2,1)}, u32[]{:S(2)}, u32[]{:S(2)}) collective-permute-start(bf16[96,1536]{1,0:T(8,128)(2,1)} %slice.490), channel_id=1, source_target_pairs={{0,8},{8,0},{16,24},{24,16},{1,9},{9,1},{17,25},{25,17},{2,10},{10... | collective-permute-start | bytes 884744 | tf_op jit(solution)/shard_map/ppermute | solution.py:54
  171.9 20.8 %collective-permute-start = (bf16[1024,384]{1,0:T(8,128)(2,1)}, bf16[1024,384]{1,0:T(8,128)(2,1)}, u32[]{:S(2)}, u32[]{:S(2)}) collective-permute-start(bf16[1024,384]{1,0:T(8,128)(2,1)} %copy.61), channel_id=1, source_target_pairs={{0,8},{8,0},{16,24},{24,16},{1,9},{9,1},{17,25},{25,17},{2,10},{10... | collective-permute-start | bytes 2359304 | tf_op jit(solution)/shard_map/ppermute | solution.py:54
  179.4 29.8 %collective-permute-start.8 = (bf16[4,192,1536]{2,1,0:T(8,128)(2,1)}, bf16[4,192,1536]{2,1,0:T(8,128)(2,1)}, u32[]{:S(2)}, u32[]{:S(2)}) collective-permute-start(bf16[4,192,1536]{2,1,0:T(8,128)(2,1)} %get-tuple-element.58), channel_id=1, source_target_pairs={{0,1},{1,0},{2,3},{3,2},{4,5},{5,4},{6,7},{7,6},{8,9},{9,8},{10,11... | collective-permute-start | bytes 7077896 | tf_op jit(solution)/shard_map/ppermute | solution.py:85
  181.6 26.1 %collective-permute-start.15 = (bf16[128,1536]{1,0:T(8,128)(2,1)S(1)}, bf16[128,1536]{1,0:T(8,128)(2,1)S(1)}, u32[]{:S(2)}, u32[]{:S(2)}) collective-permute-start(bf16[128,1536]{1,0:T(8,128)(2,1)S(1)} %slice.501), channel_id=1, source_target_pairs={{0,8},{8,0},{16,24},{24,16},{1,9},{9,1},{17,25},{25,17},{2,10},{10... | collective-permute-start | bytes 1179656 | tf_op jit(solution)/shard_map/ppermute | solution.py:54
  184.0 24.4 %collective-permute-start.16 = (bf16[128,1536]{1,0:T(8,128)(2,1)S(1)}, bf16[128,1536]{1,0:T(8,128)(2,1)S(1)}, u32[]{:S(2)}, u32[]{:S(2)}) collective-permute-start(bf16[128,1536]{1,0:T(8,128)(2,1)S(1)} %slice.502), channel_id=1, source_target_pairs={{0,16},{8,24},{16,0},{24,8},{1,17},{9,25},{17,1},{25,9},{2,18},{10... | collective-permute-start | bytes 1179656 | tf_op jit(solution)/shard_map/ppermute | solution.py:54
  185.7 21.7 %collective-permute-start.3 = (bf16[512,384]{1,0:T(8,128)(2,1)S(1)}, bf16[512,384]{1,0:T(8,128)(2,1)S(1)}, u32[]{:S(2)}, u32[]{:S(2)}) collective-permute-start(bf16[512,384]{1,0:T(8,128)(2,1)S(1)} %slice.487), channel_id=1, source_target_pairs={{0,8},{8,0},{16,24},{24,16},{1,9},{9,1},{17,25},{25,17},{2,10},{10... | collective-permute-start | bytes 1179656 | tf_op jit(solution)/shard_map/ppermute | solution.py:54
  288.6 274.2 %reduce-scatter.8.cloned.1.call-start = ((), (), s32[]{:S(2)}) async-start(), calls=%async_computation.8 | async-start | bytes 7962624 | tf_op jit(solution)/shard_map/reduce_scatter | solution.py:356
  302.2 263.1 %reduce-scatter.4.cloned.1.call-start = ((), (), s32[]{:S(2)}) async-start(), calls=%async_computation.6 | async-start | bytes 7962624 | tf_op jit(solution)/shard_map/reduce_scatter | solution.py:356
  332.8 15.8 %collective-permute-start.19 = (bf16[128,1536]{1,0:T(8,128)(2,1)S(1)}, bf16[128,1536]{1,0:T(8,128)(2,1)S(1)}, u32[]{:S(2)}, u32[]{:S(2)}) collective-permute-start(bf16[128,1536]{1,0:T(8,128)(2,1)S(1)} %get-tuple-element.51), channel_id=1, source_target_pairs={{0,8},{8,0},{16,24},{24,16},{1,9},{9,1},{17,25},{25,17},{2,10},{10... | collective-permute-start | bytes 1179656 | tf_op jit(solution)/shard_map/ppermute | solution.py:54
  333.9 14.7 %collective-permute-start.17 = (bf16[128,1536]{1,0:T(8,128)(2,1)S(1)}, bf16[128,1536]{1,0:T(8,128)(2,1)S(1)}, u32[]{:S(2)}, u32[]{:S(2)}) collective-permute-start(bf16[128,1536]{1,0:T(8,128)(2,1)S(1)} %get-tuple-element.52), channel_id=1, source_target_pairs={{0,16},{8,24},{16,0},{24,8},{1,17},{9,25},{17,1},{25,9},{2,18},{10... | collective-permute-start | bytes 1179656 | tf_op jit(solution)/shard_map/ppermute | solution.py:54
  348.9 27.7 %collective-permute-start.20 = (bf16[256,1536]{1,0:T(8,128)(2,1)S(1)}, bf16[256,1536]{1,0:T(8,128)(2,1)S(1)}, u32[]{:S(2)}, u32[]{:S(2)}) collective-permute-start(bf16[256,1536]{1,0:T(8,128)(2,1)S(1)} %pad_maximum_fusion.10), channel_id=1, source_target_pairs={{0,16},{8,24},{16,0},{24,8},{1,17},{9,25},{17,1},{25,9},{2,18},{10... | collective-permute-start | bytes 2359304 | tf_op jit(solution)/shard_map/ppermute | solution.py:54
  350.1 26.5 %collective-permute-start.18 = (bf16[256,1536]{1,0:T(8,128)(2,1)S(1)}, bf16[256,1536]{1,0:T(8,128)(2,1)S(1)}, u32[]{:S(2)}, u32[]{:S(2)}) collective-permute-start(bf16[256,1536]{1,0:T(8,128)(2,1)S(1)} %pad_maximum_fusion.9), channel_id=1, source_target_pairs={{0,8},{8,0},{16,24},{24,16},{1,9},{9,1},{17,25},{25,17},{2,10},{10... | collective-permute-start | bytes 2359304 | tf_op jit(solution)/shard_map/ppermute | solution.py:54
  360.9 31.0 %collective-permute-start.12 = (bf16[256,1536]{1,0:T(8,128)(2,1)}, bf16[256,1536]{1,0:T(8,128)(2,1)}, u32[]{:S(2)}, u32[]{:S(2)}) collective-permute-start(bf16[256,1536]{1,0:T(8,128)(2,1)} %pad_maximum_fusion.8), channel_id=1, source_target_pairs={{0,16},{8,24},{16,0},{24,8},{1,17},{9,25},{17,1},{25,9},{2,18},{10... | collective-permute-start | bytes 2359304 | tf_op jit(solution)/shard_map/ppermute | solution.py:54
  362.7 29.1 %collective-permute-start.10 = (bf16[256,1536]{1,0:T(8,128)(2,1)}, bf16[256,1536]{1,0:T(8,128)(2,1)}, u32[]{:S(2)}, u32[]{:S(2)}) collective-permute-start(bf16[256,1536]{1,0:T(8,128)(2,1)} %pad_maximum_fusion.7), channel_id=1, source_target_pairs={{0,8},{8,0},{16,24},{24,16},{1,9},{9,1},{17,25},{25,17},{2,10},{10... | collective-permute-start | bytes 2359304 | tf_op jit(solution)/shard_map/ppermute | solution.py:54
  400.6 17.9 %collective-permute-start.22 = (bf16[256,1536]{1,0:T(8,128)(2,1)S(1)}, bf16[256,1536]{1,0:T(8,128)(2,1)S(1)}, u32[]{:S(2)}, u32[]{:S(2)}) collective-permute-start(bf16[256,1536]{1,0:T(8,128)(2,1)S(1)} %get-tuple-element.27), channel_id=1, source_target_pairs={{0,16},{8,24},{16,0},{24,8},{1,17},{9,25},{17,1},{25,9},{2,18},{10... | collective-permute-start | bytes 2359304 | tf_op jit(solution)/shard_map/ppermute | solution.py:54
  401.1 18.9 %collective-permute-start.21 = (bf16[256,1536]{1,0:T(8,128)(2,1)S(1)}, bf16[256,1536]{1,0:T(8,128)(2,1)S(1)}, u32[]{:S(2)}, u32[]{:S(2)}) collective-permute-start(bf16[256,1536]{1,0:T(8,128)(2,1)S(1)} %get-tuple-element.27), channel_id=1, source_target_pairs={{0,8},{8,0},{16,24},{24,16},{1,9},{9,1},{17,25},{25,17},{2,10},{10... | collective-permute-start | bytes 2359304 | tf_op jit(solution)/shard_map/ppermute | solution.py:54
  483.4 16.6 %collective-permute-start.29 = (bf16[4,208,640]{2,1,0:T(8,128)(2,1)S(1)}, bf16[4,208,640]{2,1,0:T(8,128)(2,1)S(1)}, u32[]{:S(2)}, u32[]{:S(2)}) collective-permute-start(bf16[4,208,640]{2,1,0:T(8,128)(2,1)S(1)} %fusion.38), channel_id=1, source_target_pairs={{0,1},{1,0},{2,3},{3,2},{4,5},{5,4},{6,7},{7,6},{8,9},{9,8},{10,11... | collective-permute-start | bytes 3194888 | tf_op jit(solution)/shard_map/ppermute | solution.py:85
  486.9 53.1 %collective-permute-start.28 = (bf16[256,1536]{1,0:T(8,128)(2,1)S(1)}, bf16[256,1536]{1,0:T(8,128)(2,1)S(1)}, u32[]{:S(2)}, u32[]{:S(2)}) collective-permute-start(bf16[256,1536]{1,0:T(8,128)(2,1)S(1)} %pad_maximum_fusion.12), channel_id=1, source_target_pairs={{0,16},{8,24},{16,0},{24,8},{1,17},{9,25},{17,1},{25,9},{2,18},{10... | collective-permute-start | bytes 2359304 | tf_op jit(solution)/shard_map/ppermute | solution.py:54
  499.4 40.6 %collective-permute-start.26 = (bf16[256,1536]{1,0:T(8,128)(2,1)S(1)}, bf16[256,1536]{1,0:T(8,128)(2,1)S(1)}, u32[]{:S(2)}, u32[]{:S(2)}) collective-permute-start(bf16[256,1536]{1,0:T(8,128)(2,1)S(1)} %pad_maximum_fusion.11), channel_id=1, source_target_pairs={{0,8},{8,0},{16,24},{24,16},{1,9},{9,1},{17,25},{25,17},{2,10},{10... | collective-permute-start | bytes 2359304 | tf_op jit(solution)/shard_map/ppermute | solution.py:54
  500.0 22.5 %collective-permute-start.30 = (bf16[208,640]{1,0:T(8,128)(2,1)S(1)}, bf16[208,640]{1,0:T(8,128)(2,1)S(1)}, u32[]{:S(2)}, u32[]{:S(2)}) collective-permute-start(bf16[208,640]{1,0:T(8,128)(2,1)S(1)} %fusion.50), channel_id=1, source_target_pairs={{0,2},{1,3},{2,4},{3,5},{4,6},{5,7},{6,0},{7,1},{8,10},{9,11},{10,... | collective-permute-start | bytes 798728 | tf_op jit(solution)/shard_map/ppermute | solution.py:237
  512.1 16.8 %collective-permute-start.39 = (bf16[48,1536]{1,0:T(8,128)(2,1)S(1)}, bf16[48,1536]{1,0:T(8,128)(2,1)S(1)}, u32[]{:S(2)}, u32[]{:S(2)}) collective-permute-start(bf16[48,1536]{1,0:T(8,128)(2,1)S(1)} %fusion.65), channel_id=1, source_target_pairs={{0,2},{1,3},{2,4},{3,5},{4,6},{5,7},{6,0},{7,1},{8,10},{9,11},{10,... | collective-permute-start | bytes 442376 | tf_op jit(solution)/shard_map/ppermute | solution.py:237
  522.7 17.1 %collective-permute-start.31 = (bf16[208,640]{1,0:T(8,128)(2,1)S(1)}, bf16[208,640]{1,0:T(8,128)(2,1)S(1)}, u32[]{:S(2)}, u32[]{:S(2)}) collective-permute-start(bf16[208,640]{1,0:T(8,128)(2,1)S(1)} %fusion.52), channel_id=1, source_target_pairs={{0,2},{1,3},{2,4},{3,5},{4,6},{5,7},{6,0},{7,1},{8,10},{9,11},{10,... | collective-permute-start | bytes 798728 | tf_op jit(solution)/shard_map/ppermute | solution.py:237
  (65 other events, 550.7 us)
Sparse Core Ops, SparseCore 0:
  9.7 93.6 all-gather.5
  105.0 79.1 all-gather.3
  185.9 70.6 all-gather.7
  288.7 75.8 reduce-scatter.5
  366.7 75.5 reduce-scatter.7
  444.5 96.4 reduce-scatter.3

commit v3 on v2

--- a/solution.py
+++ b/solution.py
@@ -1,3 +1,5 @@
+import functools
+
 import jax
 import jax.numpy as jnp
 from jax import lax
@@ -31,22 +33,17 @@
     return dot(a, b, ((0,), (0,)), out)
 
 
-def rope_tables(positions):
+def rope_tables(length):
     exponent = jnp.arange(0, HEAD_SIZE, 2).astype(F32) / HEAD_SIZE
     freqs = THETA ** (-exponent)
-    angles = positions.astype(F32)[:, None] * freqs[None, :]
-    angles = jnp.concatenate([angles, angles], axis=-1)
-    return jnp.cos(angles), jnp.sin(angles)
-
-
-def turn(u):
-    half = u.shape[-1] // 2
-    return jnp.concatenate([-u[..., half:], u[..., :half]], axis=-1)
-
-
-def turn_back(w):
+    angles = jnp.arange(length, dtype=jnp.int32).astype(F32)[:, None] * freqs[None, :]
+    cosine, sine = jnp.cos(angles), jnp.sin(angles)
+    return jnp.concatenate([cosine, cosine], axis=-1), jnp.concatenate([-sine, sine], axis=-1)
+
+
+def swap_halves(w):
     half = w.shape[-1] // 2
-    return jnp.concatenate([w[..., half:], -w[..., :half]], axis=-1)
+    return jnp.concatenate([w[..., half:], w[..., :half]], axis=-1)
 
 
 def swap_seq(value, k):
@@ -85,10 +82,25 @@
     return lax.ppermute(value, "dp", [(i, i ^ 1) for i in range(size)])
 
 
+def remote(src, dst, send, recv, where):
+    return pltpu.make_async_remote_copy(
+        src_ref=src, dst_ref=dst, send_sem=send, recv_sem=recv,
+        device_id=where, device_id_type=pl.DeviceIdType.MESH,
+    )
+
+
+def greet(partners):
+    barrier = pltpu.get_barrier_semaphore()
+    for partner in partners:
+        pl.semaphore_signal(barrier, inc=1, device_id=partner, device_id_type=pl.DeviceIdType.MESH)
+    pl.semaphore_wait(barrier, len(partners))
+
+
 def start_kernel(
-    x_in, ids_in, small_in, pack_in, out_in,
-    x_out, ids_out, small_out, pack_out, out_out,
+    x_in, c_in, ids_in, small_in, pack_in, out_in,
+    x_out, c_out, ids_out, small_out, pack_out, out_out,
     local_sem, seq_send, seq_recv, far_send, far_recv, ring_send, ring_recv, core_send, core_recv,
+    out_send, out_recv, slot_send, slot_recv,
 ):
     seqs, dps = lax.axis_size("seq"), lax.axis_size("dp")
     chips = dps // 2
@@ -97,74 +109,71 @@
     ahead = ((chip + chips - 1) % chips) * 2 + core
     behind = ((chip + 1) % chips) * 2 + core
     sibling = chip * 2 + 1 - core
-
-    barrier = pltpu.get_barrier_semaphore()
-    for k in range(1, seqs):
-        pl.semaphore_signal(barrier, inc=1, device_id=(seq ^ k, dpi), device_id_type=pl.DeviceIdType.MESH)
-    for other in (ahead, behind, sibling):
-        pl.semaphore_signal(barrier, inc=1, device_id=(seq, other), device_id_type=pl.DeviceIdType.MESH)
-    pl.semaphore_wait(barrier, seqs + 2)
+    greet([(seq ^ k, dpi) for k in range(1, seqs)] + [(seq, other) for other in (ahead, behind, sibling)])
 
     rows = x_in.shape[0]
     half = rows // 2
 
-    def remote(src, dst, send, recv, where):
-        return pltpu.make_async_remote_copy(
-            src_ref=src, dst_ref=dst, send_sem=send, recv_sem=recv,
-            device_id=where, device_id_type=pl.DeviceIdType.MESH,
-        )
-
-    small_sends = [
-        remote(small_in, small_out.at[dpi, seq], seq_send.at[0, k], seq_recv.at[0, k], (seq ^ k, dpi))
-        for k in range(1, seqs)
-    ]
+    def to_slots(i, src, dst, slots):
+        return [remote(src, dst, seq_send.at[i, k], seq_recv.at[i, k], (seq ^ k, dpi)) for k in slots]
+
+    def block(index, low=0, count=rows):
+        return pl.ds(pl.multiple_of(index * rows + low, half), count)
+
+    small_sends = to_slots(0, small_in, small_out.at[dpi, seq], range(1, seqs))
     pack_sends = [
         remote(
             pack_in.at[seq ^ k], pack_out.at[seq, dpi], seq_send.at[1, k], seq_recv.at[1, k], (seq ^ k, dpi)
         )
         for k in range(1, seqs)
     ]
-    id_sends = [
-        remote(ids_in, ids_out.at[k], seq_send.at[2, k], seq_recv.at[2, k], (seq ^ k, dpi))
-        for k in range(1, seqs)
-    ]
-    x_sends = [
-        remote(x_in, x_out.at[pl.ds(k * rows, rows)], seq_send.at[3, k], seq_recv.at[3, k], (seq ^ k, dpi))
-        for k in (1, 2)
-    ]
+    id_sends = to_slots(2, ids_in, ids_out.at[seq], range(1, seqs))
+    x_sends = to_slots(3, x_in, x_out.at[block(seq)], (1, 2))
+    c_sends = to_slots(4, c_in, c_out.at[block(seq)], (1, 2))
     locals_ = [
         pltpu.make_async_copy(small_in, small_out.at[dpi, seq], local_sem.at[0]),
         pltpu.make_async_copy(pack_in.at[seq], pack_out.at[seq, dpi], local_sem.at[1]),
-        pltpu.make_async_copy(out_in, out_out.at[dpi], local_sem.at[2]),
-        pltpu.make_async_copy(ids_in, ids_out.at[0], local_sem.at[3]),
-        pltpu.make_async_copy(x_in, x_out.at[pl.ds(0, rows)], local_sem.at[4]),
+        pltpu.make_async_copy(out_in, out_out.at[0, dpi], local_sem.at[2]),
+        pltpu.make_async_copy(ids_in, ids_out.at[seq], local_sem.at[3]),
+        pltpu.make_async_copy(x_in, x_out.at[block(seq)], local_sem.at[4]),
+        pltpu.make_async_copy(c_in, c_out.at[block(seq)], local_sem.at[5]),
     ]
     for copy in small_sends + pack_sends + locals_[:3] + id_sends + x_sends + locals_[3:]:
         copy.start()
     for copy in locals_[:3] + small_sends + pack_sends:
         copy.wait()
 
-    far_sends = [
-        remote(
-            x_out.at[pl.ds(2 * rows, half)], x_out.at[pl.ds(3 * rows, half)],
-            far_send.at[0], far_recv.at[0], (seq ^ 1, dpi),
-        ),
-        remote(
-            x_out.at[pl.ds(rows + half, half)], x_out.at[pl.ds(3 * rows + half, half)],
-            far_send.at[1], far_recv.at[1], (seq ^ 2, dpi),
-        ),
-    ]
+    def far_sends(i, field):
+        return [
+            remote(
+                field.at[block(seq ^ 2, 0, half)], field.at[block(seq ^ 2, 0, half)],
+                far_send.at[i, 0], far_recv.at[i, 0], (seq ^ 1, dpi),
+            ),
+            remote(
+                field.at[block(seq ^ 1, half, half)], field.at[block(seq ^ 1, half, half)],
+                far_send.at[i, 1], far_recv.at[i, 1], (seq ^ 2, dpi),
+            ),
+        ]
 
     def hop_sends(hop, to_core):
-        block = ((chip + hop) % chips) * 2 + core
+        at = ((chip + hop) % chips) * 2 + core
         send, recv = (core_send, core_recv) if to_core else (ring_send, ring_recv)
         where = (seq, sibling) if to_core else (seq, ahead)
         return [
             remote(field, field, send.at[i, hop], recv.at[i, hop], where)
-            for i, field in enumerate((small_out.at[block], pack_out.at[:, block], out_out.at[block]))
+            for i, field in enumerate((small_out.at[at], pack_out.at[:, at], out_out.at[0, at]))
         ]
 
-    flying = []
+    def out_sends(hop):
+        at = ((chip + hop) % chips) * 2 + core
+        return [
+            remote(
+                out_out.at[0, at], out_out.at[k, at], out_send.at[k, hop], out_recv.at[k, hop], (seq ^ k, dpi)
+            )
+            for k in range(1, seqs)
+        ]
+
+    flying, outs = [], []
     for hop in range(chips):
         if hop > 0:
             for copy in rings:
@@ -178,42 +187,290 @@
         if hop == 0:
             for copy in x_sends:
                 copy.wait()
-            for copy in far_sends:
+            far_x = far_sends(0, x_out)
+            for copy in far_x:
                 copy.start()
-    for copy in flying:
+        more = out_sends(hop)
+        outs += more
+        for copy in more:
+            copy.start()
+        if hop == 0:
+            for copy in c_sends:
+                copy.start()
+    for copy in c_sends:
+        copy.wait()
+    far_c = far_sends(1, c_out)
+    for copy in far_c:
+        copy.start()
+    for copy in outs:
+        copy.wait_recv()
+    slots = [
+        remote(
+            out_out.at[k, ((chip + hop) % chips) * 2 + core], out_out.at[k, ((chip + hop) % chips) * 2 + core],
+            slot_send.at[k, hop], slot_recv.at[k, hop], (seq, sibling),
+        )
+        for k in range(1, seqs)
+        for hop in range(chips)
+    ]
+    for copy in slots:
+        copy.start()
+    for copy in flying + outs:
         copy.wait_send()
     for hop in range(chips):
         for copy in hop_sends(hop, True):
             copy.wait_recv()
-    for copy in far_sends + id_sends + locals_[3:]:
+    for copy in slots + far_x + far_c + id_sends + locals_[3:]:
         copy.wait()
 
 
-def start_call(x, ids, small, pack, out):
+def start_call(x, c, ids, small, pack, out):
     seqs, dps = lax.axis_size("seq"), lax.axis_size("dp")
     chips = dps // 2
     share, wide = pack.shape[1:]
     any_space = pl.BlockSpec(memory_space=pl.ANY)
     shapes = (
         jax.ShapeDtypeStruct((seqs * x.shape[0], x.shape[1]), x.dtype),
+        jax.ShapeDtypeStruct((seqs * c.shape[0], c.shape[1]), c.dtype),
         jax.ShapeDtypeStruct((seqs,) + ids.shape, ids.dtype),
         jax.ShapeDtypeStruct((dps, seqs) + small.shape, small.dtype),
         jax.ShapeDtypeStruct((seqs, dps, share, wide), pack.dtype),
-        jax.ShapeDtypeStruct((dps,) + out.shape, out.dtype),
+        jax.ShapeDtypeStruct((seqs, dps) + out.shape, out.dtype),
     )
     dma = pltpu.SemaphoreType.DMA
     return pl.pallas_call(
         start_kernel,
         out_shape=shapes,
-        in_specs=[any_space] * 5,
-        out_specs=(any_space,) * 5,
+        in_specs=[any_space] * 6,
+        out_specs=(any_space,) * 6,
         scratch_shapes=[
-            dma((5,)), dma((4, seqs)), dma((4, seqs)), dma((2,)), dma((2,)),
+            dma((6,)), dma((5, seqs)), dma((5, seqs)), dma((2, 2)), dma((2, 2)),
             dma((3, chips)), dma((3, chips)), dma((3, chips)), dma((3, chips)),
+            dma((seqs, chips)), dma((seqs, chips)), dma((seqs, chips)), dma((seqs, chips)),
         ],
         compiler_params=pltpu.CompilerParams(collective_id=0, has_side_effects=True),
         name="start_gather",
-    )(x, ids, small, pack, out)
+    )(x, c, ids, small, pack, out)
+
+
+def attend_kernel(
+    x_ref, w_ref, bias_ref, cos_ref, sin_ref, ids_row_ref, ids_col_ref, gain_one_ref, gain_two_ref, out_ref,
+    normed_ref, qkv_ref, mixed_ref, lse_ref, hidden_ref, second_ref,
+    all_ref, send_sem, recv_sem,
+):
+    seqs = lax.axis_size("seq")
+    seq, dpi = lax.axis_index("seq"), lax.axis_index("dp")
+    greet([(seq ^ k, dpi) for k in range(1, seqs)])
+    length, model = x_ref.shape
+    wq = mixed_ref.shape[1]
+    heads = wq // HEAD_SIZE
+    rows = length // seqs
+
+    @pl.loop(0, seqs)
+    def _(i):
+        at = pl.ds(pl.multiple_of(i * rows, rows), rows)
+        x = x_ref[at, :].astype(F32)
+        factor = lax.rsqrt(jnp.mean(x * x, axis=-1, keepdims=True) + EPS)
+        normed_ref[at, :] = (x * factor * gain_one_ref[...]).astype(BF)
+
+    @pl.loop(0, 2)
+    def _(i):
+        at = pl.ds(pl.multiple_of(i * 2 * rows, 2 * rows), 2 * rows)
+        pre = jnp.dot(normed_ref[at, :], w_ref[...], preferred_element_type=F32) + bias_ref[...]
+        cosine, sine = cos_ref[at, :], sin_ref[at, :]
+        for h in range(heads + 1):
+            u = pre[:, h * HEAD_SIZE : (h + 1) * HEAD_SIZE]
+            turned = pltpu.roll(u, HEAD_SIZE // 2, 1)
+            qkv_ref[at, h * HEAD_SIZE : (h + 1) * HEAD_SIZE] = (u * cosine + turned * sine).astype(BF)
+        qkv_ref[at, wq + HEAD_SIZE :] = pre[:, wq + HEAD_SIZE :].astype(BF)
+
+    copies = []
+    for t in range(seqs):
+        at = slice(t * rows, (t + 1) * rows)
+        reach = min(t + 2, seqs) * rows
+        keys = qkv_ref[:reach, wq : wq + HEAD_SIZE]
+        values = qkv_ref[:reach, wq + HEAD_SIZE :]
+        allowed = ids_row_ref[:, :reach] <= ids_col_ref[at, :]
+        sums = []
+        for h in range(heads):
+            lanes = slice(h * HEAD_SIZE, (h + 1) * HEAD_SIZE)
+            scores = nt(qkv_ref[at, lanes], keys) * SCALE
+            scores = jnp.where(allowed, scores, -1000000000.0)
+            peak = jnp.max(scores, axis=-1, keepdims=True)
+            raised = jnp.exp(scores - peak)
+            total = jnp.sum(raised, axis=-1, keepdims=True)
+            low = (raised * (1.0 / total)).astype(BF)
+            mixed_ref[at, lanes] = nn(low, values).astype(BF)
+            sums.append(peak + jnp.log(total))
+        lse_ref[at, :heads] = jnp.concatenate(sums, axis=1)
+        more = [
+            remote(
+                mixed_ref.at[pl.ds(t * rows, rows)], all_ref.at[pl.ds(t * rows, rows), pl.ds(k * wq, wq)],
+                send_sem.at[k, t], recv_sem.at[k, t], (seq ^ k, dpi),
+            )
+            for k in range(1, seqs)
+        ]
+        for copy in more:
+            copy.start()
+        copies.append(more)
+        all_ref[at, :wq] = mixed_ref[at, :]
+
+    for t in range(seqs):
+        at = slice(t * rows, (t + 1) * rows)
+        for copy in copies[t]:
+            copy.wait_recv()
+        hidden = x_ref[at, :].astype(F32) + nn(all_ref[at, :], out_ref[...])
+        hidden_ref[at, :] = hidden
+        factor = lax.rsqrt(jnp.mean(hidden * hidden, axis=-1, keepdims=True) + EPS)
+        second_ref[at, :] = (hidden * factor * gain_two_ref[...]).astype(BF)
+    for t in range(seqs):
+        for copy in copies[t]:
+            copy.wait_send()
+
+
+def attend_call(x, w, bias, cosine, sine, ids, gain_one, gain_two, out):
+    seqs = lax.axis_size("seq")
+    length, model = x.shape
+    wide = w.shape[1]
+    wq = wide - 2 * HEAD_SIZE
+    vmem = pl.BlockSpec(memory_space=pltpu.VMEM)
+    shape = jax.ShapeDtypeStruct
+    return pl.pallas_call(
+        attend_kernel,
+        out_shape=(
+            shape((length, model), BF),
+            shape((length, wide), BF),
+            shape((length, wq), BF),
+            shape((length, 128), F32),
+            shape((length, model), F32),
+            shape((length, model), BF),
+        ),
+        in_specs=[vmem] * 10,
+        out_specs=(vmem,) * 6,
+        scratch_shapes=[
+            pltpu.VMEM((length, seqs * wq), BF),
+            pltpu.SemaphoreType.DMA((seqs, seqs)),
+            pltpu.SemaphoreType.DMA((seqs, seqs)),
+        ],
+        cost_estimate=pl.CostEstimate(flops=9 * 10**9, bytes_accessed=30 * 10**6, transcendentals=3 * 10**6),
+        compiler_params=pltpu.CompilerParams(
+            collective_id=1, has_side_effects=True, vmem_limit_bytes=60 * 2**20
+        ),
+        name="attend",
+    )(x, w, bias, cosine, sine, ids[None], ids[:, None], gain_one[None], gain_two[None], out)
+
+
+TILE = 256
+
+
+def act_kernel(x_ref, w_ref, active_ref, by_gate_ref, by_up_ref, *, tail):
+    last = pl.program_id(0) == pl.num_programs(0) - 1
+
+    def body(shift):
+        both = jnp.dot(x_ref[...], w_ref[...], preferred_element_type=F32)
+        gate, up = both[:, :TILE], both[:, shift : shift + TILE]
+        sigma = jax.nn.sigmoid(gate)
+        silu = gate * sigma
+        active_ref[...] = (silu * up).astype(BF)
+        by_gate_ref[...] = (up * sigma * (1.0 + gate * (1.0 - sigma))).astype(BF)
+        by_up_ref[...] = silu.astype(BF)
+
+    if tail == TILE:
+        body(TILE)
+    else:
+        pl.when(jnp.logical_not(last))(lambda: body(TILE))
+        pl.when(last)(lambda: body(tail))
+
+
+def act_call(x, both):
+    rows, model = x.shape
+    units = both.shape[1] // 2
+    tiles = -(-units // TILE)
+    tail = units - (tiles - 1) * TILE
+    tile = pl.BlockSpec((rows, TILE), lambda j: (0, j))
+    return pl.pallas_call(
+        functools.partial(act_kernel, tail=tail),
+        grid=(tiles,),
+        out_shape=[jax.ShapeDtypeStruct((rows, units), BF)] * 3,
+        in_specs=[
+            pl.BlockSpec((rows, model), lambda j: (0, 0)),
+            pl.BlockSpec((model, 2 * TILE), lambda j: (0, j)),
+        ],
+        out_specs=[tile] * 3,
+        cost_estimate=pl.CostEstimate(
+            flops=4 * rows * model * units,
+            bytes_accessed=2 * (both.size + x.size + 3 * rows * units),
+            transcendentals=rows * units,
+        ),
+        compiler_params=pltpu.CompilerParams(vmem_limit_bytes=56 * 2**20),
+        name="gate_up",
+    )(x, both)
+
+
+def back_kernel(order_ref, x_ref, w_ref, by_gate_ref, by_up_ref, out_ref, *, tail):
+    last = pl.program_id(0) == pl.num_programs(0) - 1
+
+    def body(widths):
+        back = jnp.dot(x_ref[...], w_ref[...], preferred_element_type=F32)
+        to_gate = (back * by_gate_ref[...].astype(F32)).astype(BF)
+        to_up = (back * by_up_ref[...].astype(F32)).astype(BF)
+        for i, width in enumerate(widths):
+            low = i * TILE
+            pair = jnp.concatenate([to_gate[:, low : low + width], to_up[:, low : low + width]], axis=1)
+            out_ref[:, 2 * low : 2 * low + 2 * width] = pair
+
+    if tail == (TILE, TILE):
+        body(tail)
+    else:
+        pl.when(jnp.logical_not(last))(lambda: body((TILE, TILE)))
+        pl.when(last)(lambda: body(tail))
+
+
+def back_call(order, x, down, by_gate, by_up):
+    rows, model = x.shape
+    units = down.shape[1]
+    step = 2 * TILE
+    tiles = -(-units // step)
+    rest = units - (tiles - 1) * step
+    tail = (rest,) if rest <= TILE else (TILE, rest - TILE)
+    tile = pl.BlockSpec((rows, step), lambda j: (0, j))
+    return pl.pallas_call(
+        functools.partial(back_kernel, tail=tail),
+        grid=(tiles,),
+        out_shape=jax.ShapeDtypeStruct((rows, 2 * units), BF),
+        in_specs=[
+            pl.BlockSpec(memory_space=pl.ANY),
+            pl.BlockSpec((rows, model), lambda j: (0, 0)),
+            pl.BlockSpec((model, step), lambda j: (0, j)),
+            tile,
+            tile,
+        ],
+        out_specs=pl.BlockSpec((rows, 2 * step), lambda j: (0, j)),
+        cost_estimate=pl.CostEstimate(
+            flops=2 * rows * model * units,
+            bytes_accessed=2 * (down.size + x.size + 4 * rows * units),
+            transcendentals=0,
+        ),
+        compiler_params=pltpu.CompilerParams(vmem_limit_bytes=56 * 2**20),
+        name="back_down",
+    )(order, x, down, by_gate, by_up)
+
+
+def pair_tiles(left, right):
+    units = left.shape[1]
+    cuts = list(range(0, units, TILE)) + [units]
+    return jnp.concatenate(
+        [field[:, low:high] for low, high in zip(cuts[:-1], cuts[1:]) for field in (left, right)], axis=1
+    )
+
+
+def split_tiles(both):
+    units = both.shape[1] // 2
+    cuts = list(range(0, units, TILE)) + [units]
+    spans = list(zip(cuts[:-1], cuts[1:]))
+    return (
+        jnp.concatenate([both[:, 2 * low : low + high] for low, high in spans], axis=1),
+        jnp.concatenate([both[:, low + high : 2 * high] for low, high in spans], axis=1),
+    )
 
 
 def ring_scatter(terms):
@@ -281,13 +538,13 @@
     ).transpose(1, 0, 2)
     one = small.shape[0]
     small = jnp.pad(small[None], ((0, 15), (0, -one % 128)))
-    tokens, blocks, smalls, weight_qkv, out_head = start_call(
-        inputs[0], block_ids.reshape(-1, 128), small, packed, output_weight
-    )
-    tokens = tokens.astype(F32)
+    tokens, incoming, blocks, smalls, weight_qkv, weight_out = start_call(
+        inputs[0], cotangent[0], block_ids.reshape(-1, 128), small, packed, output_weight
+    )
     blocks = blocks.reshape(-1)
     weight_qkv = weight_qkv.reshape(model, wide)
-    out_head = out_head.reshape(dps * share, model)
+    out_head = weight_out[0].reshape(dps * share, model)
+    weight_out = weight_out.reshape(model, model)
     smalls = smalls[:, :, 0, :one].transpose(1, 0, 2).astype(F32)
     gain_first = smalls[:, :, :share].reshape(model)
     gain_second = smalls[:, :, share : 2 * share].reshape(model)
@@ -302,81 +559,54 @@
             lax.dynamic_index_in_dim(bias_v, group, 0, keepdims=False),
         ]
     )
-    positions = jnp.concatenate(
-        [(seq ^ k) * tokens_here + jnp.arange(tokens_here, dtype=jnp.int32) for k in range(seqs)]
-    )
     length = tokens.shape[0]
-    cosine, sine = rope_tables(positions)
-
-    half_rows = out_head.shape[0] // 2
-    mine = jnp.stack(gather_seq(lax.dynamic_slice_in_dim(out_head, core * half_rows, half_rows, 0)))
-    theirs = swap_core(mine)
-    weight_out = jnp.where(
-        core == 0, jnp.stack([mine, theirs], 1), jnp.stack([theirs, mine], 1)
-    ).reshape(model, model)
-
-    down_turned = down_weight.T
-    whole_gate, whole_up, whole_down = (
-        lax.all_gather(field, "dp", axis=0, tiled=True)
-        for field in (gate_weight, up_weight, down_turned)
-    )
-
+    cosine, sine = rope_tables(length)
+
+    gather = lambda field: lax.all_gather(field, "dp", axis=0, tiled=True)
+    whole_both = gather(pair_tiles(gate_weight, up_weight))
+    tokens, down_turned = lax.optimization_barrier((tokens, down_weight.T))
+    whole_down = gather(down_turned)
+
+    normed, qkv, mixed, logsum, hidden, second = attend_call(
+        tokens, weight_qkv, bias[None], cosine, sine, blocks, gain_first, gain_second, weight_out
+    )
+    tokens = tokens.astype(F32)
     first_factor = lax.rsqrt(jnp.mean(tokens * tokens, axis=-1, keepdims=True) + EPS)
-    normed = (tokens * first_factor * gain_first).astype(BF)
-    pre = nn(normed, weight_qkv) + bias
-    rotating = pre[:, : wq + HEAD_SIZE].reshape(length, heads + 1, HEAD_SIZE)
-    rotated = (rotating * cosine[:, None] + turn(rotating) * sine[:, None]).astype(BF)
-    queries, keys = rotated[:, :heads], rotated[:, heads]
-    values = pre[:, wq + HEAD_SIZE :].astype(BF)
+    second_factor = lax.rsqrt(jnp.mean(hidden * hidden, axis=-1, keepdims=True) + EPS)
+    own = lambda field: lax.dynamic_slice_in_dim(field, seq * tokens_here, tokens_here, 0)
+    split = lambda field: [
+        lax.dynamic_slice_in_dim(field, (seq ^ k) * tokens_here, tokens_here, 0) for k in range(seqs)
+    ]
+    by_place = lambda field: jnp.concatenate(by_index(gather_seq(field), seq), axis=0)
+
+    active, by_gate, by_up = act_call(second, whole_both)
+    scatter = lambda field: lax.psum_scatter(field, "dp", scatter_dimension=0, tiled=True)
+    down_grad = tn(incoming, active, BF)
+    grad_both = back_call(down_grad, incoming, whole_down, by_gate, by_up)
+    down_grad = scatter(down_grad).astype(F32)
+    second_sum = nt(grad_both, whole_both)
+    out_sum = nt(active, whole_down)
+    gate_grad, up_grad = split_tiles(scatter(tn(second, grad_both, BF)).astype(F32))
+    grad_second = scatter_seq(split(second_sum))
+    layer_out = (own(hidden) + scatter_seq(split(out_sum))).astype(BF)
+
+    gain_two_grad = jnp.sum(second_sum * (hidden * second_factor), axis=0)
+    factor = own(second_factor)
+    unit = own(hidden) * factor
+    scaled = grad_second * gain_second
+    grad_hidden = cotangent[0].astype(F32) + factor * (
+        scaled - unit * jnp.mean(scaled * unit, axis=-1, keepdims=True)
+    )
+    branch = by_place(grad_hidden.astype(BF))
+    out_weight_grad = tn(mixed, branch, BF)
+    grad_mixed = nt(branch, out_head, BF).reshape(length, heads, HEAD_SIZE)
+
+    queries, keys = qkv[:, :wq].reshape(length, heads, HEAD_SIZE), qkv[:, wq : wq + HEAD_SIZE]
+    values = qkv[:, wq + HEAD_SIZE :]
     allowed = blocks[None, :] <= blocks[:, None]
-
     scores = jnp.einsum("rhd,td->hrt", queries, keys, preferred_element_type=F32) * SCALE
     scores = jnp.where(allowed[None], scores, -1000000000.0)
-    peak = jnp.max(scores, axis=-1, keepdims=True)
-    raised = jnp.exp(scores - peak)
-    total = jnp.sum(raised, axis=-1, keepdims=True)
-    probs_low = (raised / total).astype(BF)
-    logsum = peak + jnp.log(total)
-    mixed = jnp.einsum("hrt,td->rhd", probs_low, values, preferred_element_type=F32).astype(BF)
-    mixed = mixed.reshape(length, wq)
-    all_mixed = []
-    for k, field in enumerate(gather_seq(mixed)):
-        split = field.reshape(seqs, tokens_here, wq)
-        all_mixed.append(jnp.stack([split[i ^ k] for i in range(seqs)]).reshape(length, wq))
-    hidden = tokens + nn(jnp.concatenate(all_mixed, axis=1), weight_out)
-
-    incoming = jnp.concatenate(gather_seq(lax.optimization_barrier((cotangent, tokens))[0][0]), axis=0)
-    second_factor = lax.rsqrt(jnp.mean(hidden * hidden, axis=-1, keepdims=True) + EPS)
-    second = (hidden * second_factor * gain_second).astype(BF)
-    gate = nn(second, whole_gate)
-    up = nn(second, whole_up)
-    sigma = jax.nn.sigmoid(gate)
-    silu = gate * sigma
-    active = (silu * up).astype(BF)
-    scatter = lambda field: lax.psum_scatter(field, "dp", scatter_dimension=0, tiled=True)
-    down_grad = scatter(tn(incoming, active, BF)).astype(F32)
-    back = nn(incoming, whole_down)
-    grad_gate = (back * up * sigma * (1.0 + gate * (1.0 - sigma))).astype(BF)
-    grad_up = (back * silu).astype(BF)
-    second_sum = nt(grad_gate, whole_gate) + nt(grad_up, whole_up)
-    out_sum = nt(active, whole_down)
-    gate_grad = scatter(tn(second, grad_gate, BF)).astype(F32)
-    up_grad = scatter(tn(second, grad_up, BF)).astype(F32)
-    split = lambda field: [field[k * tokens_here : (k + 1) * tokens_here] for k in range(seqs)]
-    grad_second = scatter_seq(split(second_sum))
-    layer_out = (hidden[:tokens_here] + scatter_seq(split(out_sum))).astype(BF)
-
-    gain_two_grad = jnp.sum(second_sum * (hidden * second_factor), axis=0)
-    unit = hidden[:tokens_here] * second_factor[:tokens_here]
-    scaled = grad_second * gain_second
-    grad_hidden = cotangent[0].astype(F32) + second_factor[:tokens_here] * (
-        scaled - unit * jnp.mean(scaled * unit, axis=-1, keepdims=True)
-    )
-    branch = jnp.concatenate(gather_seq(grad_hidden.astype(BF)), axis=0)
-    out_weight_grad = tn(mixed, branch, BF)
-    grad_mixed = nt(branch, out_head, BF).reshape(length, heads, HEAD_SIZE)
-
-    probs = jnp.exp(scores - logsum)
+    probs = jnp.exp(scores - logsum[:, :heads].T[:, :, None])
     grad_probs = jnp.einsum("rhd,td->hrt", grad_mixed, values, preferred_element_type=F32)
     delta = jnp.sum(probs * grad_probs, axis=-1, keepdims=True)
     grad_scores = (probs * (grad_probs - delta)).astype(BF)
@@ -386,17 +616,17 @@
         "hrt,rhd->td", probs.astype(BF), grad_mixed, preferred_element_type=F32
     )
     grad_rotated = jnp.concatenate([grad_queries, grad_keys[:, None]], axis=1)
-    grad_rotating = grad_rotated * cosine[:, None] + turn_back(grad_rotated * sine[:, None])
+    grad_rotating = grad_rotated * cosine[:, None] + swap_halves(grad_rotated * sine[:, None])
     grad_pre = jnp.concatenate(
         [grad_rotating.reshape(length, wq + HEAD_SIZE), grad_values], axis=1
     ).astype(BF)
     grad_normed = nt(grad_pre, weight_qkv)
-    unit = tokens * first_factor
-    gain_one_grad = jnp.sum(grad_normed * unit, axis=0)
+    gain_one_grad = jnp.sum(grad_normed * (tokens * first_factor), axis=0)
     grad_normed = scatter_seq(split(grad_normed))
-    unit = unit[:tokens_here]
+    factor = own(first_factor)
+    unit = own(tokens) * factor
     scaled = grad_normed * gain_first
-    input_grad = grad_hidden + first_factor[:tokens_here] * (
+    input_grad = grad_hidden + factor * (
         scaled - unit * jnp.mean(scaled * unit, axis=-1, keepdims=True)
     )
     input_grad = input_grad.astype(BF)

time: 586 us -> 529 us (0.903)
  Pallas kernels: 90.4 us -> 209 us
  matrix products: 183 us -> 103 us
  waiting for transfers between devices: 130 us -> 72.2 us
  local copies, waits for them, and re-layouts: 58.3 us -> 43.3 us
  starting transfers between devices: 35.8 us -> 22.5 us
    pallas_call x1 -> x4, Pallas kernels: 90.4 us -> 209 us  [the longest x1 116 us: start_call(): pl.pallas_call(start_kernel, out_shape=shapes, in_specs=[any_space] * 6,...]
    dot_general x15 -> x8, matrix products: 155 us -> 78.8 us  [dot(): lax.dot_general(a, b, (dims, ((), ())), preferred_element_type=F32)]
    ppermute x31 -> x19, waiting for transfers between devices: 75.1 us -> 34.6 us  [swap_seq(): return lax.ppermute(value, 'seq', [(i, i ^ k) for i in range(size)])]
    ppermute x6, waiting for transfers between devices: 53.5 us -> 29.2 us  [ring_scatter(): lax.ppermute(send.astype(BF), 'dp', [(i, (i + 2) % size) for i in range(s...]
    ppermute x31 -> x19, starting transfers between devices: 34.3 us -> 21.1 us  [swap_seq(): return lax.ppermute(value, 'seq', [(i, i ^ k) for i in range(size)])]
    unnamed x109 -> x98, local copies, waits for them, and re-layouts: 20.9 us -> 8.27 us
    all_gather x3 -> x2, waiting for transfers between devices: 0.02 us -> 8.37 us  [shards(): gather = lambda field: lax.all_gather(field, 'dp', axis=0, tiled=True)]
    slice x16 -> x12, local copies, waits for them, and re-layouts: 11.9 us -> 9.68 us  [the longest x2 4.39 us: shards(): qkv[:, :wq].reshape(length, heads, HEAD_SIZE)]
  transfers between devices with their start and end apart: 46 -> 31, of which waited for: 16 -> 16; matrix products, arithmetic and copies ran while one was open for 45% -> 36% of each run, Pallas kernels for 16% -> 40%
where the time goes in v3:
time: 529 us; the launch traced here: 524 us
  Pallas kernels  209 us (40%)
  matrix products  103 us (19%)
  waiting for transfers between devices  72.2 us (14%)
  other arithmetic  58.3 us (11%)
  local copies, waits for them, and re-layouts  43.3 us (8%)
  starting transfers between devices  22.5 us (4%)
  between operations  15.5 us (3%)
    pallas_call x1, Pallas kernels, start_call(): pl.pallas_call(start_kernel, out_shape=shapes, in_specs=[any_space] * 6,...  116 us
    dot_general x8, matrix products, dot(): lax.dot_general(a, b, (dims, ((), ())), preferred_element_type=F32)  78.8 us
    pallas_call x1, Pallas kernels, attend_call(): pl.pallas_call(attend_kernel, out_shape=(shape((length, model), BF), shap...  55.1 us
    ppermute x19, waiting for transfers between devices, swap_seq(): return lax.ppermute(value, 'seq', [(i, i ^ k) for i in range(size)])  34.6 us
    ppermute x6, waiting for transfers between devices, ring_scatter(): lax.ppermute(send.astype(BF), 'dp', [(i, (i + 2) % size) for i in range(s...  29.2 us
    pallas_call x1, Pallas kernels, act_call(): pl.pallas_call(functools.partial(act_kernel, tail=tail), grid=(tiles,), o...  23 us
    ppermute x19, starting transfers between devices, swap_seq(): return lax.ppermute(value, 'seq', [(i, i ^ k) for i in range(size)])  21.1 us
    pallas_call x1, Pallas kernels, back_call(): pl.pallas_call(functools.partial(back_kernel, tail=tail), grid=(tiles,),...  15.2 us
  transfers between devices with their start and end apart: 31, of which 16 were waited for; matrix products, arithmetic and copies ran while one was open for 36% of the time, Pallas kernels for 40%

profile of v3, /device:TPU:0, one launch (start us, length us, event | category | flops | bytes accessed | tf_op | source)
XLA Modules:
  0.0 523.8 jit_solution(13007849527142237587)
XLA Ops:
  12.6 115.6 %start_gather.1 = (bf16[1024,1536]{1,0:T(8,128)(2,1)}, bf16[1024,1536]{1,0:T(8,128)(2,1)}, s32[4,2,128]{2,1,0:T(2,128)}, bf16[8,4,16,256]{3,2,1,0:T(8,128)(2,1)}...) custom-call(bf16[256,1536]{1,0:T(8,128)(2,1)} %bitcast.259, bf16[256,1536]{1,0:T(8,128)(2,1)} %bitcast.247, ...), custom_call_target="tpu_custom_call" | custom-call | tf_op jit(solution)/shard_map/start_gather/pallas_call | solution.py:240
  136.7 55.1 %attend.1 = (bf16[1024,1536]{1,0:T(8,128)(2,1)}, bf16[1024,640]{1,0:T(8,128)(2,1)}, bf16[1024,384]{1,0:T(8,128)(2,1)}, f32[1024,128]{1,0:T(8,128)}, f32[1024,1536]{1,0:T(8,128)}, /*index=5*/bf16[1024,1536]{1,0:T(8,128)(2,1)}) custom-call(bf16[1024,1536]{1,0:T(8,128)(2,1)} %get-tuple-element.32.x_ref, bf16[1536,640]{1,0:T(8,128)(2,1)} %bitcast.278, ...), custom_call_target="tpu_custom_call" | custom-call | flops 8999999488 | bytes 30000000 | tf_op jit(solution)/shard_map/attend/pallas_call | solution.py:337
  191.9 23.0 %gate_up.1 = (bf16[1024,2240]{1,0:T(8,128)(2,1)}, bf16[1024,2240]{1,0:T(8,128)(2,1)}, bf16[1024,2240]{1,0:T(8,128)(2,1)}) custom-call(bf16[1024,1536]{1,0:T(8,128)(2,1)} %get-tuple-element.38.x_ref, bf16[1536,4480]{1,0:T(8,128)(2,1)} %all-gather.3.cloned.1.call-done.w_ref), custom_call_target="tpu_custom_call" | custom-call | flops 14092861440 | bytes 30670848 | tf_op jit(solution)/shard_map/gate_up/pallas_call | solution.py:390
  214.9 11.8 %convolution_convert_fusion.1.order_ref = bf16[1536,2240]{1,0:T(8,128)(2,1)} fusion(bf16[1024,1536]{1,0:T(8,128)(2,1)S(1)} %copy-done.8, bf16[1024,2240]{1,0:T(8,128)(2,1)} %get-tuple-element.39), kind=kOutput, calls=%fused_computation.9 | convolution fusion | flops 7049871360 | bytes 14614528 | tf_op jit(solution)/shard_map/dot_general | solution.py:21
  226.8 3.3 multiply_reduce_fusion.3
  230.1 8.3 %all-gather.5.cloned.1.call-done.w_ref = bf16[1536,2240]{1,0:T(8,128)(2,1)} async-done(((bf16[192,2240]{1,0:T(8,128)(2,1)}), bf16[1536,2240]{1,0:T(8,128)(2,1)}) %all-gather.5.cloned.1.call-update) | async-done | bytes 6881296 | tf_op jit(solution)/shard_map/all_gather | solution.py:565
  238.5 15.2 %back_down.1 = bf16[1024,4480]{1,0:T(8,128)(2,1)} custom-call(bf16[1536,2240]{1,0:T(8,128)(2,1)} %convolution_convert_fusion.1.order_ref, bf16[1024,1536]{1,0:T(8,128)(2,1)} %get-tuple-element.41.x_ref, bf16[1536,2240]{1,0:T(8,128)(2,1)} %all-gather.5.cloned.1.call-done.w_ref, bf16[1024,2240]{1,0:T(8,128)(2,1)} %get-tuple-element.42.by_gate_ref, ...), custom_call_target="tpu_custom_call" | custom-call | flops 7046430720 | bytes 28377088 | tf_op jit(solution)/shard_map/back_down/pallas_call | solution.py:436
  253.7 21.1 %convolution_convert_fusion = bf16[1536,4480]{1,0:T(8,128)(2,1)} fusion(bf16[1024,1536]{1,0:T(8,128)(2,1)S(1)} %copy-done.38, bf16[1024,4480]{1,0:T(8,128)(2,1)} %back_down.1), kind=kOutput, calls=%fused_computation | convolution fusion | flops 14099742720 | bytes 26083328 | tf_op jit(solution)/shard_map/dot_general | solution.py:21
  274.8 21.2 %multiply_reduce_fusion = (bf16[1536]{0:T(1024)(128)(2,1)S(1)}, f32[1024,1536]{1,0:T(8,128)S(1)}) fusion(f32[1024,1536]{1,0:T(8,128)} %get-tuple-element.37, f32[1024]{0:T(1024)S(1)} %add_rsqrt_fusion.1, bf16[1024,4480]{1,0:T(8,128)(2,1)} %back_down.1, bf16[1536,4480]{1,0:T(8,128)(2,1)} %all-gather.3.cloned.1.call-done.w_ref), kind=kOutput, calls=%fused_computation.11 | convolution fusion | flops 14097577984 | bytes 35527680 | tf_op jit(solution)/shard_map/dot_general | solution.py:21
  299.1 11.5 %fusion.83 = f32[1024,1536]{1,0:T(8,128)} fusion(bf16[1024,2240]{1,0:T(8,128)(2,1)} %get-tuple-element.39, bf16[1536,2240]{1,0:T(8,128)(2,1)S(1)} %bitcast.238), kind=kOutput, calls=%fused_computation.223 | convolution fusion | flops 7046430720 | bytes 17760256 | tf_op jit(solution)/shard_map/dot_general | solution.py:21
  320.1 4.3 collective-permute-done
  332.2 9.1 %collective-permute-done.7 = bf16[256,1536]{1,0:T(8,128)(2,1)} collective-permute-done((bf16[256,1536]{1,0:T(8,128)(2,1)}, bf16[256,1536]{1,0:T(8,128)(2,1)}, u32[]{:S(2)}, u32[]{:S(2)}) %collective-permute-start.7) | collective-permute-done | bytes 786464 | tf_op jit(solution)/shard_map/ppermute | solution.py:51
  341.7 2.9 multiply_reduce_fusion.5
  344.7 12.1 %collective-permute-done.3 = bf16[256,1536]{1,0:T(8,128)(2,1)} collective-permute-done((bf16[256,1536]{1,0:T(8,128)(2,1)}, bf16[256,1536]{1,0:T(8,128)(2,1)}, u32[]{:S(2)}, u32[]{:S(2)}) %collective-permute-start.3) | collective-permute-done | bytes 786464 | tf_op jit(solution)/shard_map/ppermute | solution.py:51
  357.5 5.7 %fusion.71 = (bf16[256,1536]{1,0:T(8,128)(2,1)}, f32[256,1536]{1,0:T(8,128)}, bf16[1,256,1536]{2,1,0:T(8,128)(2,1)}) fusion(f32[256]{0:T(256)S(1)} %broadcast_multiply_fusion.1, f32[1024,1536]{1,0:T(8,128)} %get-tuple-element.37, s32[]{:T(128)S(6)} %select_n.156, f32[1536]{0:T(1024)S(1)} %mul.229, bf16[256,1536]{1,0:T(8,128)(2,1)} %collective-permute-done.7, ...), kind=kLoop, calls=%fused_computation.211 | loop fusion | flops 7077888 | bytes 11804676 | tf_op jit(solution)/shard_map/convert_element_type | solution.py:600
  365.2 3.5 convert_element_type.334
  381.1 7.7 %fusion.51 = f32[1024,1024,3]{1,0,2:T(8,128)} fusion(bf16[1024,3,128]{0,2,1:T(8,128)(2,1)} %bitcast.248, bf16[1024,640]{1,0:T(8,128)(2,1)} %get-tuple-element.44), kind=kOutput, calls=%fused_computation.128 | convolution fusion | flops 805306368 | bytes 13631488 | tf_op jit(solution)/shard_map/rhd,td->hrt/dot_general | solution.py:607
  396.2 4.6 collective-permute-done.11
  400.8 2.8 collective-permute-done.10
  408.2 4.1 convolution_convert_fusion.4
  413.1 8.1 %fusion = (f32[3,1024]{1,0:T(4,128)S(1)}, f32[1024,1024,3]{1,0,2:T(8,128)}) fusion(f32[1024,1024,3]{1,0,2:T(8,128)S(1)} %bitcast.231, f32[3,1024]{1,0:T(4,128)S(1)} %copy.58, pred[1024,1024]{0,1:T(8,128)(4,1)S(1)} %copy-done.3, bf16[1024,3,128]{0,2,1:T(8,128)(2,1)S(1)} %bitcast.260, bf16[1024,640]{1,0:T(8,128)(2,1)} %get-tuple-element.44), kind=kOutput, calls=%fused_computation.3 | convolution fusion | flops 821031936 | bytes 27287552 | tf_op jit(solution)/shard_map/rhd,td->hrt/dot_general | solution.py:610
  421.2 7.0 %fusion.2 = bf16[3,1024,1024]{1,2,0:T(8,128)(2,1)S(1)} fusion(f32[1024,1024,3]{1,0,2:T(8,128)} %get-tuple-element.138, f32[1024,1024,3]{1,0,2:T(8,128)S(1)} %bitcast.231, f32[3,1024]{1,0:T(4,128)S(1)} %get-tuple-element.137, f32[3,1024]{1,0:T(4,128)S(1)} %copy.58, pred[1024,1024]{0,1:T(8,128)(4,1)S(1)} %copy-done.3), kind=kLoop, calls=%fused_computation.5 | loop fusion | flops 18874368 | bytes 32530432 | tf_op jit(solution)/shard_map/convert_element_type | solution.py:612
  435.0 4.1 fusion.16
  439.1 3.1 multiply_reduce_fusion.1
  447.3 3.3 convolution_convert_fusion.3
  460.7 6.1 %collective-permute-done.24 = bf16[48,1536]{1,0:T(8,128)(2,1)S(1)} collective-permute-done((bf16[48,1536]{1,0:T(8,128)(2,1)S(1)}, bf16[48,1536]{1,0:T(8,128)(2,1)S(1)}, u32[]{:S(2)}, u32[]{:S(2)}) %collective-permute-start.24) | collective-permute-done | bytes 147488 | tf_op jit(solution)/shard_map/ppermute | solution.py:494
  469.7 6.6 %collective-permute-done.25 = bf16[48,1536]{1,0:T(8,128)(2,1)S(1)} collective-permute-done((bf16[48,1536]{1,0:T(8,128)(2,1)S(1)}, bf16[48,1536]{1,0:T(8,128)(2,1)S(1)}, u32[]{:S(2)}, u32[]{:S(2)}) %collective-permute-start.25) | collective-permute-done | bytes 147488 | tf_op jit(solution)/shard_map/ppermute | solution.py:494
  477.4 4.5 collective-permute-done.17
  482.1 3.3 collective-permute-done.26
  487.1 3.2 collective-permute-done.18
  493.5 5.5 %collective-permute-done.19 = bf16[208,640]{1,0:T(8,128)(2,1)S(1)} collective-permute-done((bf16[208,640]{1,0:T(8,128)(2,1)S(1)}, bf16[208,640]{1,0:T(8,128)(2,1)S(1)}, u32[]{:S(2)}, u32[]{:S(2)}) %collective-permute-start.19) | collective-permute-done | bytes 266272 | tf_op jit(solution)/shard_map/ppermute | solution.py:494
  502.9 3.9 fusion.22
  (291 shorter events, 106.7 us)
Async XLA Ops:
  7.2 184.7 %all-gather.3.cloned.1.call-start = ((), (), s32[]{:S(2)}) async-start(), calls=%async_computation.2 | async-start | bytes 15482880 | tf_op jit(solution)/shard_map/all_gather | solution.py:565
  10.9 227.5 %all-gather.5.cloned.1.call-start = ((), (), s32[]{:S(2)}) async-start(), calls=%async_computation.3 | async-start | bytes 7962624 | tf_op jit(solution)/shard_map/all_gather | solution.py:565
  128.2 382.1 %reduce-scatter.5.cloned.1.call-start = ((), (), s32[]{:S(2)}) async-start(), calls=%async_computation.5 | async-start | bytes 7962624 | tf_op jit(solution)/shard_map/reduce_scatter | solution.py:583
  226.7 286.1 %reduce-scatter.3.cloned.1.call-start = ((), (), s32[]{:S(2)}) async-start(), calls=%async_computation.4 | async-start | bytes 15482880 | tf_op jit(solution)/shard_map/reduce_scatter | solution.py:583
  296.2 19.5 %collective-permute-start.4 = (bf16[128,1536]{1,0:T(8,128)(2,1)S(1)}, bf16[128,1536]{1,0:T(8,128)(2,1)S(1)}, u32[]{:S(2)}, u32[]{:S(2)}) collective-permute-start(bf16[128,1536]{1,0:T(8,128)(2,1)S(1)} %get-tuple-element.105), channel_id=1, source_target_pairs={{0,16},{8,24},{16,0},{24,8},{1,17},{9,25},{17,1},{25,9},{2,18},{10... | collective-permute-start | bytes 1179656 | tf_op jit(solution)/shard_map/ppermute | solution.py:51
  297.7 18.1 %collective-permute-start.6 = (bf16[128,1536]{1,0:T(8,128)(2,1)S(1)}, bf16[128,1536]{1,0:T(8,128)(2,1)S(1)}, u32[]{:S(2)}, u32[]{:S(2)}) collective-permute-start(bf16[128,1536]{1,0:T(8,128)(2,1)S(1)} %get-tuple-element.106), channel_id=1, source_target_pairs={{0,8},{8,0},{16,24},{24,16},{1,9},{9,1},{17,25},{25,17},{2,10},{10... | collective-permute-start | bytes 1179656 | tf_op jit(solution)/shard_map/ppermute | solution.py:51
  312.2 12.1 %collective-permute-start = (bf16[128,1536]{1,0:T(8,128)(2,1)S(1)}, bf16[128,1536]{1,0:T(8,128)(2,1)S(1)}, u32[]{:S(2)}, u32[]{:S(2)}) collective-permute-start(bf16[128,1536]{1,0:T(8,128)(2,1)S(1)} %get-tuple-element.107), channel_id=1, source_target_pairs={{0,16},{8,24},{16,0},{24,8},{1,17},{9,25},{17,1},{25,9},{2,18},{10... | collective-permute-start | bytes 1179656 | tf_op jit(solution)/shard_map/ppermute | solution.py:51
  312.8 12.0 %collective-permute-start.2 = (bf16[128,1536]{1,0:T(8,128)(2,1)S(1)}, bf16[128,1536]{1,0:T(8,128)(2,1)S(1)}, u32[]{:S(2)}, u32[]{:S(2)}) collective-permute-start(bf16[128,1536]{1,0:T(8,128)(2,1)S(1)} %get-tuple-element.108), channel_id=1, source_target_pairs={{0,8},{8,0},{16,24},{24,16},{1,9},{9,1},{17,25},{25,17},{2,10},{10... | collective-permute-start | bytes 1179656 | tf_op jit(solution)/shard_map/ppermute | solution.py:51
  316.9 24.4 %collective-permute-start.7 = (bf16[256,1536]{1,0:T(8,128)(2,1)}, bf16[256,1536]{1,0:T(8,128)(2,1)}, u32[]{:S(2)}, u32[]{:S(2)}) collective-permute-start(bf16[256,1536]{1,0:T(8,128)(2,1)} %pad_maximum_fusion.7), channel_id=1, source_target_pairs={{0,16},{8,24},{16,0},{24,8},{1,17},{9,25},{17,1},{25,9},{2,18},{10... | collective-permute-start | bytes 2359304 | tf_op jit(solution)/shard_map/ppermute | solution.py:51
  318.5 23.2 %collective-permute-start.5 = (bf16[256,1536]{1,0:T(8,128)(2,1)}, bf16[256,1536]{1,0:T(8,128)(2,1)}, u32[]{:S(2)}, u32[]{:S(2)}) collective-permute-start(bf16[256,1536]{1,0:T(8,128)(2,1)} %pad_maximum_fusion.6), channel_id=1, source_target_pairs={{0,8},{8,0},{16,24},{24,16},{1,9},{9,1},{17,25},{25,17},{2,10},{10... | collective-permute-start | bytes 2359304 | tf_op jit(solution)/shard_map/ppermute | solution.py:51
  327.3 29.4 %collective-permute-start.3 = (bf16[256,1536]{1,0:T(8,128)(2,1)}, bf16[256,1536]{1,0:T(8,128)(2,1)}, u32[]{:S(2)}, u32[]{:S(2)}) collective-permute-start(bf16[256,1536]{1,0:T(8,128)(2,1)} %pad_maximum_fusion.5), channel_id=1, source_target_pairs={{0,16},{8,24},{16,0},{24,8},{1,17},{9,25},{17,1},{25,9},{2,18},{10... | collective-permute-start | bytes 2359304 | tf_op jit(solution)/shard_map/ppermute | solution.py:51
  329.9 27.6 %collective-permute-start.1 = (bf16[256,1536]{1,0:T(8,128)(2,1)}, bf16[256,1536]{1,0:T(8,128)(2,1)}, u32[]{:S(2)}, u32[]{:S(2)}) collective-permute-start(bf16[256,1536]{1,0:T(8,128)(2,1)} %pad_maximum_fusion.4), channel_id=1, source_target_pairs={{0,8},{8,0},{16,24},{24,16},{1,9},{9,1},{17,25},{25,17},{2,10},{10... | collective-permute-start | bytes 2359304 | tf_op jit(solution)/shard_map/ppermute | solution.py:51
  332.2 25.3 %copy-start.9 = (bf16[1,256,1536]{2,1,0:T(8,128)(2,1)S(1)}, bf16[1,256,1536]{2,1,0:T(8,128)(2,1)}, u32[]{:S(2)}) copy-start(bf16[1,256,1536]{2,1,0:T(8,128)(2,1)} %param.17) | copy-start | bytes 2359300
  363.2 25.6 %collective-permute-start.8 = (bf16[256,1536]{1,0:T(8,128)(2,1)}, bf16[256,1536]{1,0:T(8,128)(2,1)}, u32[]{:S(2)}, u32[]{:S(2)}) collective-permute-start(bf16[256,1536]{1,0:T(8,128)(2,1)} %get-tuple-element.48), channel_id=1, source_target_pairs={{0,8},{8,0},{16,24},{24,16},{1,9},{9,1},{17,25},{25,17},{2,10},{10... | collective-permute-start | bytes 2359304 | tf_op jit(solution)/shard_map/ppermute | solution.py:51
  364.7 27.4 %collective-permute-start.9 = (bf16[256,1536]{1,0:T(8,128)(2,1)}, bf16[256,1536]{1,0:T(8,128)(2,1)}, u32[]{:S(2)}, u32[]{:S(2)}) collective-permute-start(bf16[256,1536]{1,0:T(8,128)(2,1)} %get-tuple-element.48), channel_id=1, source_target_pairs={{0,16},{8,24},{16,0},{24,8},{1,17},{9,25},{17,1},{25,9},{2,18},{10... | collective-permute-start | bytes 2359304 | tf_op jit(solution)/shard_map/ppermute | solution.py:51
  390.6 10.2 %collective-permute-start.11 = (bf16[128,1536]{1,0:T(8,128)(2,1)}, bf16[128,1536]{1,0:T(8,128)(2,1)}, u32[]{:S(2)}, u32[]{:S(2)}) collective-permute-start(bf16[128,1536]{1,0:T(8,128)(2,1)} %slice.393), channel_id=1, source_target_pairs={{0,16},{8,24},{16,0},{24,8},{1,17},{9,25},{17,1},{25,9},{2,18},{10... | collective-permute-start | bytes 1179656 | tf_op jit(solution)/shard_map/ppermute | solution.py:51
  393.9 9.7 %collective-permute-start.10 = (bf16[128,1536]{1,0:T(8,128)(2,1)}, bf16[128,1536]{1,0:T(8,128)(2,1)}, u32[]{:S(2)}, u32[]{:S(2)}) collective-permute-start(bf16[128,1536]{1,0:T(8,128)(2,1)} %slice.392), channel_id=1, source_target_pairs={{0,8},{8,0},{16,24},{24,16},{1,9},{9,1},{17,25},{25,17},{2,10},{10... | collective-permute-start | bytes 1179656 | tf_op jit(solution)/shard_map/ppermute | solution.py:51
  445.9 11.4 %collective-permute-start.12 = (bf16[128,1536]{1,0:T(8,128)(2,1)}, bf16[128,1536]{1,0:T(8,128)(2,1)}, u32[]{:S(2)}, u32[]{:S(2)}) collective-permute-start(bf16[128,1536]{1,0:T(8,128)(2,1)} %get-tuple-element.103), channel_id=1, source_target_pairs={{0,16},{8,24},{16,0},{24,8},{1,17},{9,25},{17,1},{25,9},{2,18},{10... | collective-permute-start | bytes 1179656 | tf_op jit(solution)/shard_map/ppermute | solution.py:51
  446.5 10.8 %collective-permute-start.14 = (bf16[128,1536]{1,0:T(8,128)(2,1)}, bf16[128,1536]{1,0:T(8,128)(2,1)}, u32[]{:S(2)}, u32[]{:S(2)}) collective-permute-start(bf16[128,1536]{1,0:T(8,128)(2,1)} %get-tuple-element.104), channel_id=1, source_target_pairs={{0,8},{8,0},{16,24},{24,16},{1,9},{9,1},{17,25},{25,17},{2,10},{10... | collective-permute-start | bytes 1179656 | tf_op jit(solution)/shard_map/ppermute | solution.py:51
  455.1 4.0 collective-permute-start.23
  456.7 12.8 %collective-permute-start.16 = (bf16[4,208,640]{2,1,0:T(8,128)(2,1)S(1)}, bf16[4,208,640]{2,1,0:T(8,128)(2,1)S(1)}, u32[]{:S(2)}, u32[]{:S(2)}) collective-permute-start(bf16[4,208,640]{2,1,0:T(8,128)(2,1)S(1)} %fusion.20), channel_id=1, source_target_pairs={{0,1},{1,0},{2,3},{3,2},{4,5},{5,4},{6,7},{7,6},{8,9},{9,8},{10,11... | collective-permute-start | bytes 3194888 | tf_op jit(solution)/shard_map/ppermute | solution.py:82
  459.2 7.6 %collective-permute-start.24 = (bf16[48,1536]{1,0:T(8,128)(2,1)S(1)}, bf16[48,1536]{1,0:T(8,128)(2,1)S(1)}, u32[]{:S(2)}, u32[]{:S(2)}) collective-permute-start(bf16[48,1536]{1,0:T(8,128)(2,1)S(1)} %fusion.39), channel_id=1, source_target_pairs={{0,2},{1,3},{2,4},{3,5},{4,6},{5,7},{6,0},{7,1},{8,10},{9,11},{10,... | collective-permute-start | bytes 442376 | tf_op jit(solution)/shard_map/ppermute | solution.py:494
  459.3 31.5 %collective-permute-start.15 = (bf16[256,1536]{1,0:T(8,128)(2,1)S(1)}, bf16[256,1536]{1,0:T(8,128)(2,1)S(1)}, u32[]{:S(2)}, u32[]{:S(2)}) collective-permute-start(bf16[256,1536]{1,0:T(8,128)(2,1)S(1)} %pad_maximum_fusion.9), channel_id=1, source_target_pairs={{0,16},{8,24},{16,0},{24,8},{1,17},{9,25},{17,1},{25,9},{2,18},{10... | collective-permute-start | bytes 2359304 | tf_op jit(solution)/shard_map/ppermute | solution.py:51
  467.8 8.6 %collective-permute-start.25 = (bf16[48,1536]{1,0:T(8,128)(2,1)S(1)}, bf16[48,1536]{1,0:T(8,128)(2,1)S(1)}, u32[]{:S(2)}, u32[]{:S(2)}) collective-permute-start(bf16[48,1536]{1,0:T(8,128)(2,1)S(1)} %fusion.41), channel_id=1, source_target_pairs={{0,2},{1,3},{2,4},{3,5},{4,6},{5,7},{6,0},{7,1},{8,10},{9,11},{10,... | collective-permute-start | bytes 442376 | tf_op jit(solution)/shard_map/ppermute | solution.py:494
  467.9 22.9 %collective-permute-start.13 = (bf16[256,1536]{1,0:T(8,128)(2,1)S(1)}, bf16[256,1536]{1,0:T(8,128)(2,1)S(1)}, u32[]{:S(2)}, u32[]{:S(2)}) collective-permute-start(bf16[256,1536]{1,0:T(8,128)(2,1)S(1)} %pad_maximum_fusion.8), channel_id=1, source_target_pairs={{0,8},{8,0},{16,24},{24,16},{1,9},{9,1},{17,25},{25,17},{2,10},{10... | collective-permute-start | bytes 2359304 | tf_op jit(solution)/shard_map/ppermute | solution.py:51
  469.6 12.2 %collective-permute-start.17 = (bf16[208,640]{1,0:T(8,128)(2,1)S(1)}, bf16[208,640]{1,0:T(8,128)(2,1)S(1)}, u32[]{:S(2)}, u32[]{:S(2)}) collective-permute-start(bf16[208,640]{1,0:T(8,128)(2,1)S(1)} %fusion.30), channel_id=1, source_target_pairs={{0,2},{1,3},{2,4},{3,5},{4,6},{5,7},{6,0},{7,1},{8,10},{9,11},{10,... | collective-permute-start | bytes 798728 | tf_op jit(solution)/shard_map/ppermute | solution.py:494
  477.3 8.1 %collective-permute-start.26 = (bf16[48,1536]{1,0:T(8,128)(2,1)S(1)}, bf16[48,1536]{1,0:T(8,128)(2,1)S(1)}, u32[]{:S(2)}, u32[]{:S(2)}) collective-permute-start(bf16[48,1536]{1,0:T(8,128)(2,1)S(1)} %fusion.43), channel_id=1, source_target_pairs={{0,2},{1,3},{2,4},{3,5},{4,6},{5,7},{6,0},{7,1},{8,10},{9,11},{10,... | collective-permute-start | bytes 442376 | tf_op jit(solution)/shard_map/ppermute | solution.py:494
  482.0 8.3 %collective-permute-start.18 = (bf16[208,640]{1,0:T(8,128)(2,1)S(1)}, bf16[208,640]{1,0:T(8,128)(2,1)S(1)}, u32[]{:S(2)}, u32[]{:S(2)}) collective-permute-start(bf16[208,640]{1,0:T(8,128)(2,1)S(1)} %fusion.32), channel_id=1, source_target_pairs={{0,2},{1,3},{2,4},{3,5},{4,6},{5,7},{6,0},{7,1},{8,10},{9,11},{10,... | collective-permute-start | bytes 798728 | tf_op jit(solution)/shard_map/ppermute | solution.py:494
  490.4 8.6 %collective-permute-start.19 = (bf16[208,640]{1,0:T(8,128)(2,1)S(1)}, bf16[208,640]{1,0:T(8,128)(2,1)S(1)}, u32[]{:S(2)}, u32[]{:S(2)}) collective-permute-start(bf16[208,640]{1,0:T(8,128)(2,1)S(1)} %fusion.34), channel_id=1, source_target_pairs={{0,2},{1,3},{2,4},{3,5},{4,6},{5,7},{6,0},{7,1},{8,10},{9,11},{10,... | collective-permute-start | bytes 798728 | tf_op jit(solution)/shard_map/ppermute | solution.py:494
  499.4 7.4 %collective-permute-start.22 = (bf16[64,640]{1,0:T(8,128)(2,1)S(1)}, bf16[64,640]{1,0:T(8,128)(2,1)S(1)}, u32[]{:S(2)}, u32[]{:S(2)}) collective-permute-start(bf16[64,640]{1,0:T(8,128)(2,1)S(1)} %get-tuple-element.114), channel_id=1, source_target_pairs={{0,24},{8,16},{16,8},{24,0},{1,25},{9,17},{17,9},{25,1},{2,26},{10... | collective-permute-start | bytes 245768 | tf_op jit(solution)/shard_map/ppermute | solution.py:51
  501.9 4.9 collective-permute-start.21
  502.5 4.4 collective-permute-start.20
  (45 other events, 263.7 us)
Sparse Core Ops, SparseCore 0:
  11.1 156.2 all-gather.2
  169.0 69.4 all-gather.4
  240.8 75.8 reduce-scatter.4
  318.8 138.6 reduce-scatter.2

commit v4 on v3

--- a/solution.py
+++ b/solution.py
@@ -49,32 +49,6 @@
 def swap_seq(value, k):
     size = lax.axis_size("seq")
     return lax.ppermute(value, "seq", [(i, i ^ k) for i in range(size)])
-
-
-def gather_seq(value):
-    half = value.shape[0] // 2
-    one = swap_seq(value, 1)
-    two = swap_seq(value, 2)
-    far = jnp.concatenate([swap_seq(two[:half], 1), swap_seq(one[half:], 2)], axis=0)
-    return [value, one, two, far]
-
-
-def scatter_seq(parts):
-    low = [part.astype(BF) for part in parts[1:]]
-    half = low[0].shape[0] // 2
-    from_one = swap_seq(low[2][:half], 1)
-    from_two = swap_seq(low[2][half:], 2)
-    wide = [part.astype(F32) for part in parts]
-    to_one = jnp.concatenate([wide[1][:half], wide[1][half:] + from_two.astype(F32)], axis=0).astype(BF)
-    to_two = jnp.concatenate([wide[2][:half] + from_one.astype(F32), wide[2][half:]], axis=0).astype(BF)
-    return wide[0] + swap_seq(to_one, 1).astype(F32) + swap_seq(to_two, 2).astype(F32)
-
-
-def by_index(slots, index):
-    stacked = jnp.stack(slots)
-    return [
-        lax.dynamic_index_in_dim(stacked, index ^ i, 0, keepdims=False) for i in range(len(slots))
-    ]
 
 
 def swap_core(value):
@@ -359,6 +333,235 @@
     )(x, w, bias, cosine, sine, ids[None], ids[:, None], gain_one[None], gain_two[None], out)
 
 
+PIECES = 4
+
+
+def slot_rows(index, rows):
+    return pl.ds(pl.multiple_of(index * rows, rows), rows)
+
+
+class SeqSum:
+    def __init__(self, field, rows, came, sums, from_one, from_two, sems, dpi, seq):
+        self.field, self.rows, self.piece = field, rows, rows // PIECES
+        self.came, self.sums, self.got = came, sums, {1: from_one, 2: from_two}
+        self.send, self.recv = sems
+        self.dpi, self.seq = dpi, seq
+        self.started = []
+
+    def at(self, k, c):
+        start = (self.seq ^ k) * self.rows + c * self.piece
+        return pl.ds(pl.multiple_of(start, self.piece), self.piece)
+
+    def pass_on(self, c):
+        by = 1 + c % 2
+        return remote(
+            self.field.at[self.at(3, c)], self.came.at[c], self.send.at[0, c], self.recv.at[0, c], (self.seq ^ by, self.dpi)
+        )
+
+    def direct(self, k, c):
+        late = (k == 2) == (c % 2 == 0)
+        src = self.sums.at[c] if late else self.field.at[self.at(k, c)]
+        return remote(src, self.got[k].at[c], self.send.at[k, c], self.recv.at[k, c], (self.seq ^ k, self.dpi))
+
+    def begin(self):
+        for c in range(PIECES):
+            self.pass_on(c).start()
+            self.direct(1 + c % 2, c).start()
+
+    def middle(self):
+        for c in range(PIECES):
+            k = 2 - c % 2
+            self.pass_on(c).wait_recv()
+            own = self.field[self.at(k, c), :].astype(F32)
+            self.sums[c] = (self.came[c].astype(F32) + own).astype(BF)
+            self.direct(k, c).start()
+
+    def take(self, c):
+        for k in (1, 2):
+            self.direct(k, c).wait_recv()
+        total = self.field[self.at(0, c), :].astype(F32) + self.got[1][c].astype(F32)
+        return total + self.got[2][c].astype(F32)
+
+    def finish(self):
+        for c in range(PIECES):
+            self.pass_on(c).wait_send()
+            for k in (1, 2):
+                self.direct(k, c).wait_send()
+
+
+def backward_kernel(
+    second_grad_ref, hidden_ref, cotangent_ref, gain_one_ref, gain_two_ref, lse_ref, cos_ref, sin_ref,
+    ids_row_ref, ids_col_ref, tokens_hbm, normed_hbm, w_hbm, out_hbm, qkv_hbm, mixed_hbm, order_hbm,
+    normed_grad_ref, hidden_grad_ref, w_grad_ref, out_grad_ref, bias_grad_ref, gain_grad_ref,
+    tokens_ref, normed_ref, w_ref, out_ref, qkv_ref, mixed_ref,
+    branch_ref, mixed_grad_ref, pre_grad_ref, key_grad_ref, value_grad_ref,
+    came_ref, sums_ref, one_ref, two_ref,
+    load_sem, sum_send, sum_recv, branch_send, branch_recv,
+):
+    seqs = lax.axis_size("seq")
+    seq, dpi = lax.axis_index("seq"), lax.axis_index("dp")
+    length, model = second_grad_ref.shape
+    rows = length // seqs
+    piece = rows // PIECES
+    wq = mixed_ref.shape[1]
+    heads = wq // HEAD_SIZE
+    loads = [
+        pltpu.make_async_copy(src, dst, load_sem.at[i])
+        for i, (src, dst) in enumerate(
+            (
+                (out_hbm, out_ref), (qkv_hbm, qkv_ref), (w_hbm, w_ref),
+                (tokens_hbm, tokens_ref), (normed_hbm, normed_ref), (mixed_hbm, mixed_ref),
+            )
+        )
+    ]
+    for load in loads:
+        load.start()
+    greet([(seq ^ k, dpi) for k in range(1, seqs)])
+
+    total = SeqSum(second_grad_ref, rows, came_ref, sums_ref, one_ref, two_ref, (sum_send, sum_recv), dpi, seq)
+    total.begin()
+    total.middle()
+
+    def branch_at(k, c):
+        start = (seq ^ k) * rows + c * piece
+        return branch_ref.at[pl.ds(pl.multiple_of(start, piece), piece)]
+
+    def branch_copy(k, c):
+        if k < 3:
+            return remote(
+                branch_at(0, c), branch_at(0, c), branch_send.at[k, c], branch_recv.at[k, c], (seq ^ k, dpi)
+            )
+        came, to = (2, 1) if c % 2 == 0 else (1, 2)
+        return remote(
+            branch_at(came, c), branch_at(came, c), branch_send.at[3, c], branch_recv.at[3, c], (seq ^ to, dpi)
+        )
+
+    for c in range(PIECES):
+        at = pl.ds(c * piece, piece)
+        grad = total.take(c)
+        hidden = hidden_ref[at, :]
+        factor = lax.rsqrt(jnp.mean(hidden * hidden, axis=-1, keepdims=True) + EPS)
+        unit = hidden * factor
+        scaled = grad * gain_two_ref[...]
+        grad = cotangent_ref[at, :].astype(F32) + factor * (
+            scaled - unit * jnp.mean(scaled * unit, axis=-1, keepdims=True)
+        )
+        hidden_grad_ref[at, :] = grad
+        start = pl.multiple_of(seq * rows + c * piece, piece)
+        branch_ref[pl.ds(start, piece), :] = grad.astype(BF)
+        for k in (1, 2):
+            branch_copy(k, c).start()
+    total.finish()
+    for load in loads[:2]:
+        load.wait()
+
+    key_grad_ref[...] = jnp.zeros_like(key_grad_ref)
+    value_grad_ref[...] = jnp.zeros_like(value_grad_ref)
+
+    def rot_back(w, at):
+        return w * cos_ref[at, :] + pltpu.roll(w * sin_ref[at, :], HEAD_SIZE // 2, 1)
+
+    def attend_back(k):
+        at = slot_rows(seq ^ k, rows)
+        mixed_grad_ref[at, :] = nt(branch_ref[at, :], out_ref[...]).astype(BF)
+        allowed = ids_row_ref[...] <= ids_col_ref[at, :]
+        keys = qkv_ref[:, wq : wq + HEAD_SIZE]
+        values = qkv_ref[:, wq + HEAD_SIZE :]
+        for h in range(heads):
+            lanes = slice(h * HEAD_SIZE, (h + 1) * HEAD_SIZE)
+            queries = qkv_ref[at, lanes]
+            grad = mixed_grad_ref[at, lanes]
+            scores = jnp.where(allowed, nt(queries, keys) * SCALE, -1000000000.0)
+            probs = jnp.exp(scores - lse_ref[at, h : h + 1])
+            prob_grad = nt(grad, values)
+            delta = jnp.sum(probs * prob_grad, axis=-1, keepdims=True)
+            score_grad = (probs * (prob_grad - delta)).astype(BF)
+            pre_grad_ref[at, lanes] = rot_back(nn(score_grad, keys) * SCALE, at).astype(BF)
+            key_grad_ref[...] += tn(score_grad, queries)
+            value_grad_ref[...] += tn(probs.astype(BF), grad)
+
+    attend_back(0)
+    for k in (1, 2):
+        for c in range(PIECES):
+            branch_copy(k, c).wait_recv()
+            if (k == 2) == (c % 2 == 0):
+                branch_copy(3, c).start()
+        attend_back(k)
+    for c in range(PIECES):
+        branch_copy(3, c).wait_recv()
+    attend_back(3)
+    for c in range(PIECES):
+        for k in (1, 2, 3):
+            branch_copy(k, c).wait_send()
+
+    every = pl.ds(0, length)
+    pre_grad_ref[:, wq : wq + HEAD_SIZE] = rot_back(key_grad_ref[...] * SCALE, every).astype(BF)
+    pre_grad_ref[:, wq + HEAD_SIZE :] = value_grad_ref[...].astype(BF)
+    bias_grad_ref[...] = jnp.sum(pre_grad_ref[...].astype(F32), axis=0, keepdims=True)
+    for load in loads[2:]:
+        load.wait()
+    gain_grad_ref[...] = jnp.zeros_like(gain_grad_ref)
+
+    @pl.loop(0, seqs)
+    def _(i):
+        at = slot_rows(i, rows)
+        grad = nt(pre_grad_ref[at, :], w_ref[...])
+        x = tokens_ref[at, :].astype(F32)
+        factor = lax.rsqrt(jnp.mean(x * x, axis=-1, keepdims=True) + EPS)
+        gain_grad_ref[...] += jnp.sum(grad * (x * factor), axis=0, keepdims=True)
+        normed_grad_ref[at, :] = grad.astype(BF)
+
+    @pl.loop(0, model // wq)
+    def _(i):
+        lanes = pl.ds(pl.multiple_of(i * wq, HEAD_SIZE), wq)
+        w_grad_ref[pl.ds(pl.multiple_of(i * wq, HEAD_SIZE), wq), :] = tn(normed_ref[:, lanes], pre_grad_ref[...]).astype(BF)
+        out_grad_ref[:, lanes] = tn(mixed_ref[...], branch_ref[:, lanes]).astype(BF)
+
+
+def backward_call(
+    second_grad, hidden, cotangent, gain_one, gain_two, logsum, cosine, sine, ids, tokens, normed, w, out, qkv, mixed, order
+):
+    seqs = lax.axis_size("seq")
+    length, model = tokens.shape
+    rows = length // seqs
+    wide = w.shape[1]
+    wq = mixed.shape[1]
+    vmem, hbm = pl.BlockSpec(memory_space=pltpu.VMEM), pl.BlockSpec(memory_space=pl.ANY)
+    shape, dma = jax.ShapeDtypeStruct, pltpu.SemaphoreType.DMA
+    held = pltpu.VMEM((PIECES, rows // PIECES, model), BF)
+    return pl.pallas_call(
+        backward_kernel,
+        out_shape=(
+            shape((length, model), BF),
+            shape((rows, model), F32),
+            shape((model, wide), BF),
+            shape((wq, model), BF),
+            shape((1, wide), F32),
+            shape((1, model), F32),
+        ),
+        in_specs=[vmem] * 10 + [hbm] * 7,
+        out_specs=(vmem,) * 6,
+        scratch_shapes=[pltpu.VMEM(field.shape, field.dtype) for field in (tokens, normed, w, out, qkv, mixed)]
+        + [
+            pltpu.VMEM((length, model), BF),
+            pltpu.VMEM((length, wq), BF),
+            pltpu.VMEM((length, wide), BF),
+            pltpu.VMEM((length, HEAD_SIZE), F32),
+            pltpu.VMEM((length, HEAD_SIZE), F32),
+            held, held, held, held,
+            dma((6,)), dma((3, PIECES)), dma((3, PIECES)), dma((4, PIECES)), dma((4, PIECES)),
+        ],
+        cost_estimate=pl.CostEstimate(flops=13 * 10**9, bytes_accessed=30 * 10**6, transcendentals=3 * 10**6),
+        compiler_params=pltpu.CompilerParams(
+            collective_id=2, has_side_effects=True, vmem_limit_bytes=62 * 2**20
+        ),
+        name="backward",
+    )(
+        second_grad, hidden, cotangent, gain_one[None], gain_two[None], logsum, cosine, sine,
+        ids[None], ids[:, None], tokens, normed, w, out, qkv, mixed, order,
+    )
+
+
 TILE = 256
 
 
@@ -455,6 +658,150 @@
     )(order, x, down, by_gate, by_up)
 
 
+def end_kernel(
+    normed_grad_ref, hidden_grad_ref, x_ref, gain_ref, qkv_ref, out_ref, small_ref, feed_ref, hidden_ref,
+    input_grad_ref, qkv_out_ref, out_out_ref, small_out_ref, layer_out_ref,
+    qkv_got_ref, out_got_ref, small_got_ref,
+    qkv_move_ref, out_move_ref, small_move_ref, qkv_came_ref, out_came_ref, small_came_ref,
+    came_ref, sums_ref, one_ref, two_ref, came2_ref, sums2_ref, one2_ref, two2_ref,
+    sum_send, sum_recv, sum2_send, sum2_recv, core_send, core_recv, ring_send, ring_recv, seq_send, seq_recv,
+):
+    seqs, dps = lax.axis_size("seq"), lax.axis_size("dp")
+    chips = dps // 2
+    seq, dpi = lax.axis_index("seq"), lax.axis_index("dp")
+    chip, core = dpi // 2, dpi % 2
+    ahead = ((chip + 1) % chips) * 2 + core
+    behind = ((chip + chips - 1) % chips) * 2 + core
+    sibling = chip * 2 + 1 - core
+    greet([(seq ^ k, dpi) for k in range(1, seqs)] + [(seq, other) for other in (ahead, behind, sibling)])
+    rows = x_ref.shape[0]
+    piece = rows // PIECES
+
+    cores = [
+        remote(src.at[..., 1 - core, :, :], dst, core_send.at[i], core_recv.at[i], (seq, sibling))
+        for i, (src, dst) in enumerate(
+            ((qkv_ref, qkv_got_ref), (out_ref, out_got_ref), (small_ref, small_got_ref))
+        )
+    ]
+    for copy in cores:
+        copy.start()
+    total = SeqSum(normed_grad_ref, rows, came_ref, sums_ref, one_ref, two_ref, (sum_send, sum_recv), dpi, seq)
+    total.begin()
+    feed = SeqSum(feed_ref, rows, came2_ref, sums2_ref, one2_ref, two2_ref, (sum2_send, sum2_recv), dpi, seq)
+    for copy in cores:
+        copy.wait_recv()
+
+    def term(which, step):
+        parts = [
+            qkv_ref[:, which, core].astype(F32) + qkv_got_ref[:, which].astype(F32),
+            out_ref[which, core].astype(F32) + out_got_ref[which].astype(F32),
+            small_ref[which, core].astype(F32) + small_got_ref[which].astype(F32),
+        ]
+        if step > 0:
+            came = (qkv_came_ref, out_came_ref, small_came_ref)
+            parts = [part + field[step - 1].astype(F32) for part, field in zip(parts, came)]
+        return parts
+
+    def ring(step):
+        return [
+            remote(src.at[step], dst.at[step], ring_send.at[i, step], ring_recv.at[i, step], (seq, ahead))
+            for i, (src, dst) in enumerate(
+                ((qkv_move_ref, qkv_came_ref), (out_move_ref, out_came_ref), (small_move_ref, small_came_ref))
+            )
+        ]
+
+    def input_piece(c):
+        at = pl.ds(c * piece, piece)
+        x = x_ref[at, :].astype(F32)
+        factor = lax.rsqrt(jnp.mean(x * x, axis=-1, keepdims=True) + EPS)
+        unit = x * factor
+        scaled = total.take(c) * gain_ref[...]
+        grad = scaled - unit * jnp.mean(scaled * unit, axis=-1, keepdims=True)
+        input_grad_ref[at, :] = (hidden_grad_ref[at, :] + factor * grad).astype(BF)
+
+    for step in range(chips - 1):
+        if step > 0:
+            for copy in ring(step - 1):
+                copy.wait_recv()
+        for field, part in zip((qkv_move_ref, out_move_ref, small_move_ref), term((chip + chips - 1 - step) % chips, step)):
+            field[step] = part.astype(BF)
+        for copy in ring(step):
+            copy.start()
+        if step == 0:
+            total.middle()
+            feed.begin()
+        if step == 1:
+            for c in range(PIECES):
+                input_piece(c)
+            feed.middle()
+    for c in range(PIECES):
+        at = pl.ds(c * piece, piece)
+        layer_out_ref[at, :] = (hidden_ref[at, :] + feed.take(c)).astype(BF)
+    for copy in ring(chips - 2):
+        copy.wait_recv()
+    qkv, out, small = term(chip, chips - 1)
+    out_out_ref[...] = out
+    qkv_move_ref[chips - 1] = qkv.astype(BF)
+    small_move_ref[chips - 1] = small.astype(BF)
+    last = [
+        remote(
+            src, dst.at[seq], seq_send.at[i, k], seq_recv.at[i, k], (seq ^ k, dpi)
+        )
+        for k in range(1, seqs)
+        for i, (src, dst) in enumerate(
+            ((qkv_move_ref.at[chips - 1, seq ^ k], qkv_out_ref), (small_move_ref.at[chips - 1], small_out_ref))
+        )
+    ]
+    for copy in last:
+        copy.start()
+    qkv_out_ref[seq] = qkv_move_ref[chips - 1, seq]
+    small_out_ref[seq] = small_move_ref[chips - 1]
+    total.finish()
+    feed.finish()
+    for copy in cores + [copy for step in range(chips - 1) for copy in ring(step)]:
+        copy.wait_send()
+    for copy in last:
+        copy.wait()
+
+
+def end_call(normed_grad, hidden_grad, x, gain, qkv, out, small, feed, hidden):
+    seqs, chips, _, share, wide = qkv.shape
+    rows, model = x.shape
+    vmem = pl.BlockSpec(memory_space=pltpu.VMEM)
+    shape, dma = jax.ShapeDtypeStruct, pltpu.SemaphoreType.DMA
+    held = pltpu.VMEM((PIECES, rows // PIECES, model), BF)
+    blocks = ((seqs, share, wide), (share, model), small.shape[2:])
+    return pl.pallas_call(
+        end_kernel,
+        out_shape=(
+            shape((rows, model), BF),
+            shape(blocks[0], BF),
+            shape(blocks[1], F32),
+            shape((seqs,) + blocks[2], BF),
+            shape((rows, model), BF),
+        ),
+        in_specs=[vmem] * 9,
+        out_specs=(vmem,) * 5,
+        scratch_shapes=[
+            pltpu.VMEM((seqs, chips, share, wide), BF),
+            pltpu.VMEM((chips, share, model), BF),
+            pltpu.VMEM((chips,) + blocks[2], BF),
+        ]
+        + [pltpu.VMEM((chips,) + block, BF) for block in blocks]
+        + [pltpu.VMEM((chips - 1,) + block, BF) for block in blocks]
+        + [
+            held, held, held, held, held, held, held, held,
+            dma((3, PIECES)), dma((3, PIECES)), dma((3, PIECES)), dma((3, PIECES)), dma((3,)), dma((3,)),
+            dma((3, chips)), dma((3, chips)), dma((2, seqs)), dma((2, seqs)),
+        ],
+        cost_estimate=pl.CostEstimate(flops=10**8, bytes_accessed=2 * 10**7, transcendentals=0),
+        compiler_params=pltpu.CompilerParams(
+            collective_id=3, has_side_effects=True, vmem_limit_bytes=48 * 2**20
+        ),
+        name="end_sums",
+    )(normed_grad, hidden_grad, x, gain[None], qkv, out, small, feed, hidden)
+
+
 def pair_tiles(left, right):
     units = left.shape[1]
     cuts = list(range(0, units, TILE)) + [units]
@@ -471,29 +818,6 @@
         jnp.concatenate([both[:, 2 * low : low + high] for low, high in spans], axis=1),
         jnp.concatenate([both[:, low + high : 2 * high] for low, high in spans], axis=1),
     )
-
-
-def ring_scatter(terms):
-    size = lax.axis_size("dp")
-    chips = size // 2
-    index = lax.axis_index("dp")
-    chip, core = index // 2, index % 2
-    give = lax.dynamic_index_in_dim(terms, 1 - core, 1, keepdims=False)
-    keep = lax.dynamic_index_in_dim(terms, core, 1, keepdims=False)
-    got = swap_core(give)
-
-    def term(which):
-        pick = lambda field: lax.dynamic_index_in_dim(field, which, 0, keepdims=False).astype(F32)
-        return pick(keep) + pick(got)
-
-    came = None
-    for step in range(chips - 1):
-        send = term((chip + chips - 1 - step) % chips)
-        if came is not None:
-            send = send + came.astype(F32)
-        came = lax.ppermute(send.astype(BF), "dp", [(i, (i + 2) % size) for i in range(size)])
-    total = term(chip)
-    return total if came is None else total + came.astype(F32)
 
 
 def shards(
@@ -570,68 +894,26 @@
     normed, qkv, mixed, logsum, hidden, second = attend_call(
         tokens, weight_qkv, bias[None], cosine, sine, blocks, gain_first, gain_second, weight_out
     )
-    tokens = tokens.astype(F32)
-    first_factor = lax.rsqrt(jnp.mean(tokens * tokens, axis=-1, keepdims=True) + EPS)
     second_factor = lax.rsqrt(jnp.mean(hidden * hidden, axis=-1, keepdims=True) + EPS)
     own = lambda field: lax.dynamic_slice_in_dim(field, seq * tokens_here, tokens_here, 0)
-    split = lambda field: [
-        lax.dynamic_slice_in_dim(field, (seq ^ k) * tokens_here, tokens_here, 0) for k in range(seqs)
-    ]
-    by_place = lambda field: jnp.concatenate(by_index(gather_seq(field), seq), axis=0)
-
     active, by_gate, by_up = act_call(second, whole_both)
     scatter = lambda field: lax.psum_scatter(field, "dp", scatter_dimension=0, tiled=True)
     down_grad = tn(incoming, active, BF)
     grad_both = back_call(down_grad, incoming, whole_down, by_gate, by_up)
     down_grad = scatter(down_grad).astype(F32)
     second_sum = nt(grad_both, whole_both)
-    out_sum = nt(active, whole_down)
-    gate_grad, up_grad = split_tiles(scatter(tn(second, grad_both, BF)).astype(F32))
-    grad_second = scatter_seq(split(second_sum))
-    layer_out = (own(hidden) + scatter_seq(split(out_sum))).astype(BF)
-
     gain_two_grad = jnp.sum(second_sum * (hidden * second_factor), axis=0)
-    factor = own(second_factor)
-    unit = own(hidden) * factor
-    scaled = grad_second * gain_second
-    grad_hidden = cotangent[0].astype(F32) + factor * (
-        scaled - unit * jnp.mean(scaled * unit, axis=-1, keepdims=True)
-    )
-    branch = by_place(grad_hidden.astype(BF))
-    out_weight_grad = tn(mixed, branch, BF)
-    grad_mixed = nt(branch, out_head, BF).reshape(length, heads, HEAD_SIZE)
-
-    queries, keys = qkv[:, :wq].reshape(length, heads, HEAD_SIZE), qkv[:, wq : wq + HEAD_SIZE]
-    values = qkv[:, wq + HEAD_SIZE :]
-    allowed = blocks[None, :] <= blocks[:, None]
-    scores = jnp.einsum("rhd,td->hrt", queries, keys, preferred_element_type=F32) * SCALE
-    scores = jnp.where(allowed[None], scores, -1000000000.0)
-    probs = jnp.exp(scores - logsum[:, :heads].T[:, :, None])
-    grad_probs = jnp.einsum("rhd,td->hrt", grad_mixed, values, preferred_element_type=F32)
-    delta = jnp.sum(probs * grad_probs, axis=-1, keepdims=True)
-    grad_scores = (probs * (grad_probs - delta)).astype(BF)
-    grad_queries = jnp.einsum("hrt,td->rhd", grad_scores, keys, preferred_element_type=F32) * SCALE
-    grad_keys = jnp.einsum("hrt,rhd->td", grad_scores, queries, preferred_element_type=F32) * SCALE
-    grad_values = jnp.einsum(
-        "hrt,rhd->td", probs.astype(BF), grad_mixed, preferred_element_type=F32
-    )
-    grad_rotated = jnp.concatenate([grad_queries, grad_keys[:, None]], axis=1)
-    grad_rotating = grad_rotated * cosine[:, None] + swap_halves(grad_rotated * sine[:, None])
-    grad_pre = jnp.concatenate(
-        [grad_rotating.reshape(length, wq + HEAD_SIZE), grad_values], axis=1
-    ).astype(BF)
-    grad_normed = nt(grad_pre, weight_qkv)
-    gain_one_grad = jnp.sum(grad_normed * (tokens * first_factor), axis=0)
-    grad_normed = scatter_seq(split(grad_normed))
-    factor = own(first_factor)
-    unit = own(tokens) * factor
-    scaled = grad_normed * gain_first
-    input_grad = grad_hidden + factor * (
-        scaled - unit * jnp.mean(scaled * unit, axis=-1, keepdims=True)
-    )
-    input_grad = input_grad.astype(BF)
-
-    bias_grad = jnp.sum(grad_pre.astype(F32), axis=0)
+    second, second_sum = lax.optimization_barrier((second, second_sum.astype(BF)))
+    both_grad = tn(second, grad_both, BF)
+    gate_grad, up_grad = split_tiles(scatter(both_grad).astype(F32))
+    normed_grad, grad_hidden, qkv_grad, out_weight_grad, bias_grad, gain_one_grad = backward_call(
+        second_sum, own(hidden), cotangent[0], gain_first, gain_second, logsum, cosine, sine, blocks,
+        tokens, normed, weight_qkv, out_head, qkv, mixed, both_grad,
+    )
+    bias_grad, gain_one_grad = bias_grad[0], gain_one_grad[0]
+    normed_grad, whole_down = lax.optimization_barrier((normed_grad, whole_down))
+    out_sum = nt(active, whole_down, BF)
+
     place = lambda field, count, at: jnp.where(
         (jnp.arange(count) == at)[:, None], field[None], 0.0
     ).reshape(seqs, dps, -1)
@@ -649,19 +931,17 @@
     small_grad = small_grad.transpose(1, 0, 2).reshape(dps, seqs * one).astype(BF)
     small_grad = jnp.pad(small_grad, ((0, 0), (0, small_rows * wide - seqs * one)))
     small_grad = jnp.pad(small_grad.reshape(dps, -1, wide), ((0, 0), (0, 16 - small_rows), (0, 0)))
-    qkv_grad = tn(normed, grad_pre, BF).reshape(seqs, dps, share, wide)
-    qkv_grad = qkv_grad.transpose(1, 0, 2, 3).reshape(dps, seqs * share, wide)
-    qkv_grad = ring_scatter(
-        jnp.concatenate([qkv_grad, small_grad], axis=1).reshape(chips, 2, -1, wide)
-    ).astype(BF)
-    out_weight_grad = ring_scatter(out_weight_grad.reshape(chips, 2, share, model))
-    smalls = qkv_grad[seqs * share : seqs * share + small_rows]
-    smalls = smalls.reshape(-1)[: seqs * one].reshape(seqs, 1, one)
-    smalls = jnp.pad(smalls, ((0, 0), (0, 15), (0, wide - one)))
-    qkv_grad = qkv_grad[: seqs * share].reshape(seqs, share, wide)
-    qkv_grad = jnp.concatenate([qkv_grad, smalls], axis=1)
-    parts = [lax.dynamic_index_in_dim(qkv_grad, seq ^ k, 0, keepdims=False) for k in range(seqs)]
-    parts = by_index([parts[0]] + [swap_seq(parts[k], k) for k in range(1, seqs)], seq)
+    input_grad, parts, out_weight_grad, smalls, layer_out = end_call(
+        normed_grad, grad_hidden, inputs[0], gain_first,
+        qkv_grad.reshape(seqs, chips, 2, share, wide),
+        out_weight_grad.reshape(chips, 2, share, model),
+        small_grad.reshape(chips, 2, 16, wide),
+        out_sum, own(hidden),
+    )
+    smalls = smalls[:, :small_rows].reshape(seqs, -1)[:, : seqs * one].reshape(seqs, seqs, one)
+    small_sum = jnp.sum(
+        lax.dynamic_index_in_dim(smalls, seq, 1, keepdims=False).astype(F32), axis=0
+    )
     query_weight_grad = jnp.concatenate([part[:share, :wq] for part in parts], axis=1).astype(F32)
     pairs = [
         sum(part[:share, wq:].astype(F32) for part in parts[g * copies : (g + 1) * copies])
@@ -669,7 +949,6 @@
     ]
     key_weight_grad = jnp.concatenate([pair[:, :HEAD_SIZE] for pair in pairs], axis=1)
     value_weight_grad = jnp.concatenate([pair[:, HEAD_SIZE:] for pair in pairs], axis=1)
-    small_sum = sum(part[share, :one].astype(F32) for part in parts)
     gain_one_grad, gain_two_grad, query_bias_grad, key_bias_grad, value_bias_grad = jnp.split(
         small_sum, [share, 2 * share, 3 * share, 3 * share + kv_share]
     )

time: 529 us -> 501 us (0.947)
  Pallas kernels: 209 us -> 363 us
  waiting for transfers between devices: 72.2 us -> 16 us
  other arithmetic: 58.3 us -> 15.5 us
  matrix products: 103 us -> 66 us
  local copies, waits for them, and re-layouts: 43.3 us -> 20.6 us
  starting transfers between devices: 22.5 us -> 0.16 us
    pallas_call x0 -> x2, Pallas kernels: none -> 154 us  [the longest x1 78.1 us: backward_call(): pl.pallas_call(backward_kernel, out_shape=(shape((length, model), BF), sh...]
    ppermute x27 -> x0, waiting for transfers between devices: 63.8 us -> none  [the longest x19 34.6 us: swap_seq(): return lax.ppermute(value, 'seq', [(i, i ^ k) for i in range(size)])]
    dot_general x5 -> x0, matrix products: 24.1 us -> none  [the longest x1 8.1 us: shards(): jnp.einsum('rhd,td->hrt', grad_mixed, values, preferred_element_type=F32)]
    ppermute x27 -> x0, starting transfers between devices: 22.3 us -> none  [the longest x19 21.1 us: swap_seq(): return lax.ppermute(value, 'seq', [(i, i ^ k) for i in range(size)])]
    convert_element_type x11 -> x1, other arithmetic: 20.3 us -> 1.68 us  [shards(): gate_grad, up_grad = split_tiles(scatter(both_grad).astype(F32))]
    dot_general x8 -> x4, matrix products: 78.8 us -> 66 us  [dot(): lax.dot_general(a, b, (dims, ((), ())), preferred_element_type=F32)]
    slice x10 -> x1, local copies, waits for them, and re-layouts: 9.35 us -> 0.04 us  [shards(): smalls[:, :small_rows].reshape(seqs, -1)[:, :seqs * one]]
    reduce_scatter x2, waiting for transfers between devices: 0.01 us -> 7.59 us  [shards(): lax.psum_scatter(field, 'dp', scatter_dimension=0, tiled=True)]
  transfers between devices with their start and end apart: 31 -> 4, of which waited for: 16 -> 2; matrix products, arithmetic and copies ran while one was open for 36% -> 19% of each run, Pallas kernels for 40% -> 73%
where the time goes in v4:
time: 501 us; the launch traced here: 496 us
  Pallas kernels  363 us (72%)
  matrix products  66 us (13%)
  local copies, waits for them, and re-layouts  20.6 us (4%)
  waiting for transfers between devices  16 us (3%)
  other arithmetic  15.5 us (3%)
  between operations  14.7 us (3%)
    pallas_call x1, Pallas kernels, start_call(): pl.pallas_call(start_kernel, out_shape=shapes, in_specs=[any_space] * 6,...  116 us
    pallas_call x1, Pallas kernels, backward_call(): pl.pallas_call(backward_kernel, out_shape=(shape((length, model), BF), sh...  78.1 us
    pallas_call x1, Pallas kernels, end_call(): pl.pallas_call(end_kernel, out_shape=(shape((rows, model), BF), shape(blo...  76.3 us
    dot_general x4, matrix products, dot(): lax.dot_general(a, b, (dims, ((), ())), preferred_element_type=F32)  66 us
    pallas_call x1, Pallas kernels, attend_call(): pl.pallas_call(attend_kernel, out_shape=(shape((length, model), BF), shap...  55 us
    pallas_call x1, Pallas kernels, act_call(): pl.pallas_call(functools.partial(act_kernel, tail=tail), grid=(tiles,), o...  23 us
    pallas_call x1, Pallas kernels, back_call(): pl.pallas_call(functools.partial(back_kernel, tail=tail), grid=(tiles,),...  15.2 us
  transfers between devices with their start and end apart: 4, of which 2 were waited for; matrix products, arithmetic and copies ran while one was open for 19% of the time, Pallas kernels for 73%

profile of v4, /device:TPU:0, one launch (start us, length us, event | category | flops | bytes accessed | tf_op | source)
XLA Modules:
  0.0 496.1 jit_solution(11385166649232927191)
XLA Ops:
  7.3 1.6 fusion.5
  9.0 1.9 concatenate.42
  11.8 0.7 maximum_bitcast_fusion.pack_in
  12.6 115.6 %start_gather.1 = (bf16[1024,1536]{1,0:T(8,128)(2,1)}, bf16[1024,1536]{1,0:T(8,128)(2,1)}, s32[4,2,128]{2,1,0:T(2,128)}, bf16[8,4,16,256]{3,2,1,0:T(8,128)(2,1)}...) custom-call(bf16[256,1536]{1,0:T(8,128)(2,1)} %bitcast.71, bf16[256,1536]{1,0:T(8,128)(2,1)} %bitcast.82, ...), custom_call_target="tpu_custom_call" | custom-call | tf_op jit(solution)/shard_map/start_gather/pallas_call | solution.py:214
  128.3 0.9 slice_convert_fusion
  129.5 0.7 broadcast_in_dim_reshape.20.gain_two_ref
  131.1 0.7 broadcast_in_dim_reshape.19.gain_one_ref.gain_ref
  131.8 1.7 copy.56.ids_col_ref
  133.5 1.9 fusion
  135.4 1.3 pad_maximum_fusion
  136.7 55.0 %attend.1 = (bf16[1024,1536]{1,0:T(8,128)(2,1)}, bf16[1024,640]{1,0:T(8,128)(2,1)}, bf16[1024,384]{1,0:T(8,128)(2,1)}, f32[1024,128]{1,0:T(8,128)}, f32[1024,1536]{1,0:T(8,128)}, /*index=5*/bf16[1024,1536]{1,0:T(8,128)(2,1)}) custom-call(bf16[1024,1536]{1,0:T(8,128)(2,1)} %get-tuple-element.47.x_ref.tokens_hbm, bf16[1536,640]{1,0:T(8,128)(2,1)} %bitcast.97, ...), custom_call_target="tpu_custom_call" | custom-call | flops 8999999488 | bytes 30000000 | tf_op jit(solution)/shard_map/attend/pallas_call | solution.py:311
  191.8 23.0 %gate_up.1 = (bf16[1024,2240]{1,0:T(8,128)(2,1)}, bf16[1024,2240]{1,0:T(8,128)(2,1)}, bf16[1024,2240]{1,0:T(8,128)(2,1)}) custom-call(bf16[1024,1536]{1,0:T(8,128)(2,1)} %get-tuple-element.64.x_ref, bf16[1536,4480]{1,0:T(8,128)(2,1)} %all-gather.3.cloned.1.call-done.w_ref), custom_call_target="tpu_custom_call" | custom-call | flops 14092861440 | bytes 30670848 | tf_op jit(solution)/shard_map/gate_up/pallas_call | solution.py:593
  214.8 11.8 %convolution_convert_fusion.1.order_ref = bf16[1536,2240]{1,0:T(8,128)(2,1)} fusion(bf16[1024,1536]{1,0:T(8,128)(2,1)S(1)} %copy-done.7, bf16[1024,2240]{1,0:T(8,128)(2,1)} %get-tuple-element.54), kind=kOutput, calls=%fused_computation.1 | convolution fusion | flops 7049871360 | bytes 14614528 | tf_op jit(solution)/shard_map/dot_general | solution.py:21
  226.7 3.4 multiply_reduce_fusion.1
  230.2 8.3 %all-gather.5.cloned.1.call-done.w_ref = bf16[1536,2240]{1,0:T(8,128)(2,1)} async-done(((bf16[192,2240]{1,0:T(8,128)(2,1)}), bf16[1536,2240]{1,0:T(8,128)(2,1)}) %all-gather.5.cloned.1.call-update) | async-done | bytes 6881296 | tf_op jit(solution)/shard_map/all_gather | solution.py:889
  238.5 15.2 %back_down.1 = bf16[1024,4480]{1,0:T(8,128)(2,1)} custom-call(bf16[1536,2240]{1,0:T(8,128)(2,1)} %convolution_convert_fusion.1.order_ref, bf16[1024,1536]{1,0:T(8,128)(2,1)} %get-tuple-element.53.x_ref, bf16[1536,2240]{1,0:T(8,128)(2,1)} %all-gather.5.cloned.1.call-done.w_ref, bf16[1024,2240]{1,0:T(8,128)(2,1)} %get-tuple-element.56.by_gate_ref, ...), custom_call_target="tpu_custom_call" | custom-call | flops 7046430720 | bytes 28377088 | tf_op jit(solution)/shard_map/back_down/pallas_call | solution.py:639
  253.7 21.6 %multiply_reduce_fusion = (bf16[1536]{0:T(1024)(128)(2,1)S(1)}, bf16[1024,1536]{1,0:T(8,128)(2,1)}) fusion(f32[1024,1536]{1,0:T(8,128)S(1)} %bitcast.78, f32[1024]{0:T(1024)S(1)} %add_rsqrt_fusion, bf16[1024,4480]{1,0:T(8,128)(2,1)} %back_down.1, bf16[1536,4480]{1,0:T(8,128)(2,1)} %all-gather.3.cloned.1.call-done.w_ref), kind=kOutput, calls=%fused_computation.2 | convolution fusion | flops 14099150848 | bytes 32381952 | tf_op jit(solution)/shard_map/dot_general | solution.py:21
  275.3 19.8 %convolution_convert_fusion.order_hbm = bf16[1536,4480]{1,0:T(8,128)(2,1)} fusion(bf16[1024,1536]{1,0:T(8,128)(2,1)} %get-tuple-element.64.x_ref, bf16[1024,4480]{1,0:T(8,128)(2,1)S(1)} %copy-done.6), kind=kOutput, calls=%fused_computation | convolution fusion | flops 14099742720 | bytes 26083328 | tf_op jit(solution)/shard_map/dot_general | solution.py:21
  295.1 2.4 slice.210
  297.7 2.7 constant_dynamic-slice_fusion.hidden_ref
  300.4 78.1 %backward.1 = (bf16[1024,1536]{1,0:T(8,128)(2,1)}, f32[256,1536]{1,0:T(8,128)}, bf16[1536,640]{1,0:T(8,128)(2,1)}, bf16[384,1536]{1,0:T(8,128)(2,1)}, f32[1,640]{1,0:T(1,128)}, /*index=5*/f32[1,1536]{1,0:T(1,128)}) custom-call(bf16[1024,1536]{1,0:T(8,128)(2,1)} %get-tuple-element.58.second_grad_ref, f32[256,1536]{1,0:T(8,128)} %constant_dynamic-slice_fusion.hidden_ref, ...), custom_call_target="tpu_custom_call" | custom-call | flops 12999999488 | bytes 30000000 | tf_op jit(solution)/shard_map/backward/pallas_call | solution.py:532
  378.5 0.7 slice_reduce_fusion.1
  380.2 0.7 convert_reduce_fusion
  381.4 12.8 %convolution_convert_fusion.2.feed_ref = bf16[1024,1536]{1,0:T(8,128)(2,1)} fusion(bf16[1024,2240]{1,0:T(8,128)(2,1)} %get-tuple-element.54, bf16[1536,2240]{1,0:T(8,128)(2,1)} %all-gather.5.cloned.1.call-done.w_ref), kind=kOutput, calls=%fused_computation.4 | convolution fusion | flops 7048003584 | bytes 14614528 | tf_op jit(solution)/shard_map/dot_general | solution.py:21
  394.3 76.3 %end_sums.1 = (bf16[256,1536]{1,0:T(8,128)(2,1)S(1)}, bf16[4,48,640]{2,1,0:T(8,128)(2,1)S(1)}, f32[48,1536]{1,0:T(8,128)S(1)}, bf16[4,16,640]{2,1,0:T(8,128)(2,1)S(1)}, bf16[256,1536]{1,0:T(8,128)(2,1)S(1)}) custom-call(bf16[1024,1536]{1,0:T(8,128)(2,1)} %get-tuple-element.66.normed_grad_ref, f32[256,1536]{1,0:T(8,128)S(1)} %copy-done.3, ...), custom_call_target="tpu_custom_call" | custom-call | flops 100000000 | bytes 20000000 | tf_op jit(solution)/shard_map/end_sums/pallas_call | solution.py:774
  473.3 0.7 maximum_convert_fusion
  474.1 2.5 convert_bitcast_fusion
  476.6 7.6 %reduce-scatter.3.cloned.1.call-done = bf16[192,4480]{1,0:T(8,128)(2,1)} async-done(((bf16[1536,4480]{1,0:T(8,128)(2,1)}), bf16[192,4480]{1,0:T(8,128)(2,1)}) %reduce-scatter.3.cloned.1.call-update) | async-done | bytes 1720336 | tf_op jit(solution)/shard_map/reduce_scatter | solution.py:900
  484.2 1.7 convert_element_type.105
  486.3 0.9 copy.95
  487.2 1.3 copy.96
  488.6 0.7 copy.97
  (121 shorter events, 6.9 us)
Async XLA Ops:
  7.2 4.6 copy-start
  7.2 1.8 slice-start.3
  7.2 1.8 slice-start.2
  7.2 184.6 %all-gather.3.cloned.1.call-start = ((), (), s32[]{:S(2)}) async-start(), calls=%async_computation.2 | async-start | bytes 15482880 | tf_op jit(solution)/shard_map/all_gather | solution.py:889
  8.9 2.1 copy-start.12
  8.9 2.1 copy-start.13
  8.9 2.1 copy-start.14
  8.9 2.1 copy-start.15
  8.9 2.1 copy-start.16
  8.9 2.2 copy-start.8
  8.9 2.8 copy-start.9
  11.0 227.5 %all-gather.5.cloned.1.call-start = ((), (), s32[]{:S(2)}) async-start(), calls=%async_computation.3 | async-start | bytes 7962624 | tf_op jit(solution)/shard_map/all_gather | solution.py:889
  128.2 345.8 %reduce-scatter.5.cloned.1.call-start = ((), (), s32[]{:S(2)}) async-start(), calls=%async_computation.5 | async-start | bytes 7962624 | tf_op jit(solution)/shard_map/reduce_scatter | solution.py:900
  191.8 23.1 %copy-start.7 = (bf16[1024,1536]{1,0:T(8,128)(2,1)S(1)}, bf16[1024,1536]{1,0:T(8,128)(2,1)}, u32[]{:S(2)}) copy-start(bf16[1024,1536]{1,0:T(8,128)(2,1)} %get-tuple-element.53.x_ref) | copy-start | bytes 9437188
  226.7 257.5 %reduce-scatter.3.cloned.1.call-start = ((), (), s32[]{:S(2)}) async-start(), calls=%async_computation.4 | async-start | bytes 15482880 | tf_op jit(solution)/shard_map/reduce_scatter | solution.py:900
  226.7 26.9 %slice-start = ((s8[6291456]{0:T(1024)(128)(4,1)}), s8[2097152]{0:T(1024)(128)(4,1)S(1)}, s32[]{:S(2)}) async-start(s8[6291456]{0:T(1024)(128)(4,1)} %bitcast.77), calls=%async_computation.6 | async-start | bytes 4194304
  238.5 15.2 %slice-start.1 = ((s8[6291456]{0:T(1024)(128)(4,1)}), s8[4194304]{0:T(1024)(128)(4,1)S(1)}, s32[]{:S(2)}) async-start(s8[6291456]{0:T(1024)(128)(4,1)} %bitcast.77), calls=%async_computation.7 | async-start | bytes 8388608
  253.7 21.6 %copy-start.6 = (bf16[1024,4480]{1,0:T(8,128)(2,1)S(1)}, bf16[1024,4480]{1,0:T(8,128)(2,1)}, u32[]{:S(2)}) copy-start(bf16[1024,4480]{1,0:T(8,128)(2,1)} %back_down.1) | copy-start | bytes 27525124
  381.4 12.9 %copy-start.2 = (bf16[1,256,1536]{2,1,0:T(8,128)(2,1)S(1)}, bf16[1,256,1536]{2,1,0:T(8,128)(2,1)}, u32[]{:S(2)}) copy-start(bf16[1,256,1536]{2,1,0:T(8,128)(2,1)} %param.15) | copy-start | bytes 2359300
  381.4 12.9 %copy-start.3 = (f32[256,1536]{1,0:T(8,128)S(1)}, f32[256,1536]{1,0:T(8,128)}, u32[]{:S(2)}) copy-start(f32[256,1536]{1,0:T(8,128)} %get-tuple-element.67.hidden_grad_ref) | copy-start | bytes 4718596
  381.4 12.9 %copy-start.4 = (bf16[384,1536]{1,0:T(8,128)(2,1)S(1)}, bf16[384,1536]{1,0:T(8,128)(2,1)}, u32[]{:S(2)}) copy-start(bf16[384,1536]{1,0:T(8,128)(2,1)} %get-tuple-element.69) | copy-start | bytes 3538948
  381.4 12.9 %copy-start.5 = (f32[1,1536]{1,0:T(1,128)S(1)}, f32[1,1536]{1,0:T(1,128)}, u32[]{:S(2)}) copy-start(f32[1,1536]{1,0:T(1,128)} %broadcast_in_dim_reshape.19.gain_one_ref.gain_ref) | copy-start | bytes 18436
  486.0 3.3 copy-start.1
  486.3 3.0 copy-start.10
  486.3 3.0 copy-start.11
Sparse Core Ops, SparseCore 0:
  11.1 156.2 all-gather.2
  169.0 69.4 all-gather.4
  240.8 75.8 reduce-scatter.4
  318.8 165.3 reduce-scatter.2

commit v5 on v4

--- a/solution.py
+++ b/solution.py
@@ -2,6 +2,7 @@
 
 import jax
 import jax.numpy as jnp
+import numpy as np
 from jax import lax
 from jax.experimental import pallas as pl
 from jax.experimental.pallas import tpu as pltpu
@@ -34,26 +35,14 @@
 
 
 def rope_tables(length):
-    exponent = jnp.arange(0, HEAD_SIZE, 2).astype(F32) / HEAD_SIZE
-    freqs = THETA ** (-exponent)
-    angles = jnp.arange(length, dtype=jnp.int32).astype(F32)[:, None] * freqs[None, :]
-    cosine, sine = jnp.cos(angles), jnp.sin(angles)
-    return jnp.concatenate([cosine, cosine], axis=-1), jnp.concatenate([-sine, sine], axis=-1)
-
-
-def swap_halves(w):
-    half = w.shape[-1] // 2
-    return jnp.concatenate([w[..., half:], w[..., :half]], axis=-1)
-
-
-def swap_seq(value, k):
-    size = lax.axis_size("seq")
-    return lax.ppermute(value, "seq", [(i, i ^ k) for i in range(size)])
-
-
-def swap_core(value):
-    size = lax.axis_size("dp")
-    return lax.ppermute(value, "dp", [(i, i ^ 1) for i in range(size)])
+    exponent = np.arange(0, HEAD_SIZE, 2).astype(np.float32) / np.float32(HEAD_SIZE)
+    freqs = np.float32(THETA) ** (-exponent)
+    angles = np.arange(length).astype(np.float32)[:, None] * freqs[None, :]
+    cosine, sine = np.cos(angles), np.sin(angles)
+    return (
+        jnp.asarray(np.concatenate([cosine, cosine], axis=-1), F32),
+        jnp.asarray(np.concatenate([-sine, sine], axis=-1), F32),
+    )
 
 
 def remote(src, dst, send, recv, where):
@@ -68,6 +57,16 @@
     for partner in partners:
         pl.semaphore_signal(barrier, inc=1, device_id=partner, device_id_type=pl.DeviceIdType.MESH)
     pl.semaphore_wait(barrier, len(partners))
+
+
+def far_sends(field, half, seq, dpi, send, recv):
+    def rows(k, low):
+        return field.at[pl.ds(pl.multiple_of((seq ^ k) * 2 * half + low, half), half)]
+
+    return [
+        remote(rows(2, 0), rows(2, 0), send.at[0], recv.at[0], (seq ^ 1, dpi)),
+        remote(rows(1, half), rows(1, half), send.at[1], recv.at[1], (seq ^ 2, dpi)),
+    ]
 
 
 def start_kernel(
@@ -80,10 +79,9 @@
     chips = dps // 2
     seq, dpi = lax.axis_index("seq"), lax.axis_index("dp")
     chip, core = dpi // 2, dpi % 2
-    ahead = ((chip + chips - 1) % chips) * 2 + core
-    behind = ((chip + 1) % chips) * 2 + core
     sibling = chip * 2 + 1 - core
-    greet([(seq ^ k, dpi) for k in range(1, seqs)] + [(seq, other) for other in (ahead, behind, sibling)])
+    others = [((chip + h) % chips) * 2 + core for h in range(1, chips)]
+    greet([(seq ^ k, dpi) for k in range(1, seqs)] + [(seq, other) for other in others + [sibling]])
 
     rows = x_in.shape[0]
     half = rows // 2
@@ -112,68 +110,70 @@
         pltpu.make_async_copy(x_in, x_out.at[block(seq)], local_sem.at[4]),
         pltpu.make_async_copy(c_in, c_out.at[block(seq)], local_sem.at[5]),
     ]
-    for copy in small_sends + pack_sends + locals_[:3] + id_sends + x_sends + locals_[3:]:
+    def fields(at, which):
+        every = (out_out.at[0, at], small_out.at[at], pack_out.at[:, at])
+        return [(i, every[i]) for i in which]
+
+    def hop_sends(hop, which):
+        to = ((chip + chips - hop) % chips) * 2 + core
+        return [
+            remote(out_in if i == 0 else field, field, ring_send.at[i, hop], ring_recv.at[i, hop], (seq, to))
+            for i, field in fields(dpi, which)
+        ]
+
+    def core_sends(hop, which=(0, 1, 2)):
+        at = ((chip + hop) % chips) * 2 + core
+        return [
+            remote(field, field, core_send.at[i, hop], core_recv.at[i, hop], (seq, sibling))
+            for i, field in fields(at, which)
+        ]
+
+    def out_sends(hop):
+        at = ((chip + hop) % chips) * 2 + core
+        src = out_out.at[0, at] if hop else out_in
+        return [
+            remote(src, out_out.at[k, at], out_send.at[k, hop], out_recv.at[k, hop], (seq ^ k, dpi))
+            for k in range(1, seqs)
+        ]
+
+    order = sorted(range(1, chips), key=lambda hop: min(hop, chips - hop))
+    flying, outs = [], []
+    for hop in order:
+        flying += hop_sends(hop, (0,))
+    first = small_sends + pack_sends + locals_[:3] + x_sends + id_sends + locals_[3:]
+    for copy in flying + first:
         copy.start()
     for copy in locals_[:3] + small_sends + pack_sends:
         copy.wait()
-
-    def far_sends(i, field):
-        return [
-            remote(
-                field.at[block(seq ^ 2, 0, half)], field.at[block(seq ^ 2, 0, half)],
-                far_send.at[i, 0], far_recv.at[i, 0], (seq ^ 1, dpi),
-            ),
-            remote(
-                field.at[block(seq ^ 1, half, half)], field.at[block(seq ^ 1, half, half)],
-                far_send.at[i, 1], far_recv.at[i, 1], (seq ^ 2, dpi),
-            ),
-        ]
-
-    def hop_sends(hop, to_core):
-        at = ((chip + hop) % chips) * 2 + core
-        send, recv = (core_send, core_recv) if to_core else (ring_send, ring_recv)
-        where = (seq, sibling) if to_core else (seq, ahead)
-        return [
-            remote(field, field, send.at[i, hop], recv.at[i, hop], where)
-            for i, field in enumerate((small_out.at[at], pack_out.at[:, at], out_out.at[0, at]))
-        ]
-
-    def out_sends(hop):
-        at = ((chip + hop) % chips) * 2 + core
-        return [
-            remote(
-                out_out.at[0, at], out_out.at[k, at], out_send.at[k, hop], out_recv.at[k, hop], (seq ^ k, dpi)
-            )
-            for k in range(1, seqs)
-        ]
-
-    flying, outs = [], []
-    for hop in range(chips):
+    more = [copy for hop in order for copy in hop_sends(hop, (1, 2))]
+    for copy in more:
+        copy.start()
+    flying += more
+    for hop in [0] + order:
         if hop > 0:
-            for copy in rings:
+            for copy in hop_sends(hop, (0,)):
                 copy.wait_recv()
-            flying += rings
-        rings = hop_sends(hop, False) if hop < chips - 1 else []
-        cores = hop_sends(hop, True)
-        for copy in rings + cores:
+        cores, more = core_sends(hop, (0,)), out_sends(hop)
+        for copy in cores + more:
             copy.start()
         flying += cores
-        if hop == 0:
-            for copy in x_sends:
-                copy.wait()
-            far_x = far_sends(0, x_out)
-            for copy in far_x:
-                copy.start()
-        more = out_sends(hop)
         outs += more
-        for copy in more:
+    for copy in x_sends:
+        copy.wait()
+    far_x = far_sends(x_out, half, seq, dpi, far_send.at[0], far_recv.at[0])
+    for copy in far_x + c_sends:
+        copy.start()
+    for hop in [0] + order:
+        if hop > 0:
+            for copy in hop_sends(hop, (1, 2)):
+                copy.wait_recv()
+        cores = core_sends(hop, (1, 2))
+        for copy in cores:
             copy.start()
-        if hop == 0:
-            for copy in c_sends:
-                copy.start()
+        flying += cores
     for copy in c_sends:
         copy.wait()
-    far_c = far_sends(1, c_out)
+    far_c = far_sends(c_out, half, seq, dpi, far_send.at[1], far_recv.at[1])
     for copy in far_c:
         copy.start()
     for copy in outs:
@@ -191,7 +191,7 @@
     for copy in flying + outs:
         copy.wait_send()
     for hop in range(chips):
-        for copy in hop_sends(hop, True):
+        for copy in core_sends(hop):
             copy.wait_recv()
     for copy in slots + far_x + far_c + id_sends + locals_[3:]:
         copy.wait()
@@ -214,7 +214,7 @@
     return pl.pallas_call(
         start_kernel,
         out_shape=shapes,
-        in_specs=[any_space] * 6,
+        in_specs=[pl.BlockSpec(memory_space=pltpu.VMEM)] * 6,
         out_specs=(any_space,) * 6,
         scratch_shapes=[
             dma((6,)), dma((5, seqs)), dma((5, seqs)), dma((2, 2)), dma((2, 2)),
@@ -238,7 +238,6 @@
     wq = mixed_ref.shape[1]
     heads = wq // HEAD_SIZE
     rows = length // seqs
-
     @pl.loop(0, seqs)
     def _(i):
         at = pl.ds(pl.multiple_of(i * rows, rows), rows)
@@ -334,6 +333,8 @@
 
 
 PIECES = 4
+READY = 6
+SUMMED = 4
 
 
 def slot_rows(index, rows):
@@ -390,13 +391,13 @@
 
 
 def backward_kernel(
-    second_grad_ref, hidden_ref, cotangent_ref, gain_one_ref, gain_two_ref, lse_ref, cos_ref, sin_ref,
-    ids_row_ref, ids_col_ref, tokens_hbm, normed_hbm, w_hbm, out_hbm, qkv_hbm, mixed_hbm, order_hbm,
-    normed_grad_ref, hidden_grad_ref, w_grad_ref, out_grad_ref, bias_grad_ref, gain_grad_ref,
-    tokens_ref, normed_ref, w_ref, out_ref, qkv_ref, mixed_ref,
+    second_grad_ref, feed_ref, cotangent_ref, gain_one_ref, gain_two_ref, lse_ref, cos_ref, sin_ref,
+    ids_row_ref, ids_col_ref, hidden_hbm, tokens_hbm, normed_hbm, w_hbm, out_hbm, qkv_hbm, mixed_hbm,
+    normed_grad_ref, hidden_grad_ref, w_grad_ref, out_grad_ref, bias_grad_ref, gain_grad_ref, gain_two_grad_ref, layer_out_ref,
+    hidden_ref, tokens_ref, normed_ref, w_ref, out_ref, qkv_ref, mixed_ref,
     branch_ref, mixed_grad_ref, pre_grad_ref, key_grad_ref, value_grad_ref,
-    came_ref, sums_ref, one_ref, two_ref,
-    load_sem, sum_send, sum_recv, branch_send, branch_recv,
+    came_ref, sums_ref, one_ref, two_ref, came2_ref, sums2_ref, one2_ref, two2_ref,
+    load_sem, sum_send, sum_recv, sum2_send, sum2_recv, branch_send, branch_recv,
 ):
     seqs = lax.axis_size("seq")
     seq, dpi = lax.axis_index("seq"), lax.axis_index("dp")
@@ -409,6 +410,7 @@
         pltpu.make_async_copy(src, dst, load_sem.at[i])
         for i, (src, dst) in enumerate(
             (
+                (hidden_hbm.at[slot_rows(seq, rows)], hidden_ref),
                 (out_hbm, out_ref), (qkv_hbm, qkv_ref), (w_hbm, w_ref),
                 (tokens_hbm, tokens_ref), (normed_hbm, normed_ref), (mixed_hbm, mixed_ref),
             )
@@ -420,6 +422,7 @@
 
     total = SeqSum(second_grad_ref, rows, came_ref, sums_ref, one_ref, two_ref, (sum_send, sum_recv), dpi, seq)
     total.begin()
+    loads[0].wait()
     total.middle()
 
     def branch_at(k, c):
@@ -436,12 +439,14 @@
             branch_at(came, c), branch_at(came, c), branch_send.at[3, c], branch_recv.at[3, c], (seq ^ to, dpi)
         )
 
+    gain_two_grad_ref[...] = jnp.zeros_like(gain_two_grad_ref)
     for c in range(PIECES):
         at = pl.ds(c * piece, piece)
         grad = total.take(c)
         hidden = hidden_ref[at, :]
         factor = lax.rsqrt(jnp.mean(hidden * hidden, axis=-1, keepdims=True) + EPS)
         unit = hidden * factor
+        gain_two_grad_ref[...] += jnp.sum(grad * unit, axis=0, keepdims=True)
         scaled = grad * gain_two_ref[...]
         grad = cotangent_ref[at, :].astype(F32) + factor * (
             scaled - unit * jnp.mean(scaled * unit, axis=-1, keepdims=True)
@@ -452,7 +457,7 @@
         for k in (1, 2):
             branch_copy(k, c).start()
     total.finish()
-    for load in loads[:2]:
+    for load in loads[1:3]:
         load.wait()
 
     key_grad_ref[...] = jnp.zeros_like(key_grad_ref)
@@ -489,7 +494,10 @@
         attend_back(k)
     for c in range(PIECES):
         branch_copy(3, c).wait_recv()
+    feed = SeqSum(feed_ref, rows, came2_ref, sums2_ref, one2_ref, two2_ref, (sum2_send, sum2_recv), dpi, seq)
+    feed.begin()
     attend_back(3)
+    feed.middle()
     for c in range(PIECES):
         for k in (1, 2, 3):
             branch_copy(k, c).wait_send()
@@ -498,7 +506,7 @@
     pre_grad_ref[:, wq : wq + HEAD_SIZE] = rot_back(key_grad_ref[...] * SCALE, every).astype(BF)
     pre_grad_ref[:, wq + HEAD_SIZE :] = value_grad_ref[...].astype(BF)
     bias_grad_ref[...] = jnp.sum(pre_grad_ref[...].astype(F32), axis=0, keepdims=True)
-    for load in loads[2:]:
+    for load in loads[3:]:
         load.wait()
     gain_grad_ref[...] = jnp.zeros_like(gain_grad_ref)
 
@@ -517,9 +525,14 @@
         w_grad_ref[pl.ds(pl.multiple_of(i * wq, HEAD_SIZE), wq), :] = tn(normed_ref[:, lanes], pre_grad_ref[...]).astype(BF)
         out_grad_ref[:, lanes] = tn(mixed_ref[...], branch_ref[:, lanes]).astype(BF)
 
+    for c in range(PIECES):
+        at = pl.ds(c * piece, piece)
+        layer_out_ref[at, :] = (hidden_ref[at, :] + feed.take(c)).astype(BF)
+    feed.finish()
+
 
 def backward_call(
-    second_grad, hidden, cotangent, gain_one, gain_two, logsum, cosine, sine, ids, tokens, normed, w, out, qkv, mixed, order
+    second_grad, feed, cotangent, gain_one, gain_two, logsum, cosine, sine, ids, hidden, tokens, normed, w, out, qkv, mixed
 ):
     seqs = lax.axis_size("seq")
     length, model = tokens.shape
@@ -538,18 +551,22 @@
             shape((wq, model), BF),
             shape((1, wide), F32),
             shape((1, model), F32),
+            shape((1, model), F32),
+            shape((rows, model), BF),
         ),
         in_specs=[vmem] * 10 + [hbm] * 7,
-        out_specs=(vmem,) * 6,
-        scratch_shapes=[pltpu.VMEM(field.shape, field.dtype) for field in (tokens, normed, w, out, qkv, mixed)]
+        out_specs=(vmem,) * 8,
+        scratch_shapes=[pltpu.VMEM((rows, model), F32)]
+        + [pltpu.VMEM(field.shape, field.dtype) for field in (tokens, normed, w, out, qkv, mixed)]
         + [
             pltpu.VMEM((length, model), BF),
             pltpu.VMEM((length, wq), BF),
             pltpu.VMEM((length, wide), BF),
             pltpu.VMEM((length, HEAD_SIZE), F32),
             pltpu.VMEM((length, HEAD_SIZE), F32),
-            held, held, held, held,
-            dma((6,)), dma((3, PIECES)), dma((3, PIECES)), dma((4, PIECES)), dma((4, PIECES)),
+            held, held, held, held, held, held, held, held,
+            dma((7,)), dma((3, PIECES)), dma((3, PIECES)), dma((3, PIECES)), dma((3, PIECES)),
+            dma((4, PIECES)), dma((4, PIECES)),
         ],
         cost_estimate=pl.CostEstimate(flops=13 * 10**9, bytes_accessed=30 * 10**6, transcendentals=3 * 10**6),
         compiler_params=pltpu.CompilerParams(
@@ -557,114 +574,435 @@
         ),
         name="backward",
     )(
-        second_grad, hidden, cotangent, gain_one[None], gain_two[None], logsum, cosine, sine,
-        ids[None], ids[:, None], tokens, normed, w, out, qkv, mixed, order,
+        second_grad, feed, cotangent, gain_one[None], gain_two[None], logsum, cosine, sine,
+        ids[None], ids[:, None], hidden, tokens, normed, w, out, qkv, mixed,
     )
 
 
 TILE = 256
 
 
-def act_kernel(x_ref, w_ref, active_ref, by_gate_ref, by_up_ref, *, tail):
-    last = pl.program_id(0) == pl.num_programs(0) - 1
-
-    def body(shift):
-        both = jnp.dot(x_ref[...], w_ref[...], preferred_element_type=F32)
-        gate, up = both[:, :TILE], both[:, shift : shift + TILE]
-        sigma = jax.nn.sigmoid(gate)
-        silu = gate * sigma
-        active_ref[...] = (silu * up).astype(BF)
-        by_gate_ref[...] = (up * sigma * (1.0 + gate * (1.0 - sigma))).astype(BF)
-        by_up_ref[...] = silu.astype(BF)
-
-    if tail == TILE:
-        body(TILE)
-    else:
-        pl.when(jnp.logical_not(last))(lambda: body(TILE))
-        pl.when(last)(lambda: body(tail))
-
-
-def act_call(x, both):
-    rows, model = x.shape
-    units = both.shape[1] // 2
+class ChipGather:
+    def __init__(self, whole, columns, sems, seq, dpi, chips, own=None):
+        self.whole, self.columns, self.sems, self.own = whole, columns, sems, own
+        self.seq, self.dpi, self.chips = seq, dpi, chips
+        self.chip, self.core = dpi // 2, dpi % 2
+
+    def copy(self, kind, s, chip, core, to):
+        block = self.whole.at[chip * 2 + core, :, self.columns]
+        send, recv = self.sems
+        src = block if s or self.own is None else self.own.at[:, self.columns]
+        return remote(src, block, send.at[kind, s], recv.at[kind, s], (self.seq, to))
+
+    def copies(self, s):
+        z, c = self.chip, self.core
+        low, high = z - s, z + s
+        sibling = z * 2 + 1 - c
+        out = [
+            ((low >= 0) & (z < self.chips - 1), self.copy(0, s, low, c, self.dpi + 2)),
+            ((high < self.chips) & (z > 0), self.copy(1, s, high, c, self.dpi - 2)),
+            (low >= 0, self.copy(2, s, low, c, sibling)),
+        ]
+        if s > 0:
+            out.append((high < self.chips, self.copy(3, s, high, c, sibling)))
+        return out
+
+    def send(self, s):
+        for condition, copy in self.copies(s):
+            pl.when(condition)(copy.start)
+
+    def sent(self, s):
+        for condition, copy in self.copies(s):
+            pl.when(condition)(copy.wait_send)
+
+    def came(self, s):
+        z, c = self.chip, self.core
+        pl.when(z - s >= 0)(self.copy(0, s - 1, z - s, c, self.dpi).wait_recv)
+        pl.when(z + s < self.chips)(self.copy(1, s - 1, z + s, c, self.dpi).wait_recv)
+
+    def came_across(self, s):
+        z, c = self.chip, self.core
+        pl.when(z - s >= 0)(self.copy(2, s, z - s, 1 - c, self.dpi).wait_recv)
+        if s > 0:
+            pl.when(z + s < self.chips)(self.copy(3, s, z + s, 1 - c, self.dpi).wait_recv)
+
+
+class ChipScatter:
+    def __init__(self, terms, got, held, sems, seq, dpi, chips):
+        self.terms, self.got, self.held, self.sems = terms, got, held, sems
+        self.seq, self.dpi, self.chips = seq, dpi, chips
+        self.chip, self.core = dpi // 2, dpi % 2
+
+    def give(self):
+        send, recv = self.sems
+        return remote(
+            self.terms.at[:, 1 - self.core], self.got, send.at[2, 0], recv.at[2, 0], (self.seq, self.chip * 2 + 1 - self.core)
+        )
+
+    def up(self, d, to, field=None):
+        send, recv = self.sems
+        return remote((field or self.held).at[d], self.held.at[d], send.at[0, d], recv.at[0, d], (self.seq, to))
+
+    def down(self, d, to, last, field=None):
+        send, recv = self.sems
+        slot = self.chips if last else d
+        return remote((field or self.held).at[d], self.held.at[slot], send.at[1, d], recv.at[1, d], (self.seq, to))
+
+    def each(self, body):
+        size = self.got.shape[1]
+        chunk = 16 if size % 16 == 0 else size
+
+        @pl.loop(0, size // chunk)
+        def _(i):
+            body(pl.ds(pl.multiple_of(i * chunk, chunk), chunk))
+
+    def take(self):
+        self.give().wait()
+
+        @pl.loop(0, self.chips)
+        def _(d):
+            def body(rows):
+                own = self.terms[d, self.core, rows, :].astype(F32)
+                self.got[d, rows, :] = (own + self.got[d, rows, :].astype(F32)).astype(BF)
+
+            self.each(body)
+
+    def add(self, d):
+        def body(rows):
+            total = self.got[d, rows, :].astype(F32) + self.held[d, rows, :].astype(F32)
+            self.held[d, rows, :] = total.astype(BF)
+
+        self.each(body)
+
+    def step(self, r):
+        z, chips = self.chip, self.chips
+
+        @pl.when(z + r < chips)
+        def _():
+            d = z + r
+
+            @pl.when(z > 0)
+            def _():
+                self.up(d, self.dpi).wait_recv()
+                self.add(d)
+                self.up(d, self.dpi + 2).start()
+
+            @pl.when(z == 0)
+            def _():
+                self.up(d, self.dpi + 2, self.got).start()
+
+        @pl.when(z - r >= 0)
+        def _():
+            d = z - r
+
+            @pl.when(z < chips - 1)
+            def _():
+                self.down(d, self.dpi, False).wait_recv()
+                self.add(d)
+                self.down(d, self.dpi - 2, r == 1).start()
+
+            @pl.when(z == chips - 1)
+            def _():
+                self.down(d, self.dpi - 2, r == 1, self.got).start()
+
+    def finish(self, result):
+        z, chips = self.chip, self.chips
+        pl.when(z > 0)(lambda: self.up(z, self.dpi).wait_recv())
+        pl.when(z < chips - 1)(lambda: self.down(z, self.dpi, True).wait_recv())
+
+        def body(rows):
+            total = self.got[z, rows, :].astype(F32)
+            total += jnp.where(z > 0, self.held[z, rows, :].astype(F32), 0.0)
+            result[rows, :] = total + jnp.where(z < chips - 1, self.held[chips, rows, :].astype(F32), 0.0)
+
+        self.each(body)
+        for r in range(1, chips):
+            pl.when(z + r < chips)(lambda: self.up(z + r, self.dpi + 2).wait_send())
+            pl.when(z - r >= 0)(lambda: self.down(z - r, self.dpi - 2, r == 1).wait_send())
+
+
+def feed_kernel(
+    second_ref, incoming_ref, first_hbm, own_ref,
+    whole_out, out_hbm, grad_hbm, rest_hbm, mine_ref,
+    second_turned_ref, incoming_turned_ref, w_ref, terms_ref, got_ref, held_ref, active_ref, both_ref, out_ref, grad_ref, stage_ref,
+    load_sem, store_sem, stage_sem, own_sem, ahead_send, ahead_recv, sum_send, sum_recv,
+    *, tiles, ready, summed,
+):
+    dps = lax.axis_size("dp")
+    chips = dps // 2
+    seq, dpi = lax.axis_index("seq"), lax.axis_index("dp")
+    chip, core = dpi // 2, dpi % 2
+    length, model = second_ref.shape
+    width = 3 * TILE
+    later = own_ref.shape[1] // width if ready < tiles else 0
+    loose = ready >= chips + 2
+    above, below = ((chip + 1) % chips) * 2 + core, ((chip + chips - 1) % chips) * 2 + core
+    greet([(seq, above), (seq, below), (seq, chip * 2 + 1 - core)])
+
+    def columns(t):
+        return pl.ds(pl.multiple_of(t * width, width), width)
+
+    def load(t, source=first_hbm):
+        return pltpu.make_async_copy(source.at[:, :, columns(t)], w_ref.at[t % 2], load_sem.at[t % 2])
+
+    def start_load(t):
+        pl.when(t < ready)(lambda: load(t).start())
+        if later > 0:
+            first = columns(t - ready)
+            ahead = pltpu.make_async_copy(whole_out.at[:, :, first], w_ref.at[t % 2], load_sem.at[t % 2])
+            pl.when(within(t, ready, tiles))(ahead.start)
+
+    def store(t):
+        return pltpu.make_async_copy(
+            terms_ref.at[t % 3], rest_hbm.at[:, :, :, columns(t - summed)], store_sem.at[t % 3]
+        )
+
+    def gather(q):
+        return ChipGather(
+            whole_out, columns(q), (ahead_send.at[q], ahead_recv.at[q]), seq, dpi, chips, own_ref
+        )
+
+    def scatter(t):
+        return ChipScatter(
+            terms_ref.at[t % 3], got_ref.at[t], held_ref.at[t], (sum_send.at[t], sum_recv.at[t]), seq, dpi, chips
+        )
+
+    def within(value, low, high):
+        return (value >= low) & (value < high)
+
+    load(0).start()
+    own = pltpu.make_async_copy(own_ref, whole_out.at[dpi], own_sem)
+    own.start()
+    out_ref[...] = jnp.zeros_like(out_ref)
+    grad_ref[...] = jnp.zeros_like(grad_ref)
+
+    @pl.loop(0, length // TILE)
+    def _(i):
+        at = slot_rows(i, TILE)
+        second_turned_ref[:, at] = second_ref[at, :].T
+        incoming_turned_ref[:, at] = incoming_ref[at, :].T
+
+    own.wait()
+    far = list(range(chips - 1, 0, -1))
+    thirds = [far[: -(-len(far) // 3)], far[-(-len(far) // 3) : -(-2 * len(far) // 3)], far[-(-2 * len(far) // 3) :]]
+
+    @pl.loop(0, tiles)
+    def _(t):
+        def sent_at(tick):
+            q = tick - tick // 3 if loose else tick
+            return (tick >= 0) & (q < later) & ((tick % 3 != 2) if loose else True), q
+
+        def pass_on(s):
+            if later > 0:
+                one, q = sent_at(t - s)
+
+                @pl.when(one)
+                def _():
+                    gather(q).came(s)
+                    gather(q).send(s)
+
+        def sum_on(part):
+            if part == 0:
+                pl.when(within(t - 1, 0, summed))(lambda: scatter(t - 1).take())
+            v = t - 1 - part
+            j = v - v // 3
+
+            @pl.when((v >= 0) & (v % 3 != 2) & (j < summed))
+            def _():
+                sums = scatter(j)
+                if part == 3:
+                    sums.finish(mine_ref.at[j])
+                else:
+                    for r in thirds[part]:
+                        sums.step(r)
+
+        if later > 0:
+            one, q = sent_at(t)
+            pl.when(one)(lambda: gather(q).send(0))
+            arrived, q_last = sent_at(t - chips)
+
+            @pl.when(arrived)
+            def _():
+                for s in range(chips):
+                    gather(q_last).came_across(s)
+                    gather(q_last).sent(s)
+
+        start_load(t + 1)
+        pltpu.make_async_copy(
+            first_hbm.at[:, :, pl.ds(0, width)], w_ref.at[t % 2], load_sem.at[t % 2]
+        ).wait()
+        pl.when(t - 3 >= summed)(lambda: store(t - 3).wait())
+
+        w = w_ref[t % 2].reshape(model, width)
+        for i in range(2):
+            at = slice(i * length // 2, (i + 1) * length // 2)
+            both = nn(second_ref[at, :], w[:, : 2 * TILE])
+            back = nn(incoming_ref[at, :], w[:, 2 * TILE :])
+            gate, up = both[:, :TILE], both[:, TILE:]
+            sigma = jax.nn.sigmoid(gate)
+            silu = gate * sigma
+            active_ref[at, :] = (silu * up).astype(BF)
+            both_ref[at, :TILE] = (back * up * sigma * (1.0 + gate * (1.0 - sigma))).astype(BF)
+            both_ref[at, TILE:] = (back * silu).astype(BF)
+        pass_on(1)
+        sum_on(0)
+        rows = (chips, 2, model // dps)
+        terms_ref[t % 3, :, :, :, : 2 * TILE] = nn(second_turned_ref[...], both_ref[...], BF).reshape(rows + (2 * TILE,))
+        terms_ref[t % 3, :, :, :, 2 * TILE :] = nn(incoming_turned_ref[...], active_ref[...], BF).reshape(rows + (TILE,))
+        pl.when(t < summed)(lambda: scatter(t).give().start())
+        pl.when(t >= summed)(lambda: store(t).start())
+        for s in range(2, chips - 1):
+            pass_on(s)
+        sum_on(1)
+        for i in range(2):
+            at = slice(i * length // 2, (i + 1) * length // 2)
+            w = w_ref[t % 2].reshape(model, width)
+            grad_ref[at, :] += nt(both_ref[at, :], w[:, : 2 * TILE])
+            out_ref[at, :] += nt(active_ref[at, :], w[:, 2 * TILE :])
+            if i == 0:
+                sum_on(2)
+        pass_on(chips - 1)
+        sum_on(3)
+
+    for j in range(summed):
+        for part in range(4):
+            if 1 + j + j // 2 + part >= tiles:
+                if part == 3:
+                    scatter(j).finish(mine_ref.at[j])
+                else:
+                    for r in thirds[part]:
+                        scatter(j).step(r)
+    for t in range(max(summed, tiles - 3), tiles):
+        store(t).wait()
+    quarter = length // 4
+    stores = []
+    for i in range(8):
+        src, dst = (grad_ref, grad_hbm) if i < 4 else (out_ref, out_hbm)
+        at = pl.ds((i % 4) * quarter, quarter)
+        if i >= 2:
+            stores[i - 2].wait()
+        stage_ref[i % 2] = src[at, :].astype(BF)
+        stores.append(pltpu.make_async_copy(stage_ref.at[i % 2], dst.at[at], stage_sem.at[i % 2]))
+        stores[-1].start()
+    for copy in stores[-2:]:
+        copy.wait()
+
+
+def feed_call(second, incoming, first, own, summed):
+    dps, share, columns = first.shape
+    chips = dps // 2
+    length, model = second.shape
+    width = 3 * TILE
+    ready = columns // width
+    tiles = ready + own.shape[1] // width
+    if tiles == ready:
+        own = jnp.zeros((share, 128), BF)
+    vmem, hbm = pl.BlockSpec(memory_space=pltpu.VMEM), pl.BlockSpec(memory_space=pl.ANY)
+    shape, dma = jax.ShapeDtypeStruct, pltpu.SemaphoreType.DMA
+    return pl.pallas_call(
+        functools.partial(feed_kernel, tiles=tiles, ready=ready, summed=summed),
+        out_shape=(
+            shape((dps,) + own.shape, BF),
+            shape((length, model), BF),
+            shape((length, model), BF),
+            shape((chips, 2, share, (tiles - summed) * width), BF),
+            shape((summed, share, width), F32),
+        ),
+        in_specs=[vmem, vmem, hbm, vmem],
+        out_specs=(hbm, hbm, hbm, hbm, vmem),
+        scratch_shapes=[
+            pltpu.VMEM((model, length), BF),
+            pltpu.VMEM((model, length), BF),
+            pltpu.VMEM((2, dps, share, width), BF),
+            pltpu.VMEM((3, chips, 2, share, width), BF),
+            pltpu.VMEM((summed, chips, share, width), BF),
+            pltpu.VMEM((summed, chips + 1, share, width), BF),
+            pltpu.VMEM((length, TILE), BF),
+            pltpu.VMEM((length, 2 * TILE), BF),
+            pltpu.VMEM((length, model), F32),
+            pltpu.VMEM((length, model), F32),
+            pltpu.VMEM((2, length // 4, model), BF),
+            dma((2,)), dma((3,)), dma((2,)), dma,
+            dma((max(tiles - ready, 1), 4, chips)), dma((max(tiles - ready, 1), 4, chips)),
+            dma((summed, 3, chips)), dma((summed, 3, chips)),
+        ],
+        cost_estimate=pl.CostEstimate(flops=65 * 10**9, bytes_accessed=60 * 10**6, transcendentals=3 * 10**6),
+        compiler_params=pltpu.CompilerParams(
+            collective_id=4, has_side_effects=True, vmem_limit_bytes=63 * 2**20
+        ),
+        name="feed_forward",
+    )(second, incoming, first, own)
+
+
+def pack_kernel(gate_ref, up_ref, down_ref, first_ref, rest_ref):
+    units = gate_ref.shape[1]
+    split = first_ref.shape[1] // (3 * TILE)
+    for t in range(-(-units // TILE)):
+        size = min(TILE, units - t * TILE)
+        ref, at = (first_ref, t) if t < split else (rest_ref, t - split)
+        lanes = slice(t * TILE, t * TILE + size)
+        for i, part in enumerate((gate_ref[:, lanes], up_ref[:, lanes], down_ref[:, lanes])):
+            low = (3 * at + i) * TILE
+            ref[:, low : low + size] = part
+            if size < TILE:
+                ref[:, low + size : low + TILE] = jnp.zeros((part.shape[0], TILE - size), BF)
+
+
+def pack_call(gate, up, down, ready):
+    rows, units = gate.shape
     tiles = -(-units // TILE)
-    tail = units - (tiles - 1) * TILE
-    tile = pl.BlockSpec((rows, TILE), lambda j: (0, j))
+    vmem = pl.BlockSpec(memory_space=pltpu.VMEM)
+    width = 3 * TILE
     return pl.pallas_call(
-        functools.partial(act_kernel, tail=tail),
-        grid=(tiles,),
-        out_shape=[jax.ShapeDtypeStruct((rows, units), BF)] * 3,
-        in_specs=[
-            pl.BlockSpec((rows, model), lambda j: (0, 0)),
-            pl.BlockSpec((model, 2 * TILE), lambda j: (0, j)),
+        pack_kernel,
+        out_shape=[
+            jax.ShapeDtypeStruct((rows, ready * width), BF),
+            jax.ShapeDtypeStruct((rows, max(tiles - ready, 1) * width), BF),
         ],
-        out_specs=[tile] * 3,
-        cost_estimate=pl.CostEstimate(
-            flops=4 * rows * model * units,
-            bytes_accessed=2 * (both.size + x.size + 3 * rows * units),
-            transcendentals=rows * units,
-        ),
-        compiler_params=pltpu.CompilerParams(vmem_limit_bytes=56 * 2**20),
-        name="gate_up",
-    )(x, both)
-
-
-def back_kernel(order_ref, x_ref, w_ref, by_gate_ref, by_up_ref, out_ref, *, tail):
-    last = pl.program_id(0) == pl.num_programs(0) - 1
-
-    def body(widths):
-        back = jnp.dot(x_ref[...], w_ref[...], preferred_element_type=F32)
-        to_gate = (back * by_gate_ref[...].astype(F32)).astype(BF)
-        to_up = (back * by_up_ref[...].astype(F32)).astype(BF)
-        for i, width in enumerate(widths):
-            low = i * TILE
-            pair = jnp.concatenate([to_gate[:, low : low + width], to_up[:, low : low + width]], axis=1)
-            out_ref[:, 2 * low : 2 * low + 2 * width] = pair
-
-    if tail == (TILE, TILE):
-        body(tail)
-    else:
-        pl.when(jnp.logical_not(last))(lambda: body((TILE, TILE)))
-        pl.when(last)(lambda: body(tail))
-
-
-def back_call(order, x, down, by_gate, by_up):
-    rows, model = x.shape
-    units = down.shape[1]
-    step = 2 * TILE
-    tiles = -(-units // step)
-    rest = units - (tiles - 1) * step
-    tail = (rest,) if rest <= TILE else (TILE, rest - TILE)
-    tile = pl.BlockSpec((rows, step), lambda j: (0, j))
+        in_specs=[vmem] * 3,
+        out_specs=[vmem] * 2,
+        cost_estimate=pl.CostEstimate(flops=0, bytes_accessed=10**7, transcendentals=0),
+        compiler_params=pltpu.CompilerParams(vmem_limit_bytes=32 * 2**20),
+        name="pack_weights",
+    )(gate, up, down)
+
+
+def unpack_kernel(summed_ref, rest_ref, gate_ref, up_ref, down_ref):
+    units = gate_ref.shape[1]
+    split = summed_ref.shape[0]
+    for t in range(-(-units // TILE)):
+        size = min(TILE, units - t * TILE)
+        lanes = slice(t * TILE, t * TILE + size)
+        for i in range(3):
+            if t < split:
+                part = summed_ref[t, :, i * TILE : i * TILE + size]
+            else:
+                low = (3 * (t - split) + i) * TILE
+                part = rest_ref[:, low : low + size].astype(F32)
+            (gate_ref, up_ref, down_ref)[i][:, lanes] = part
+
+
+def unpack_call(summed, rest, units):
+    rows = rest.shape[0]
+    vmem = pl.BlockSpec(memory_space=pltpu.VMEM)
     return pl.pallas_call(
-        functools.partial(back_kernel, tail=tail),
-        grid=(tiles,),
-        out_shape=jax.ShapeDtypeStruct((rows, 2 * units), BF),
-        in_specs=[
-            pl.BlockSpec(memory_space=pl.ANY),
-            pl.BlockSpec((rows, model), lambda j: (0, 0)),
-            pl.BlockSpec((model, step), lambda j: (0, j)),
-            tile,
-            tile,
-        ],
-        out_specs=pl.BlockSpec((rows, 2 * step), lambda j: (0, j)),
-        cost_estimate=pl.CostEstimate(
-            flops=2 * rows * model * units,
-            bytes_accessed=2 * (down.size + x.size + 4 * rows * units),
-            transcendentals=0,
-        ),
-        compiler_params=pltpu.CompilerParams(vmem_limit_bytes=56 * 2**20),
-        name="back_down",
-    )(order, x, down, by_gate, by_up)
+        unpack_kernel,
+        out_shape=[jax.ShapeDtypeStruct((rows, units), F32)] * 3,
+        in_specs=[vmem] * 2,
+        out_specs=[vmem] * 3,
+        cost_estimate=pl.CostEstimate(flops=0, bytes_accessed=10**7, transcendentals=0),
+        compiler_params=pltpu.CompilerParams(vmem_limit_bytes=32 * 2**20),
+        name="unpack_gradients",
+    )(summed, rest)
 
 
 def end_kernel(
-    normed_grad_ref, hidden_grad_ref, x_ref, gain_ref, qkv_ref, out_ref, small_ref, feed_ref, hidden_ref,
-    input_grad_ref, qkv_out_ref, out_out_ref, small_out_ref, layer_out_ref,
+    normed_grad_ref, hidden_grad_ref, x_ref, gain_ref, qkv_ref, out_ref, small_ref,
+    input_grad_ref, qkv_out_ref, out_out_ref, small_out_ref,
     qkv_got_ref, out_got_ref, small_got_ref,
     qkv_move_ref, out_move_ref, small_move_ref, qkv_came_ref, out_came_ref, small_came_ref,
-    came_ref, sums_ref, one_ref, two_ref, came2_ref, sums2_ref, one2_ref, two2_ref,
-    sum_send, sum_recv, sum2_send, sum2_recv, core_send, core_recv, ring_send, ring_recv, seq_send, seq_recv,
+    came_ref, sums_ref, one_ref, two_ref,
+    sum_send, sum_recv, core_send, core_recv, ring_send, ring_recv, seq_send, seq_recv,
 ):
     seqs, dps = lax.axis_size("seq"), lax.axis_size("dp")
     chips = dps // 2
@@ -687,7 +1025,6 @@
         copy.start()
     total = SeqSum(normed_grad_ref, rows, came_ref, sums_ref, one_ref, two_ref, (sum_send, sum_recv), dpi, seq)
     total.begin()
-    feed = SeqSum(feed_ref, rows, came2_ref, sums2_ref, one2_ref, two2_ref, (sum2_send, sum2_recv), dpi, seq)
     for copy in cores:
         copy.wait_recv()
 
@@ -729,14 +1066,9 @@
             copy.start()
         if step == 0:
             total.middle()
-            feed.begin()
         if step == 1:
             for c in range(PIECES):
                 input_piece(c)
-            feed.middle()
-    for c in range(PIECES):
-        at = pl.ds(c * piece, piece)
-        layer_out_ref[at, :] = (hidden_ref[at, :] + feed.take(c)).astype(BF)
     for copy in ring(chips - 2):
         copy.wait_recv()
     qkv, out, small = term(chip, chips - 1)
@@ -757,14 +1089,13 @@
     qkv_out_ref[seq] = qkv_move_ref[chips - 1, seq]
     small_out_ref[seq] = small_move_ref[chips - 1]
     total.finish()
-    feed.finish()
     for copy in cores + [copy for step in range(chips - 1) for copy in ring(step)]:
         copy.wait_send()
     for copy in last:
         copy.wait()
 
 
-def end_call(normed_grad, hidden_grad, x, gain, qkv, out, small, feed, hidden):
+def end_call(normed_grad, hidden_grad, x, gain, qkv, out, small):
     seqs, chips, _, share, wide = qkv.shape
     rows, model = x.shape
     vmem = pl.BlockSpec(memory_space=pltpu.VMEM)
@@ -778,10 +1109,9 @@
             shape(blocks[0], BF),
             shape(blocks[1], F32),
             shape((seqs,) + blocks[2], BF),
-            shape((rows, model), BF),
         ),
-        in_specs=[vmem] * 9,
-        out_specs=(vmem,) * 5,
+        in_specs=[vmem] * 7,
+        out_specs=(vmem,) * 4,
         scratch_shapes=[
             pltpu.VMEM((seqs, chips, share, wide), BF),
             pltpu.VMEM((chips, share, model), BF),
@@ -790,8 +1120,8 @@
         + [pltpu.VMEM((chips,) + block, BF) for block in blocks]
         + [pltpu.VMEM((chips - 1,) + block, BF) for block in blocks]
         + [
-            held, held, held, held, held, held, held, held,
-            dma((3, PIECES)), dma((3, PIECES)), dma((3, PIECES)), dma((3, PIECES)), dma((3,)), dma((3,)),
+            held, held, held, held,
+            dma((3, PIECES)), dma((3, PIECES)), dma((3,)), dma((3,)),
             dma((3, chips)), dma((3, chips)), dma((2, seqs)), dma((2, seqs)),
         ],
         cost_estimate=pl.CostEstimate(flops=10**8, bytes_accessed=2 * 10**7, transcendentals=0),
@@ -799,7 +1129,7 @@
             collective_id=3, has_side_effects=True, vmem_limit_bytes=48 * 2**20
         ),
         name="end_sums",
-    )(normed_grad, hidden_grad, x, gain[None], qkv, out, small, feed, hidden)
+    )(normed_grad, hidden_grad, x, gain[None], qkv, out, small)
 
 
 def pair_tiles(left, right):
@@ -862,6 +1192,11 @@
     ).transpose(1, 0, 2)
     one = small.shape[0]
     small = jnp.pad(small[None], ((0, 15), (0, -one % 128)))
+    tiles = -(-hidden_units // TILE)
+    ready = READY if chips <= 4 else tiles
+    first, later = pack_call(gate_weight, up_weight, down_weight.T, ready)
+    later = later if ready < tiles else later[:, :0]
+    first = lax.all_gather(first, "dp", axis=0, tiled=True).reshape(dps, model // dps, -1)
     tokens, incoming, blocks, smalls, weight_qkv, weight_out = start_call(
         inputs[0], cotangent[0], block_ids.reshape(-1, 128), small, packed, output_weight
     )
@@ -886,33 +1221,19 @@
     length = tokens.shape[0]
     cosine, sine = rope_tables(length)
 
-    gather = lambda field: lax.all_gather(field, "dp", axis=0, tiled=True)
-    whole_both = gather(pair_tiles(gate_weight, up_weight))
-    tokens, down_turned = lax.optimization_barrier((tokens, down_weight.T))
-    whole_down = gather(down_turned)
-
     normed, qkv, mixed, logsum, hidden, second = attend_call(
         tokens, weight_qkv, bias[None], cosine, sine, blocks, gain_first, gain_second, weight_out
     )
-    second_factor = lax.rsqrt(jnp.mean(hidden * hidden, axis=-1, keepdims=True) + EPS)
-    own = lambda field: lax.dynamic_slice_in_dim(field, seq * tokens_here, tokens_here, 0)
-    active, by_gate, by_up = act_call(second, whole_both)
-    scatter = lambda field: lax.psum_scatter(field, "dp", scatter_dimension=0, tiled=True)
-    down_grad = tn(incoming, active, BF)
-    grad_both = back_call(down_grad, incoming, whole_down, by_gate, by_up)
-    down_grad = scatter(down_grad).astype(F32)
-    second_sum = nt(grad_both, whole_both)
-    gain_two_grad = jnp.sum(second_sum * (hidden * second_factor), axis=0)
-    second, second_sum = lax.optimization_barrier((second, second_sum.astype(BF)))
-    both_grad = tn(second, grad_both, BF)
-    gate_grad, up_grad = split_tiles(scatter(both_grad).astype(F32))
-    normed_grad, grad_hidden, qkv_grad, out_weight_grad, bias_grad, gain_one_grad = backward_call(
-        second_sum, own(hidden), cotangent[0], gain_first, gain_second, logsum, cosine, sine, blocks,
-        tokens, normed, weight_qkv, out_head, qkv, mixed, both_grad,
-    )
-    bias_grad, gain_one_grad = bias_grad[0], gain_one_grad[0]
-    normed_grad, whole_down = lax.optimization_barrier((normed_grad, whole_down))
-    out_sum = nt(active, whole_down, BF)
+    second, out_head = lax.optimization_barrier((second, out_head))
+    _, out_sum, second_sum, rest, summed = feed_call(second, incoming, first, later, SUMMED)
+    rest = rest.reshape(model, -1)
+    rest = lax.psum_scatter(rest, "dp", scatter_dimension=0, tiled=True)
+    gate_grad, up_grad, down_grad = unpack_call(summed, rest, hidden_units)
+    normed_grad, grad_hidden, qkv_grad, out_weight_grad, bias_grad, gain_one_grad, gain_two_grad, layer_out = backward_call(
+        second_sum, out_sum, cotangent[0], gain_first, gain_second, logsum, cosine, sine, blocks,
+        hidden, tokens, normed, weight_qkv, out_head, qkv, mixed,
+    )
+    bias_grad, gain_one_grad, gain_two_grad = bias_grad[0], gain_one_grad[0], gain_two_grad[0]
 
     place = lambda field, count, at: jnp.where(
         (jnp.arange(count) == at)[:, None], field[None], 0.0
@@ -931,12 +1252,11 @@
     small_grad = small_grad.transpose(1, 0, 2).reshape(dps, seqs * one).astype(BF)
     small_grad = jnp.pad(small_grad, ((0, 0), (0, small_rows * wide - seqs * one)))
     small_grad = jnp.pad(small_grad.reshape(dps, -1, wide), ((0, 0), (0, 16 - small_rows), (0, 0)))
-    input_grad, parts, out_weight_grad, smalls, layer_out = end_call(
+    input_grad, parts, out_weight_grad, smalls = end_call(
         normed_grad, grad_hidden, inputs[0], gain_first,
         qkv_grad.reshape(seqs, chips, 2, share, wide),
         out_weight_grad.reshape(chips, 2, share, model),
         small_grad.reshape(chips, 2, 16, wide),
-        out_sum, own(hidden),
     )
     smalls = smalls[:, :small_rows].reshape(seqs, -1)[:, : seqs * one].reshape(seqs, seqs, one)
     small_sum = jnp.sum(

time: 501 us -> 474 us (0.946)
  matrix products: 66 us -> 0 us
  Pallas kernels: 363 us -> 423 us
  waiting for transfers between devices: 16 us -> 3.98 us
  other arithmetic: 15.5 us -> 5.3 us
    dot_general x4 -> x0, matrix products: 66 us -> none  [dot(): lax.dot_general(a, b, (dims, ((), ())), preferred_element_type=F32)]
    pallas_call x3 -> x4, Pallas kernels: 154 us -> 216 us  [the longest x1 120 us: feed_call(): pl.pallas_call(functools.partial(feed_kernel, tiles=tiles, ready=ready, s...]
    pallas_call x1, Pallas kernels: 76.3 us -> 59.5 us  [end_call(): pl.pallas_call(end_kernel, out_shape=(shape((rows, model), BF), shape(blo...]
    pallas_call x1, Pallas kernels: 78.1 us -> 90.1 us  [backward_call(): pl.pallas_call(backward_kernel, out_shape=(shape((length, model), BF), sh...]
    unnamed x51 -> x45, local copies, waits for them, and re-layouts: 3.35 us -> 12.7 us
    reduce_scatter x2 -> x1, waiting for transfers between devices: 7.59 us -> 0.01 us  [shards(): rest = lax.psum_scatter(rest, 'dp', scatter_dimension=0, tiled=True)]
  transfers between devices with their start and end apart: 4 -> 2, of which waited for: 2 -> 1; matrix products, arithmetic and copies ran while one was open for 19% -> 3% of each run, Pallas kernels for 73% -> 63%
where the time goes in v5:
time: 474 us; the launch traced here: 471 us
  Pallas kernels  423 us (89%)
  local copies, waits for them, and re-layouts  23.6 us (5%)
  between operations  14.7 us (3%)
  other arithmetic  5.3 us (1%)
    pallas_call x1, Pallas kernels, feed_call(): pl.pallas_call(functools.partial(feed_kernel, tiles=tiles, ready=ready, s...  120 us
    pallas_call x1, Pallas kernels, start_call(): pl.pallas_call(start_kernel, out_shape=shapes, in_specs=[pl.BlockSpec(mem...  92.3 us
    pallas_call x1, Pallas kernels, backward_call(): pl.pallas_call(backward_kernel, out_shape=(shape((length, model), BF), sh...  90.1 us
    pallas_call x1, Pallas kernels, end_call(): pl.pallas_call(end_kernel, out_shape=(shape((rows, model), BF), shape(blo...  59.5 us
    pallas_call x1, Pallas kernels, attend_call(): pl.pallas_call(attend_kernel, out_shape=(shape((length, model), BF), shap...  56.9 us
    unnamed x45, local copies, waits for them, and re-layouts  12.7 us
  transfers between devices with their start and end apart: 2, of which 1 were waited for; matrix products, arithmetic and copies ran while one was open for 3% of the time, Pallas kernels for 63%

profile of v5, /device:TPU:0, one launch (start us, length us, event | category | flops | bytes accessed | tf_op | source)
XLA Modules:
  0.0 470.7 jit_solution(1318586358197058609)
XLA Ops:
  7.3 1.2 copy-done.7
  8.4 1.2 copy-done.8
  9.6 1.2 copy-done.9
  10.8 1.4 pack_weights.1
  12.2 0.9 copy-done.11
  14.0 0.7 maximum_bitcast_fusion.pack_in
  14.8 92.3 %start_gather.1 = (bf16[1024,1536]{1,0:T(8,128)(2,1)}, bf16[1024,1536]{1,0:T(8,128)(2,1)}, s32[4,2,128]{2,1,0:T(2,128)}, bf16[8,4,16,256]{3,2,1,0:T(8,128)(2,1)}...) custom-call(bf16[256,1536]{1,0:T(8,128)(2,1)} %bitcast.58, bf16[256,1536]{1,0:T(8,128)(2,1)} %bitcast.67, ...), custom_call_target="tpu_custom_call" | custom-call | tf_op jit(solution)/shard_map/start_gather/pallas_call | solution.py:214
  107.1 0.9 slice_convert_fusion
  108.3 0.7 broadcast_in_dim_reshape.20.gain_two_ref
  109.9 0.7 broadcast_in_dim_reshape.19.gain_one_ref.gain_ref
  110.5 1.7 copy.43.ids_col_ref
  112.2 2.4 slice.84
  114.6 56.9 %attend.1 = (bf16[1024,1536]{1,0:T(8,128)(2,1)}, bf16[1024,640]{1,0:T(8,128)(2,1)}, bf16[1024,384]{1,0:T(8,128)(2,1)}, f32[1024,128]{1,0:T(8,128)}, f32[1024,1536]{1,0:T(8,128)}, /*index=5*/bf16[1024,1536]{1,0:T(8,128)(2,1)}) custom-call(bf16[1024,1536]{1,0:T(8,128)(2,1)} %get-tuple-element.49.x_ref.tokens_hbm, bf16[1536,640]{1,0:T(8,128)(2,1)} %bitcast.86, ...), custom_call_target="tpu_custom_call" | custom-call | flops 8999999488 | bytes 30000000 | tf_op jit(solution)/shard_map/attend/pallas_call | solution.py:310
  171.6 3.9 all-gather.2.cloned.1.call-done
  175.5 120.1 %feed_forward.1 = (bf16[8,192,2304]{2,1,0:T(8,128)(2,1)}, bf16[1024,1536]{1,0:T(8,128)(2,1)}, bf16[1024,1536]{1,0:T(8,128)(2,1)}, bf16[4,2,192,3840]{3,2,1,0:T(8,128)(2,1)}, f32[4,192,768]{2,1,0:T(8,128)}) custom-call(bf16[1024,1536]{1,0:T(8,128)(2,1)} %get-tuple-element.55.second_ref, bf16[1024,1536]{1,0:T(8,128)(2,1)} %get-tuple-element.56.incoming_ref, ...), custom_call_target="tpu_custom_call" | custom-call | flops 65000001536 | bytes 60000000 | tf_op jit(solution)/shard_map/feed_forward/pallas_call | solution.py:902
  295.8 90.1 %backward.1 = (bf16[1024,1536]{1,0:T(8,128)(2,1)}, f32[256,1536]{1,0:T(8,128)}, bf16[1536,640]{1,0:T(8,128)(2,1)}, bf16[384,1536]{1,0:T(8,128)(2,1)}, f32[1,640]...) custom-call(bf16[1024,1536]{1,0:T(8,128)(2,1)} %get-tuple-element.59.second_grad_ref, ...), custom_call_target="tpu_custom_call" | custom-call | flops 12999999488 | bytes 30000000 | tf_op jit(solution)/shard_map/backward/pallas_call | solution.py:545
  386.0 0.6 slice_reduce_fusion.1
  386.7 0.7 slice_reduce_fusion.2
  387.6 0.7 convert_reduce_fusion.1
  388.4 0.7 convert_reduce_fusion
  389.7 1.5 copy-done.4
  391.2 1.3 copy-done.6
  392.5 59.5 %end_sums.1 = (bf16[256,1536]{1,0:T(8,128)(2,1)S(1)}, bf16[4,48,640]{2,1,0:T(8,128)(2,1)S(1)}, f32[48,1536]{1,0:T(8,128)S(1)}, bf16[4,16,640]{2,1,0:T(8,128)(2,1)S(1)}) custom-call(bf16[1024,1536]{1,0:T(8,128)(2,1)} %get-tuple-element.68.normed_grad_ref, f32[256,1536]{1,0:T(8,128)S(1)} %copy-done.4, bf16[256,1536]{1,0:T(8,128)(2,1)S(1)} %bitcast.59, ...), custom_call_target="tpu_custom_call" | custom-call | flops 100000000 | bytes 20000000 | tf_op jit(solution)/shard_map/end_sums/pallas_call | solution.py:1105
  452.3 0.6 pad_maximum_fusion.1
  452.9 0.6 pad_maximum_fusion
  454.7 0.7 maximum_convert_fusion
  455.4 1.7 copy-done.3
  457.1 1.4 copy-done.5
  458.5 2.7 unpack_gradients.1
  461.2 0.9 copy.67
  462.0 0.9 copy.68
  462.9 0.7 copy.69
  (95 shorter events, 4.5 us)
Async XLA Ops:
  7.2 6.8 %copy-start = (bf16[48,256]{1,0:T(8,128)(2,1)S(1)}, bf16[48,256]{1,0:T(8,128)(2,1)}, u32[]{:S(2)}) copy-start(bf16[48,256]{1,0:T(8,128)(2,1)} %param.23) | copy-start | bytes 73732
  7.2 6.0 %copy-start.16 = (bf16[48]{0:T(256)(128)(2,1)S(1)}, bf16[48]{0:T(256)(128)(2,1)}, u32[]{:S(2)}) copy-start(bf16[48]{0:T(256)(128)(2,1)} %param.28) | copy-start | bytes 292
  7.2 6.0 %copy-start.17 = (bf16[48]{0:T(256)(128)(2,1)S(1)}, bf16[48]{0:T(256)(128)(2,1)}, u32[]{:S(2)}) copy-start(bf16[48]{0:T(256)(128)(2,1)} %param.22) | copy-start | bytes 292
  7.2 6.0 %copy-start.15 = (bf16[48]{0:T(256)(128)(2,1)S(1)}, bf16[48]{0:T(256)(128)(2,1)}, u32[]{:S(2)}) copy-start(bf16[48]{0:T(256)(128)(2,1)} %param.20) | copy-start | bytes 292
  7.2 168.3 %all-gather.2.cloned.1.call-start = ((), (), s32[]{:S(2)}) async-start(), calls=%async_computation.1 | async-start | bytes 15925248 | tf_op jit(solution)/shard_map/all_gather | solution.py:1199
  7.3 1.2 copy-start.7
  8.4 1.2 copy-start.8
  9.6 1.2 copy-start.9
  10.8 2.4 copy-start.18
  10.8 2.5 copy-start.19
  10.8 2.6 copy-start.13
  10.8 3.2 copy-start.14
  12.2 0.9 copy-start.11
  13.1 442.3 %reduce-scatter.2.cloned.1.call-start = ((), (), s32[]{:S(2)}) async-start(), calls=%async_computation.2 | async-start | bytes 13271040 | tf_op jit(solution)/shard_map/reduce_scatter | solution.py:1230
  295.8 93.9 %copy-start.2 = (bf16[1,256,1536]{2,1,0:T(8,128)(2,1)S(1)}, bf16[1,256,1536]{2,1,0:T(8,128)(2,1)}, u32[]{:S(2)}) copy-start(bf16[1,256,1536]{2,1,0:T(8,128)(2,1)} %param.17) | copy-start | bytes 2359300
  295.8 93.9 %copy-start.10 = (f32[1,1536]{1,0:T(1,128)S(1)}, f32[1,1536]{1,0:T(1,128)}, u32[]{:S(2)}) copy-start(f32[1,1536]{1,0:T(1,128)} %broadcast_in_dim_reshape.19.gain_one_ref.gain_ref) | copy-start | bytes 18436
  389.7 1.5 copy-start.4
  391.2 1.3 copy-start.6
  452.0 9.2 %copy-start.12 = (bf16[256,1536]{1,0:T(8,128)(2,1)S(1)}, bf16[256,1536]{1,0:T(8,128)(2,1)}, u32[]{:S(2)}) copy-start(bf16[256,1536]{1,0:T(8,128)(2,1)} %get-tuple-element.67) | copy-start | bytes 2359300
  455.4 8.2 %copy-start.1 = (bf16[48,256]{1,0:T(8,128)(2,1)S(1)}, bf16[48,256]{1,0:T(8,128)(2,1)}, u32[]{:S(2)}) copy-start(bf16[48,256]{1,0:T(8,128)(2,1)} %param.23) | copy-start | bytes 73732
  455.4 1.7 copy-start.3
  457.1 1.4 copy-start.5
Sparse Core Ops, SparseCore 0:
  13.2 162.2 all-gather.1
  295.8 131.8 reduce-scatter.1

commit v6 on v5

--- a/solution.py
+++ b/solution.py
@@ -391,13 +391,13 @@
 
 
 def backward_kernel(
-    second_grad_ref, feed_ref, cotangent_ref, gain_one_ref, gain_two_ref, lse_ref, cos_ref, sin_ref,
+    second_grad_ref, cotangent_ref, gain_one_ref, gain_two_ref, lse_ref, cos_ref, sin_ref,
     ids_row_ref, ids_col_ref, hidden_hbm, tokens_hbm, normed_hbm, w_hbm, out_hbm, qkv_hbm, mixed_hbm,
-    normed_grad_ref, hidden_grad_ref, w_grad_ref, out_grad_ref, bias_grad_ref, gain_grad_ref, gain_two_grad_ref, layer_out_ref,
+    normed_grad_ref, hidden_grad_ref, w_grad_ref, out_grad_ref, bias_grad_ref, gain_grad_ref, gain_two_grad_ref,
     hidden_ref, tokens_ref, normed_ref, w_ref, out_ref, qkv_ref, mixed_ref,
     branch_ref, mixed_grad_ref, pre_grad_ref, key_grad_ref, value_grad_ref,
-    came_ref, sums_ref, one_ref, two_ref, came2_ref, sums2_ref, one2_ref, two2_ref,
-    load_sem, sum_send, sum_recv, sum2_send, sum2_recv, branch_send, branch_recv,
+    came_ref, sums_ref, one_ref, two_ref,
+    load_sem, sum_send, sum_recv, branch_send, branch_recv,
 ):
     seqs = lax.axis_size("seq")
     seq, dpi = lax.axis_index("seq"), lax.axis_index("dp")
@@ -494,10 +494,7 @@
         attend_back(k)
     for c in range(PIECES):
         branch_copy(3, c).wait_recv()
-    feed = SeqSum(feed_ref, rows, came2_ref, sums2_ref, one2_ref, two2_ref, (sum2_send, sum2_recv), dpi, seq)
-    feed.begin()
     attend_back(3)
-    feed.middle()
     for c in range(PIECES):
         for k in (1, 2, 3):
             branch_copy(k, c).wait_send()
@@ -525,14 +522,9 @@
         w_grad_ref[pl.ds(pl.multiple_of(i * wq, HEAD_SIZE), wq), :] = tn(normed_ref[:, lanes], pre_grad_ref[...]).astype(BF)
         out_grad_ref[:, lanes] = tn(mixed_ref[...], branch_ref[:, lanes]).astype(BF)
 
-    for c in range(PIECES):
-        at = pl.ds(c * piece, piece)
-        layer_out_ref[at, :] = (hidden_ref[at, :] + feed.take(c)).astype(BF)
-    feed.finish()
-
 
 def backward_call(
-    second_grad, feed, cotangent, gain_one, gain_two, logsum, cosine, sine, ids, hidden, tokens, normed, w, out, qkv, mixed
+    second_grad, cotangent, gain_one, gain_two, logsum, cosine, sine, ids, hidden, tokens, normed, w, out, qkv, mixed
 ):
     seqs = lax.axis_size("seq")
     length, model = tokens.shape
@@ -552,10 +544,9 @@
             shape((1, wide), F32),
             shape((1, model), F32),
             shape((1, model), F32),
-            shape((rows, model), BF),
         ),
-        in_specs=[vmem] * 10 + [hbm] * 7,
-        out_specs=(vmem,) * 8,
+        in_specs=[vmem] * 9 + [hbm] * 7,
+        out_specs=(vmem,) * 7,
         scratch_shapes=[pltpu.VMEM((rows, model), F32)]
         + [pltpu.VMEM(field.shape, field.dtype) for field in (tokens, normed, w, out, qkv, mixed)]
         + [
@@ -564,9 +555,8 @@
             pltpu.VMEM((length, wide), BF),
             pltpu.VMEM((length, HEAD_SIZE), F32),
             pltpu.VMEM((length, HEAD_SIZE), F32),
-            held, held, held, held, held, held, held, held,
-            dma((7,)), dma((3, PIECES)), dma((3, PIECES)), dma((3, PIECES)), dma((3, PIECES)),
-            dma((4, PIECES)), dma((4, PIECES)),
+            held, held, held, held,
+            dma((7,)), dma((3, PIECES)), dma((3, PIECES)), dma((4, PIECES)), dma((4, PIECES)),
         ],
         cost_estimate=pl.CostEstimate(flops=13 * 10**9, bytes_accessed=30 * 10**6, transcendentals=3 * 10**6),
         compiler_params=pltpu.CompilerParams(
@@ -574,7 +564,7 @@
         ),
         name="backward",
     )(
-        second_grad, feed, cotangent, gain_one[None], gain_two[None], logsum, cosine, sine,
+        second_grad, cotangent, gain_one[None], gain_two[None], logsum, cosine, sine,
         ids[None], ids[:, None], hidden, tokens, normed, w, out, qkv, mixed,
     )
 
@@ -967,7 +957,11 @@
     )(gate, up, down)
 
 
-def unpack_kernel(summed_ref, rest_ref, gate_ref, up_ref, down_ref):
+def unpack_kernel(summed_ref, rest_ref, *refs):
+    count = len(refs) // 2 - 1
+    gate_ref, up_ref, down_ref = refs[count : count + 3]
+    for src, dst in zip(refs[:count], refs[count + 3 :]):
+        dst[...] = src[...]
     units = gate_ref.shape[1]
     split = summed_ref.shape[0]
     for t in range(-(-units // TILE)):
@@ -982,27 +976,28 @@
             (gate_ref, up_ref, down_ref)[i][:, lanes] = part
 
 
-def unpack_call(summed, rest, units):
+def unpack_call(summed, rest, units, *given):
     rows = rest.shape[0]
     vmem = pl.BlockSpec(memory_space=pltpu.VMEM)
     return pl.pallas_call(
         unpack_kernel,
-        out_shape=[jax.ShapeDtypeStruct((rows, units), F32)] * 3,
-        in_specs=[vmem] * 2,
-        out_specs=[vmem] * 3,
+        out_shape=[jax.ShapeDtypeStruct((rows, units), F32)] * 3
+        + [jax.ShapeDtypeStruct(field.shape, field.dtype) for field in given],
+        in_specs=[vmem] * (2 + len(given)),
+        out_specs=[vmem] * (3 + len(given)),
         cost_estimate=pl.CostEstimate(flops=0, bytes_accessed=10**7, transcendentals=0),
         compiler_params=pltpu.CompilerParams(vmem_limit_bytes=32 * 2**20),
         name="unpack_gradients",
-    )(summed, rest)
+    )(summed, rest, *given)
 
 
 def end_kernel(
-    normed_grad_ref, hidden_grad_ref, x_ref, gain_ref, qkv_ref, out_ref, small_ref,
-    input_grad_ref, qkv_out_ref, out_out_ref, small_out_ref,
+    normed_grad_ref, hidden_grad_ref, x_ref, gain_ref, qkv_ref, out_ref, small_ref, feed_ref, hidden_hbm,
+    input_grad_ref, qkv_out_ref, out_out_ref, small_out_ref, layer_out_ref,
     qkv_got_ref, out_got_ref, small_got_ref,
     qkv_move_ref, out_move_ref, small_move_ref, qkv_came_ref, out_came_ref, small_came_ref,
-    came_ref, sums_ref, one_ref, two_ref,
-    sum_send, sum_recv, core_send, core_recv, ring_send, ring_recv, seq_send, seq_recv,
+    came_ref, sums_ref, one_ref, two_ref, came2_ref, sums2_ref, one2_ref, two2_ref, hidden_ref,
+    sum_send, sum_recv, sum2_send, sum2_recv, load_sem, core_send, core_recv, ring_send, ring_recv, seq_send, seq_recv,
 ):
     seqs, dps = lax.axis_size("seq"), lax.axis_size("dp")
     chips = dps // 2
@@ -1025,6 +1020,9 @@
         copy.start()
     total = SeqSum(normed_grad_ref, rows, came_ref, sums_ref, one_ref, two_ref, (sum_send, sum_recv), dpi, seq)
     total.begin()
+    feed = SeqSum(feed_ref, rows, came2_ref, sums2_ref, one2_ref, two2_ref, (sum2_send, sum2_recv), dpi, seq)
+    load = pltpu.make_async_copy(hidden_hbm.at[slot_rows(seq, rows)], hidden_ref, load_sem)
+    load.start()
     for copy in cores:
         copy.wait_recv()
 
@@ -1066,9 +1064,15 @@
             copy.start()
         if step == 0:
             total.middle()
+            feed.begin()
         if step == 1:
             for c in range(PIECES):
                 input_piece(c)
+            feed.middle()
+    load.wait()
+    for c in range(PIECES):
+        at = pl.ds(c * piece, piece)
+        layer_out_ref[at, :] = (hidden_ref[at, :] + feed.take(c)).astype(BF)
     for copy in ring(chips - 2):
         copy.wait_recv()
     qkv, out, small = term(chip, chips - 1)
@@ -1089,13 +1093,14 @@
     qkv_out_ref[seq] = qkv_move_ref[chips - 1, seq]
     small_out_ref[seq] = small_move_ref[chips - 1]
     total.finish()
+    feed.finish()
     for copy in cores + [copy for step in range(chips - 1) for copy in ring(step)]:
         copy.wait_send()
     for copy in last:
         copy.wait()
 
 
-def end_call(normed_grad, hidden_grad, x, gain, qkv, out, small):
+def end_call(normed_grad, hidden_grad, x, gain, qkv, out, small, feed, hidden):
     seqs, chips, _, share, wide = qkv.shape
     rows, model = x.shape
     vmem = pl.BlockSpec(memory_space=pltpu.VMEM)
@@ -1109,9 +1114,10 @@
             shape(blocks[0], BF),
             shape(blocks[1], F32),
             shape((seqs,) + blocks[2], BF),
+            shape((rows, model), BF),
         ),
-        in_specs=[vmem] * 7,
-        out_specs=(vmem,) * 4,
+        in_specs=[vmem] * 8 + [pl.BlockSpec(memory_space=pl.ANY)],
+        out_specs=(vmem,) * 5,
         scratch_shapes=[
             pltpu.VMEM((seqs, chips, share, wide), BF),
             pltpu.VMEM((chips, share, model), BF),
@@ -1120,8 +1126,8 @@
         + [pltpu.VMEM((chips,) + block, BF) for block in blocks]
         + [pltpu.VMEM((chips - 1,) + block, BF) for block in blocks]
         + [
-            held, held, held, held,
-            dma((3, PIECES)), dma((3, PIECES)), dma((3,)), dma((3,)),
+            held, held, held, held, held, held, held, held, pltpu.VMEM((rows, model), F32),
+            dma((3, PIECES)), dma((3, PIECES)), dma((3, PIECES)), dma((3, PIECES)), dma, dma((3,)), dma((3,)),
             dma((3, chips)), dma((3, chips)), dma((2, seqs)), dma((2, seqs)),
         ],
         cost_estimate=pl.CostEstimate(flops=10**8, bytes_accessed=2 * 10**7, transcendentals=0),
@@ -1129,7 +1135,7 @@
             collective_id=3, has_side_effects=True, vmem_limit_bytes=48 * 2**20
         ),
         name="end_sums",
-    )(normed_grad, hidden_grad, x, gain[None], qkv, out, small)
+    )(normed_grad, hidden_grad, x, gain[None], qkv, out, small, feed, hidden)
 
 
 def pair_tiles(left, right):
@@ -1228,9 +1234,8 @@
     _, out_sum, second_sum, rest, summed = feed_call(second, incoming, first, later, SUMMED)
     rest = rest.reshape(model, -1)
     rest = lax.psum_scatter(rest, "dp", scatter_dimension=0, tiled=True)
-    gate_grad, up_grad, down_grad = unpack_call(summed, rest, hidden_units)
-    normed_grad, grad_hidden, qkv_grad, out_weight_grad, bias_grad, gain_one_grad, gain_two_grad, layer_out = backward_call(
-        second_sum, out_sum, cotangent[0], gain_first, gain_second, logsum, cosine, sine, blocks,
+    normed_grad, grad_hidden, qkv_grad, out_weight_grad, bias_grad, gain_one_grad, gain_two_grad = backward_call(
+        second_sum, cotangent[0], gain_first, gain_second, logsum, cosine, sine, blocks,
         hidden, tokens, normed, weight_qkv, out_head, qkv, mixed,
     )
     bias_grad, gain_one_grad, gain_two_grad = bias_grad[0], gain_one_grad[0], gain_two_grad[0]
@@ -1252,11 +1257,12 @@
     small_grad = small_grad.transpose(1, 0, 2).reshape(dps, seqs * one).astype(BF)
     small_grad = jnp.pad(small_grad, ((0, 0), (0, small_rows * wide - seqs * one)))
     small_grad = jnp.pad(small_grad.reshape(dps, -1, wide), ((0, 0), (0, 16 - small_rows), (0, 0)))
-    input_grad, parts, out_weight_grad, smalls = end_call(
+    input_grad, parts, out_weight_grad, smalls, layer_out = end_call(
         normed_grad, grad_hidden, inputs[0], gain_first,
         qkv_grad.reshape(seqs, chips, 2, share, wide),
         out_weight_grad.reshape(chips, 2, share, model),
         small_grad.reshape(chips, 2, 16, wide),
+        out_sum, hidden,
     )
     smalls = smalls[:, :small_rows].reshape(seqs, -1)[:, : seqs * one].reshape(seqs, seqs, one)
     small_sum = jnp.sum(
@@ -1273,6 +1279,9 @@
         small_sum, [share, 2 * share, 3 * share, 3 * share + kv_share]
     )
 
+    gate_grad, up_grad, down_grad, layer_out, input_grad, out_weight_grad = unpack_call(
+        summed, rest, hidden_units, layer_out, input_grad, out_weight_grad
+    )
     return (
         layer_out[None],
         input_grad[None],

time: 474 us -> 472 us (level)
    pallas_call x1, Pallas kernels: 90.1 us -> 74.5 us  [backward_call(): pl.pallas_call(backward_kernel, out_shape=(shape((length, model), BF), sh...]
    pallas_call x1, Pallas kernels: 59.5 us -> 74 us  [end_call(): pl.pallas_call(end_kernel, out_shape=(shape((rows, model), BF), shape(blo...]
    unnamed x45 -> x40, local copies, waits for them, and re-layouts: 12.7 us -> 10.2 us
  transfers between devices with their start and end apart: 2 -> 2, of which waited for: 1 -> 1; matrix products, arithmetic and copies ran while one was open for 3% -> 3% of each run, Pallas kernels for 63% -> 64%
where the time goes in v6:
time: 472 us; the launch traced here: 468 us
  Pallas kernels  423 us (90%)
  local copies, waits for them, and re-layouts  21.2 us (4%)
  between operations  14.7 us (3%)
  other arithmetic  5.29 us (1%)
    pallas_call x1, Pallas kernels, feed_call(): pl.pallas_call(functools.partial(feed_kernel, tiles=tiles, ready=ready, s...  120 us
    pallas_call x1, Pallas kernels, start_call(): pl.pallas_call(start_kernel, out_shape=shapes, in_specs=[pl.BlockSpec(mem...  92.3 us
    pallas_call x1, Pallas kernels, backward_call(): pl.pallas_call(backward_kernel, out_shape=(shape((length, model), BF), sh...  74.5 us
    pallas_call x1, Pallas kernels, end_call(): pl.pallas_call(end_kernel, out_shape=(shape((rows, model), BF), shape(blo...  74 us
    pallas_call x1, Pallas kernels, attend_call(): pl.pallas_call(attend_kernel, out_shape=(shape((length, model), BF), shap...  56.9 us
    unnamed x40, local copies, waits for them, and re-layouts  10.2 us
  transfers between devices with their start and end apart: 2, of which 1 were waited for; matrix products, arithmetic and copies ran while one was open for 3% of the time, Pallas kernels for 64%

profile of v6, /device:TPU:0, one launch (start us, length us, event | category | flops | bytes accessed | tf_op | source)
XLA Modules:
  0.0 467.8 jit_solution(15858059785848499545)
XLA Ops:
  7.3 1.2 copy-done.7
  8.4 1.2 copy-done.8
  9.6 1.2 copy-done.9
  10.8 1.4 pack_weights.1
  12.2 0.9 copy-done.11
  13.4 0.6 pad.8.small_in
  14.0 0.7 maximum_bitcast_fusion.pack_in
  14.8 92.3 %start_gather.1 = (bf16[1024,1536]{1,0:T(8,128)(2,1)}, bf16[1024,1536]{1,0:T(8,128)(2,1)}, s32[4,2,128]{2,1,0:T(2,128)}, bf16[8,4,16,256]{3,2,1,0:T(8,128)(2,1)}...) custom-call(bf16[256,1536]{1,0:T(8,128)(2,1)} %bitcast.58, bf16[256,1536]{1,0:T(8,128)(2,1)} %bitcast.66, ...), custom_call_target="tpu_custom_call" | custom-call | tf_op jit(solution)/shard_map/start_gather/pallas_call | solution.py:214
  107.1 0.9 slice_convert_fusion
  108.3 0.7 broadcast_in_dim_reshape.20.gain_two_ref
  109.9 0.7 broadcast_in_dim_reshape.19.gain_one_ref.gain_ref
  110.5 1.7 copy.43.ids_col_ref
  112.2 2.4 slice.84
  114.6 56.9 %attend.1 = (bf16[1024,1536]{1,0:T(8,128)(2,1)}, bf16[1024,640]{1,0:T(8,128)(2,1)}, bf16[1024,384]{1,0:T(8,128)(2,1)}, f32[1024,128]{1,0:T(8,128)}, f32[1024,1536]{1,0:T(8,128)}, /*index=5*/bf16[1024,1536]{1,0:T(8,128)(2,1)}) custom-call(bf16[1024,1536]{1,0:T(8,128)(2,1)} %get-tuple-element.52.x_ref.tokens_hbm, bf16[1536,640]{1,0:T(8,128)(2,1)} %bitcast.84, ...), custom_call_target="tpu_custom_call" | custom-call | flops 8999999488 | bytes 30000000 | tf_op jit(solution)/shard_map/attend/pallas_call | solution.py:310
  171.5 4.0 all-gather.2.cloned.1.call-done
  175.5 120.1 %feed_forward.1 = (bf16[8,192,2304]{2,1,0:T(8,128)(2,1)}, bf16[1024,1536]{1,0:T(8,128)(2,1)}, bf16[1024,1536]{1,0:T(8,128)(2,1)}, bf16[4,2,192,3840]{3,2,1,0:T(8,128)(2,1)}, f32[4,192,768]{2,1,0:T(8,128)}) custom-call(bf16[1024,1536]{1,0:T(8,128)(2,1)} %get-tuple-element.58.second_ref, bf16[1024,1536]{1,0:T(8,128)(2,1)} %get-tuple-element.59.incoming_ref, ...), custom_call_target="tpu_custom_call" | custom-call | flops 65000001536 | bytes 60000000 | tf_op jit(solution)/shard_map/feed_forward/pallas_call | solution.py:892
  295.9 74.5 %backward.1 = (bf16[1024,1536]{1,0:T(8,128)(2,1)}, f32[256,1536]{1,0:T(8,128)}, bf16[1536,640]{1,0:T(8,128)(2,1)}, bf16[384,1536]{1,0:T(8,128)(2,1)}, f32[1,640]...) custom-call(bf16[1024,1536]{1,0:T(8,128)(2,1)} %get-tuple-element.64.second_grad_ref, bf16[256,1536]{1,0:T(8,128)(2,1)} %bitcast.67, ...), custom_call_target="tpu_custom_call" | custom-call | flops 12999999488 | bytes 30000000 | tf_op jit(solution)/shard_map/backward/pallas_call | solution.py:537
  370.4 0.7 slice_reduce_fusion.1
  371.2 0.7 slice_reduce_fusion.2
  372.1 0.7 convert_reduce_fusion.1
  372.9 0.7 convert_reduce_fusion
  374.2 1.5 copy-done.4
  375.7 1.3 copy-done.6
  376.9 74.0 %end_sums.1 = (bf16[256,1536]{1,0:T(8,128)(2,1)S(1)}, bf16[4,48,640]{2,1,0:T(8,128)(2,1)S(1)}, f32[48,1536]{1,0:T(8,128)S(1)}, bf16[4,16,640]{2,1,0:T(8,128)(2,1)S(1)}, bf16[256,1536]{1,0:T(8,128)(2,1)S(1)}) custom-call(bf16[1024,1536]{1,0:T(8,128)(2,1)} %get-tuple-element.71.normed_grad_ref, f32[256,1536]{1,0:T(8,128)S(1)} %copy-done.4, ...), custom_call_target="tpu_custom_call" | custom-call | flops 100000000 | bytes 20000000 | tf_op jit(solution)/shard_map/end_sums/pallas_call | solution.py:1110
  451.2 0.6 pad_maximum_fusion.1
  451.8 0.6 pad_maximum_fusion
  452.5 0.6 fusion.7
  453.0 0.6 fusion.6
  453.6 0.7 maximum_convert_fusion
  454.4 1.7 copy-done.3
  456.0 1.4 copy-done.5
  457.4 3.3 unpack_gradients.1
  (90 shorter events, 2.8 us)
Async XLA Ops:
  7.2 6.8 %copy-start = (bf16[48,256]{1,0:T(8,128)(2,1)S(1)}, bf16[48,256]{1,0:T(8,128)(2,1)}, u32[]{:S(2)}) copy-start(bf16[48,256]{1,0:T(8,128)(2,1)} %param.23) | copy-start | bytes 73732
  7.2 6.0 %copy-start.15 = (bf16[48]{0:T(256)(128)(2,1)S(1)}, bf16[48]{0:T(256)(128)(2,1)}, u32[]{:S(2)}) copy-start(bf16[48]{0:T(256)(128)(2,1)} %param.28) | copy-start | bytes 292
  7.2 6.0 %copy-start.16 = (bf16[48]{0:T(256)(128)(2,1)S(1)}, bf16[48]{0:T(256)(128)(2,1)}, u32[]{:S(2)}) copy-start(bf16[48]{0:T(256)(128)(2,1)} %param.22) | copy-start | bytes 292
  7.2 6.0 %copy-start.14 = (bf16[48]{0:T(256)(128)(2,1)S(1)}, bf16[48]{0:T(256)(128)(2,1)}, u32[]{:S(2)}) copy-start(bf16[48]{0:T(256)(128)(2,1)} %param.20) | copy-start | bytes 292
  7.2 168.3 %all-gather.2.cloned.1.call-start = ((), (), s32[]{:S(2)}) async-start(), calls=%async_computation.1 | async-start | bytes 15925248 | tf_op jit(solution)/shard_map/all_gather | solution.py:1205
  7.3 1.2 copy-start.7
  8.4 1.2 copy-start.8
  9.6 1.2 copy-start.9
  10.8 2.4 copy-start.17
  10.8 2.5 copy-start.18
  10.8 2.6 copy-start.12
  10.8 3.2 copy-start.13
  12.2 0.9 copy-start.11
  13.1 441.2 %reduce-scatter.2.cloned.1.call-start = ((), (), s32[]{:S(2)}) async-start(), calls=%async_computation.2 | async-start | bytes 13271040 | tf_op jit(solution)/shard_map/reduce_scatter | solution.py:1236
  295.9 78.3 %copy-start.2 = (bf16[1,256,1536]{2,1,0:T(8,128)(2,1)S(1)}, bf16[1,256,1536]{2,1,0:T(8,128)(2,1)}, u32[]{:S(2)}) copy-start(bf16[1,256,1536]{2,1,0:T(8,128)(2,1)} %param.17) | copy-start | bytes 2359300
  295.9 78.3 %copy-start.10 = (f32[1,1536]{1,0:T(1,128)S(1)}, f32[1,1536]{1,0:T(1,128)}, u32[]{:S(2)}) copy-start(f32[1,1536]{1,0:T(1,128)} %broadcast_in_dim_reshape.19.gain_one_ref.gain_ref) | copy-start | bytes 18436
  374.2 1.5 copy-start.4
  375.7 1.3 copy-start.6
  451.2 9.5 %copy-start.1 = (bf16[48,256]{1,0:T(8,128)(2,1)S(1)}, bf16[48,256]{1,0:T(8,128)(2,1)}, u32[]{:S(2)}) copy-start(bf16[48,256]{1,0:T(8,128)(2,1)} %param.23) | copy-start | bytes 73732
  454.4 1.7 copy-start.3
  456.0 1.4 copy-start.5
Sparse Core Ops, SparseCore 0:
  13.2 162.2 all-gather.1
  295.8 143.4 reduce-scatter.1

commit v7 on v6

--- a/solution.py
+++ b/solution.py
@@ -136,23 +136,45 @@
             for k in range(1, seqs)
         ]
 
-    order = sorted(range(1, chips), key=lambda hop: min(hop, chips - hop))
+    line = chips == 4
+    order = [2, 1, 3] if line else sorted(range(1, chips), key=lambda hop: min(hop, chips - hop))
+    ends = ((1, chip != 0), (3, chip != chips - 1))
+
+    def hops_do(which, what):
+        for hop in order:
+            for copy in hop_sends(hop, which):
+                if line and hop != 2:
+                    pl.when(dict(ends)[hop])(getattr(copy, what))
+                else:
+                    getattr(copy, what)()
+
+    def relays(which):
+        low = chip == 2
+        end, far = jnp.where(low, 3, 0), jnp.where(low, 0, 3)
+        return [
+            remote(field, field, ring_send.at[i, 0], ring_recv.at[i, jnp.where(low, 1, 3)], (seq, end * 2 + core))
+            for i, field in fields(far * 2 + core, which)
+        ]
+
+    def relay(which, what):
+        if line:
+            for copy in relays(which):
+                pl.when((chip == 1) | (chip == 2))(getattr(copy, what))
+
     flying, outs = [], []
-    for hop in order:
-        flying += hop_sends(hop, (0,))
+    hops_do((0,), "start")
     first = small_sends + pack_sends + locals_[:3] + x_sends + id_sends + locals_[3:]
-    for copy in flying + first:
+    for copy in first:
         copy.start()
     for copy in locals_[:3] + small_sends + pack_sends:
         copy.wait()
-    more = [copy for hop in order for copy in hop_sends(hop, (1, 2))]
-    for copy in more:
-        copy.start()
-    flying += more
+    hops_do((1, 2), "start")
     for hop in [0] + order:
         if hop > 0:
             for copy in hop_sends(hop, (0,)):
                 copy.wait_recv()
+            if hop == 2:
+                relay((0,), "start")
         cores, more = core_sends(hop, (0,)), out_sends(hop)
         for copy in cores + more:
             copy.start()
@@ -167,6 +189,8 @@
         if hop > 0:
             for copy in hop_sends(hop, (1, 2)):
                 copy.wait_recv()
+            if hop == 2:
+                relay((1, 2), "start")
         cores = core_sends(hop, (1, 2))
         for copy in cores:
             copy.start()
@@ -188,6 +212,8 @@
     ]
     for copy in slots:
         copy.start()
+    hops_do((0, 1, 2), "wait_send")
+    relay((0, 1, 2), "wait_send")
     for copy in flying + outs:
         copy.wait_send()
     for hop in range(chips):
@@ -1208,8 +1234,6 @@
     )
     blocks = blocks.reshape(-1)
     weight_qkv = weight_qkv.reshape(model, wide)
-    out_head = weight_out[0].reshape(dps * share, model)
-    weight_out = weight_out.reshape(model, model)
     smalls = smalls[:, :, 0, :one].transpose(1, 0, 2).astype(F32)
     gain_first = smalls[:, :, :share].reshape(model)
     gain_second = smalls[:, :, share : 2 * share].reshape(model)
@@ -1228,9 +1252,10 @@
     cosine, sine = rope_tables(length)
 
     normed, qkv, mixed, logsum, hidden, second = attend_call(
-        tokens, weight_qkv, bias[None], cosine, sine, blocks, gain_first, gain_second, weight_out
-    )
-    second, out_head = lax.optimization_barrier((second, out_head))
+        tokens, weight_qkv, bias[None], cosine, sine, blocks, gain_first, gain_second, weight_out.reshape(model, model)
+    )
+    second, weight_out = lax.optimization_barrier((second, weight_out))
+    out_head = weight_out[0].reshape(dps * share, model)
     _, out_sum, second_sum, rest, summed = feed_call(second, incoming, first, later, SUMMED)
     rest = rest.reshape(model, -1)
     rest = lax.psum_scatter(rest, "dp", scatter_dimension=0, tiled=True)

time: 472 us -> 462 us (0.979)
  Pallas kernels: 423 us -> 415 us
  transfers between devices with their start and end apart: 2 -> 2, of which waited for: 1 -> 1; matrix products, arithmetic and copies ran while one was open for 3% -> 4% of each run, Pallas kernels for 64% -> 63%
where the time goes in v7:
time: 462 us; the launch traced here: 459 us
  Pallas kernels  415 us (90%)
  local copies, waits for them, and re-layouts  21.2 us (5%)
  between operations  14.7 us (3%)
  other arithmetic  5.3 us (1%)
    pallas_call x1, Pallas kernels, feed_call(): pl.pallas_call(functools.partial(feed_kernel, tiles=tiles, ready=ready, s...  120 us
    pallas_call x1, Pallas kernels, start_call(): pl.pallas_call(start_kernel, out_shape=shapes, in_specs=[pl.BlockSpec(mem...  90.9 us
    pallas_call x1, Pallas kernels, backward_call(): pl.pallas_call(backward_kernel, out_shape=(shape((length, model), BF), sh...  74.6 us
    pallas_call x1, Pallas kernels, end_call(): pl.pallas_call(end_kernel, out_shape=(shape((rows, model), BF), shape(blo...  71.6 us
    pallas_call x1, Pallas kernels, attend_call(): pl.pallas_call(attend_kernel, out_shape=(shape((length, model), BF), shap...  53.4 us
    unnamed x40, local copies, waits for them, and re-layouts  10.2 us
  transfers between devices with their start and end apart: 2, of which 1 were waited for; matrix products, arithmetic and copies ran while one was open for 4% of the time, Pallas kernels for 63%

profile of v7, /device:TPU:0, one launch (start us, length us, event | category | flops | bytes accessed | tf_op | source)
XLA Modules:
  0.0 458.7 jit_solution(5307281551661379381)
XLA Ops:
  7.3 1.2 copy-done.7
  8.4 1.2 copy-done.8
  9.6 1.2 copy-done.9
  10.8 1.4 pack_weights.1
  12.2 0.9 copy-done.11
  13.4 0.6 pad.8.small_in
  14.0 0.7 maximum_bitcast_fusion.pack_in
  14.8 90.9 %start_gather.1 = (bf16[1024,1536]{1,0:T(8,128)(2,1)}, bf16[1024,1536]{1,0:T(8,128)(2,1)}, s32[4,2,128]{2,1,0:T(2,128)}, bf16[8,4,16,256]{3,2,1,0:T(8,128)(2,1)}...) custom-call(bf16[256,1536]{1,0:T(8,128)(2,1)} %bitcast.58, bf16[256,1536]{1,0:T(8,128)(2,1)} %bitcast.66, ...), custom_call_target="tpu_custom_call" | custom-call | tf_op jit(solution)/shard_map/start_gather/pallas_call | solution.py:240
  105.7 0.9 slice_convert_fusion
  106.9 0.7 broadcast_in_dim_reshape.20.gain_two_ref
  108.5 0.7 broadcast_in_dim_reshape.19.gain_one_ref.gain_ref
  109.1 1.7 copy.43.ids_col_ref
  110.8 53.4 %attend.1 = (bf16[1024,1536]{1,0:T(8,128)(2,1)}, bf16[1024,640]{1,0:T(8,128)(2,1)}, bf16[1024,384]{1,0:T(8,128)(2,1)}, f32[1024,128]{1,0:T(8,128)}, f32[1024,1536]{1,0:T(8,128)}, /*index=5*/bf16[1024,1536]{1,0:T(8,128)(2,1)}) custom-call(bf16[1024,1536]{1,0:T(8,128)(2,1)} %get-tuple-element.52.x_ref.tokens_hbm, bf16[1536,640]{1,0:T(8,128)(2,1)} %bitcast.84, ...), custom_call_target="tpu_custom_call" | custom-call | flops 8999999488 | bytes 30000000 | tf_op jit(solution)/shard_map/attend/pallas_call | solution.py:336
  164.2 2.1 all-gather.2.cloned.1.call-done
  166.3 120.1 %feed_forward.1 = (bf16[8,192,2304]{2,1,0:T(8,128)(2,1)}, bf16[1024,1536]{1,0:T(8,128)(2,1)}, bf16[1024,1536]{1,0:T(8,128)(2,1)}, bf16[4,2,192,3840]{3,2,1,0:T(8,128)(2,1)}, f32[4,192,768]{2,1,0:T(8,128)}) custom-call(bf16[1024,1536]{1,0:T(8,128)(2,1)} %get-tuple-element.58.second_ref, bf16[1024,1536]{1,0:T(8,128)(2,1)} %get-tuple-element.59.incoming_ref, ...), custom_call_target="tpu_custom_call" | custom-call | flops 65000001536 | bytes 60000000 | tf_op jit(solution)/shard_map/feed_forward/pallas_call | solution.py:918
  286.7 2.4 slice.84
  289.1 74.6 %backward.1 = (bf16[1024,1536]{1,0:T(8,128)(2,1)}, f32[256,1536]{1,0:T(8,128)}, bf16[1536,640]{1,0:T(8,128)(2,1)}, bf16[384,1536]{1,0:T(8,128)(2,1)}, f32[1,640]...) custom-call(bf16[1024,1536]{1,0:T(8,128)(2,1)} %get-tuple-element.64.second_grad_ref, bf16[256,1536]{1,0:T(8,128)(2,1)} %bitcast.67, ...), custom_call_target="tpu_custom_call" | custom-call | flops 12999999488 | bytes 30000000 | tf_op jit(solution)/shard_map/backward/pallas_call | solution.py:563
  363.7 0.7 slice_reduce_fusion.1
  364.5 0.7 slice_reduce_fusion.2
  365.4 0.7 convert_reduce_fusion.1
  366.2 0.7 convert_reduce_fusion
  367.5 1.4 copy-done.4
  368.9 1.3 copy-done.6
  370.2 71.6 %end_sums.1 = (bf16[256,1536]{1,0:T(8,128)(2,1)S(1)}, bf16[4,48,640]{2,1,0:T(8,128)(2,1)S(1)}, f32[48,1536]{1,0:T(8,128)S(1)}, bf16[4,16,640]{2,1,0:T(8,128)(2,1)S(1)}, bf16[256,1536]{1,0:T(8,128)(2,1)S(1)}) custom-call(bf16[1024,1536]{1,0:T(8,128)(2,1)} %get-tuple-element.71.normed_grad_ref, f32[256,1536]{1,0:T(8,128)S(1)} %copy-done.4, ...), custom_call_target="tpu_custom_call" | custom-call | flops 100000000 | bytes 20000000 | tf_op jit(solution)/shard_map/end_sums/pallas_call | solution.py:1136
  442.2 0.6 pad_maximum_fusion.1
  442.8 0.6 pad_maximum_fusion
  443.4 0.6 fusion.7
  444.0 0.6 fusion.6
  444.6 0.7 maximum_convert_fusion
  445.3 1.7 copy-done.3
  447.0 1.4 copy-done.5
  448.4 3.3 unpack_gradients.1
  (90 shorter events, 2.8 us)
Async XLA Ops:
  7.2 6.8 %copy-start = (bf16[48,256]{1,0:T(8,128)(2,1)S(1)}, bf16[48,256]{1,0:T(8,128)(2,1)}, u32[]{:S(2)}) copy-start(bf16[48,256]{1,0:T(8,128)(2,1)} %param.23) | copy-start | bytes 73732
  7.2 6.0 %copy-start.15 = (bf16[48]{0:T(256)(128)(2,1)S(1)}, bf16[48]{0:T(256)(128)(2,1)}, u32[]{:S(2)}) copy-start(bf16[48]{0:T(256)(128)(2,1)} %param.28) | copy-start | bytes 292
  7.2 6.0 %copy-start.16 = (bf16[48]{0:T(256)(128)(2,1)S(1)}, bf16[48]{0:T(256)(128)(2,1)}, u32[]{:S(2)}) copy-start(bf16[48]{0:T(256)(128)(2,1)} %param.22) | copy-start | bytes 292
  7.2 6.0 %copy-start.14 = (bf16[48]{0:T(256)(128)(2,1)S(1)}, bf16[48]{0:T(256)(128)(2,1)}, u32[]{:S(2)}) copy-start(bf16[48]{0:T(256)(128)(2,1)} %param.20) | copy-start | bytes 292
  7.2 159.1 %all-gather.2.cloned.1.call-start = ((), (), s32[]{:S(2)}) async-start(), calls=%async_computation.1 | async-start | bytes 15925248 | tf_op jit(solution)/shard_map/all_gather | solution.py:1231
  7.3 1.2 copy-start.7
  8.4 1.2 copy-start.8
  9.6 1.2 copy-start.9
  10.8 2.4 copy-start.17
  10.8 2.5 copy-start.18
  10.8 2.6 copy-start.12
  10.8 3.2 copy-start.13
  12.2 0.9 copy-start.11
  13.1 432.2 %reduce-scatter.2.cloned.1.call-start = ((), (), s32[]{:S(2)}) async-start(), calls=%async_computation.2 | async-start | bytes 13271040 | tf_op jit(solution)/shard_map/reduce_scatter | solution.py:1261
  289.1 78.4 %copy-start.2 = (bf16[1,256,1536]{2,1,0:T(8,128)(2,1)S(1)}, bf16[1,256,1536]{2,1,0:T(8,128)(2,1)}, u32[]{:S(2)}) copy-start(bf16[1,256,1536]{2,1,0:T(8,128)(2,1)} %param.17) | copy-start | bytes 2359300
  289.1 78.4 %copy-start.10 = (f32[1,1536]{1,0:T(1,128)S(1)}, f32[1,1536]{1,0:T(1,128)}, u32[]{:S(2)}) copy-start(f32[1,1536]{1,0:T(1,128)} %broadcast_in_dim_reshape.19.gain_one_ref.gain_ref) | copy-start | bytes 18436
  367.5 1.4 copy-start.4
  368.9 1.3 copy-start.6
  442.1 9.5 %copy-start.1 = (bf16[48,256]{1,0:T(8,128)(2,1)S(1)}, bf16[48,256]{1,0:T(8,128)(2,1)}, u32[]{:S(2)}) copy-start(bf16[48,256]{1,0:T(8,128)(2,1)} %param.23) | copy-start | bytes 73732
  445.3 1.7 copy-start.3
  447.0 1.4 copy-start.5
Sparse Core Ops, SparseCore 0:
  13.2 153.0 all-gather.1
  286.6 141.5 reduce-scatter.1

commit v8 on v7

--- a/solution.py
+++ b/solution.py
@@ -1256,6 +1256,7 @@
     )
     second, weight_out = lax.optimization_barrier((second, weight_out))
     out_head = weight_out[0].reshape(dps * share, model)
+    second, out_head = lax.optimization_barrier((second, out_head))
     _, out_sum, second_sum, rest, summed = feed_call(second, incoming, first, later, SUMMED)
     rest = rest.reshape(model, -1)
     rest = lax.psum_scatter(rest, "dp", scatter_dimension=0, tiled=True)

time: 462 us -> 462 us (level)
  transfers between devices with their start and end apart: 2 -> 2, of which waited for: 1 -> 0; matrix products, arithmetic and copies ran while one was open for 4% -> 4% of each run, Pallas kernels for 63% -> 64%
where the time goes in v8:
time: 462 us; the launch traced here: 459 us
  Pallas kernels  417 us (90%)
  local copies, waits for them, and re-layouts  21.2 us (5%)
  between operations  14.7 us (3%)
  other arithmetic  5.29 us (1%)
    pallas_call x1, Pallas kernels, feed_call(): pl.pallas_call(functools.partial(feed_kernel, tiles=tiles, ready=ready, s...  121 us
    pallas_call x1, Pallas kernels, start_call(): pl.pallas_call(start_kernel, out_shape=shapes, in_specs=[pl.BlockSpec(mem...  90.9 us
    pallas_call x1, Pallas kernels, end_call(): pl.pallas_call(end_kernel, out_shape=(shape((rows, model), BF), shape(blo...  73.9 us
    pallas_call x1, Pallas kernels, backward_call(): pl.pallas_call(backward_kernel, out_shape=(shape((length, model), BF), sh...  73.6 us
    pallas_call x1, Pallas kernels, attend_call(): pl.pallas_call(attend_kernel, out_shape=(shape((length, model), BF), shap...  53.3 us
    unnamed x40, local copies, waits for them, and re-layouts  10.2 us
  transfers between devices with their start and end apart: 2, of which 0 were waited for; matrix products, arithmetic and copies ran while one was open for 4% of the time, Pallas kernels for 64%

profile of v8, /device:TPU:0, one launch (start us, length us, event | category | flops | bytes accessed | tf_op | source)
XLA Modules:
  0.0 458.6 jit_solution(18292694250106154599)
XLA Ops:
  7.3 1.2 copy-done.7
  8.4 1.2 copy-done.8
  9.6 1.2 copy-done.9
  10.8 1.4 pack_weights.1
  12.2 0.9 copy-done.11
  13.4 0.6 pad.8.small_in
  14.0 0.7 maximum_bitcast_fusion.pack_in
  14.8 90.9 %start_gather.1 = (bf16[1024,1536]{1,0:T(8,128)(2,1)}, bf16[1024,1536]{1,0:T(8,128)(2,1)}, s32[4,2,128]{2,1,0:T(2,128)}, bf16[8,4,16,256]{3,2,1,0:T(8,128)(2,1)}...) custom-call(bf16[256,1536]{1,0:T(8,128)(2,1)} %bitcast.58, bf16[256,1536]{1,0:T(8,128)(2,1)} %bitcast.66, ...), custom_call_target="tpu_custom_call" | custom-call | tf_op jit(solution)/shard_map/start_gather/pallas_call | solution.py:240
  105.7 0.9 slice_convert_fusion
  106.9 0.7 broadcast_in_dim_reshape.20.gain_two_ref
  107.9 0.6 broadcast_in_dim.90.bias_ref
  108.5 0.7 broadcast_in_dim_reshape.19.gain_one_ref.gain_ref
  109.2 1.7 copy.43.ids_col_ref
  110.9 53.3 %attend.1 = (bf16[1024,1536]{1,0:T(8,128)(2,1)}, bf16[1024,640]{1,0:T(8,128)(2,1)}, bf16[1024,384]{1,0:T(8,128)(2,1)}, f32[1024,128]{1,0:T(8,128)}, f32[1024,1536]{1,0:T(8,128)}, /*index=5*/bf16[1024,1536]{1,0:T(8,128)(2,1)}) custom-call(bf16[1024,1536]{1,0:T(8,128)(2,1)} %get-tuple-element.54.x_ref.tokens_hbm, bf16[1536,640]{1,0:T(8,128)(2,1)} %bitcast.84, ...), custom_call_target="tpu_custom_call" | custom-call | flops 8999999488 | bytes 30000000 | tf_op jit(solution)/shard_map/attend/pallas_call | solution.py:336
  164.2 2.4 slice.84
  166.6 120.8 %feed_forward.1 = (bf16[8,192,2304]{2,1,0:T(8,128)(2,1)}, bf16[1024,1536]{1,0:T(8,128)(2,1)}, bf16[1024,1536]{1,0:T(8,128)(2,1)}, bf16[4,2,192,3840]{3,2,1,0:T(8,128)(2,1)}, f32[4,192,768]{2,1,0:T(8,128)}) custom-call(bf16[1024,1536]{1,0:T(8,128)(2,1)} %get-tuple-element.62.second_ref, bf16[1024,1536]{1,0:T(8,128)(2,1)} %get-tuple-element.63.incoming_ref, ...), custom_call_target="tpu_custom_call" | custom-call | flops 65000001536 | bytes 60000000 | tf_op jit(solution)/shard_map/feed_forward/pallas_call | solution.py:918
  287.6 73.6 %backward.1 = (bf16[1024,1536]{1,0:T(8,128)(2,1)}, f32[256,1536]{1,0:T(8,128)}, bf16[1536,640]{1,0:T(8,128)(2,1)}, bf16[384,1536]{1,0:T(8,128)(2,1)}, f32[1,640]...) custom-call(bf16[1024,1536]{1,0:T(8,128)(2,1)} %get-tuple-element.68.second_grad_ref, bf16[256,1536]{1,0:T(8,128)(2,1)} %bitcast.67, ...), custom_call_target="tpu_custom_call" | custom-call | flops 12999999488 | bytes 30000000 | tf_op jit(solution)/shard_map/backward/pallas_call | solution.py:563
  361.2 0.7 slice_reduce_fusion.1
  362.0 0.7 slice_reduce_fusion.2
  362.9 0.7 convert_reduce_fusion.1
  363.7 0.7 convert_reduce_fusion
  365.0 1.5 copy-done.4
  366.5 1.3 copy-done.6
  367.8 73.9 %end_sums.1 = (bf16[256,1536]{1,0:T(8,128)(2,1)S(1)}, bf16[4,48,640]{2,1,0:T(8,128)(2,1)S(1)}, f32[48,1536]{1,0:T(8,128)S(1)}, bf16[4,16,640]{2,1,0:T(8,128)(2,1)S(1)}, bf16[256,1536]{1,0:T(8,128)(2,1)S(1)}) custom-call(bf16[1024,1536]{1,0:T(8,128)(2,1)} %get-tuple-element.75.normed_grad_ref, f32[256,1536]{1,0:T(8,128)S(1)} %copy-done.4, ...), custom_call_target="tpu_custom_call" | custom-call | flops 100000000 | bytes 20000000 | tf_op jit(solution)/shard_map/end_sums/pallas_call | solution.py:1136
  442.0 0.6 pad_maximum_fusion.1
  442.6 0.6 pad_maximum_fusion
  443.3 0.6 fusion.7
  443.9 0.6 fusion.6
  444.4 0.7 maximum_convert_fusion
  445.2 1.7 copy-done.3
  446.9 1.4 copy-done.5
  448.2 3.3 unpack_gradients.1
  (90 shorter events, 2.2 us)
Async XLA Ops:
  7.2 6.8 %copy-start = (bf16[48,256]{1,0:T(8,128)(2,1)S(1)}, bf16[48,256]{1,0:T(8,128)(2,1)}, u32[]{:S(2)}) copy-start(bf16[48,256]{1,0:T(8,128)(2,1)} %param.23) | copy-start | bytes 73732
  7.2 6.0 %copy-start.15 = (bf16[48]{0:T(256)(128)(2,1)S(1)}, bf16[48]{0:T(256)(128)(2,1)}, u32[]{:S(2)}) copy-start(bf16[48]{0:T(256)(128)(2,1)} %param.28) | copy-start | bytes 292
  7.2 6.0 %copy-start.16 = (bf16[48]{0:T(256)(128)(2,1)S(1)}, bf16[48]{0:T(256)(128)(2,1)}, u32[]{:S(2)}) copy-start(bf16[48]{0:T(256)(128)(2,1)} %param.22) | copy-start | bytes 292
  7.2 6.0 %copy-start.14 = (bf16[48]{0:T(256)(128)(2,1)S(1)}, bf16[48]{0:T(256)(128)(2,1)}, u32[]{:S(2)}) copy-start(bf16[48]{0:T(256)(128)(2,1)} %param.20) | copy-start | bytes 292
  7.2 159.3 %all-gather.2.cloned.1.call-start = ((), (), s32[]{:S(2)}) async-start(), calls=%async_computation.1 | async-start | bytes 15925248 | tf_op jit(solution)/shard_map/all_gather | solution.py:1231
  7.3 1.2 copy-start.7
  8.4 1.2 copy-start.8
  9.6 1.2 copy-start.9
  10.8 2.4 copy-start.17
  10.8 2.5 copy-start.18
  10.8 2.6 copy-start.12
  10.8 3.2 copy-start.13
  12.2 0.9 copy-start.11
  13.1 432.1 %reduce-scatter.2.cloned.1.call-start = ((), (), s32[]{:S(2)}) async-start(), calls=%async_computation.2 | async-start | bytes 13271040 | tf_op jit(solution)/shard_map/reduce_scatter | solution.py:1262
  287.6 77.4 %copy-start.2 = (bf16[1,256,1536]{2,1,0:T(8,128)(2,1)S(1)}, bf16[1,256,1536]{2,1,0:T(8,128)(2,1)}, u32[]{:S(2)}) copy-start(bf16[1,256,1536]{2,1,0:T(8,128)(2,1)} %param.17) | copy-start | bytes 2359300
  287.6 77.4 %copy-start.10 = (f32[1,1536]{1,0:T(1,128)S(1)}, f32[1,1536]{1,0:T(1,128)}, u32[]{:S(2)}) copy-start(f32[1,1536]{1,0:T(1,128)} %broadcast_in_dim_reshape.19.gain_one_ref.gain_ref) | copy-start | bytes 18436
  365.0 1.5 copy-start.4
  366.5 1.3 copy-start.6
  442.0 9.5 %copy-start.1 = (bf16[48,256]{1,0:T(8,128)(2,1)S(1)}, bf16[48,256]{1,0:T(8,128)(2,1)}, u32[]{:S(2)}) copy-start(bf16[48,256]{1,0:T(8,128)(2,1)} %param.23) | copy-start | bytes 73732
  445.2 1.7 copy-start.3
  446.8 1.4 copy-start.5
Sparse Core Ops, SparseCore 0:
  13.2 153.0 all-gather.1
  287.5 142.8 reduce-scatter.1
